TPU v7x, 32 devices: a whole 2x2x4 slice. The times are simulated.
32 devices in a mesh: dp: 8 (over z, x), rows: 4 (over y, core).
Axes of the slice: x: 2, y: 2, z: 4, core: 2. Of those that a mesh axis runs over, the one named last changes fastest.
Arguments:
- images: bfloat16 [32, 8, 8, 1024], P(('dp', 'rows')), may hold values from -6 to 6
- styles: bfloat16 [32, 512], P('dp'), may hold values from -6 to 6
- labels: int32 [32], P('dp'), may hold values from 0 to 999
- noise_map: bfloat16 [32, 16, 16], P(('dp', 'rows')), may hold values from -6 to 6
- counts: int32 [32], P('dp'), may hold values from 0 to 1, as said below
- cot_features: bfloat16 [32, 16, 16, 1024], P(('dp', 'rows')), may hold values from -6 to 6
- cot_image: float32 [32, 3, 16, 16], P(('dp', 'rows')), may hold values from -6 to 6
- kernel_bank: bfloat16 [3, 3, 1024, 8, 1024], P(None, None, None, None, 'rows'), may hold values from -0.0625 to 0.0625
- select_proj: bfloat16 [512, 8], replicated, may hold values from -0.25 to 0.25
- style_proj: bfloat16 [512, 1024], replicated, may hold values from -0.125 to 0.125
- conv_bias: bfloat16 [1024], replicated, may hold values from -3 to 3
- noise_gain: bfloat16 [1024], replicated, may hold values from 0.19921875 to 0.796875
- norm_attn: bfloat16 [1024], replicated, may hold values from 0.099609375 to 1.8984375
- query_proj: bfloat16 [1024, 1024], P(None, 'rows'), may hold values from -0.1875 to 0.1875
- key_proj: bfloat16 [1024, 1024], P(None, 'rows'), may hold values from -0.1875 to 0.1875
- value_proj: bfloat16 [1024, 1024], P(None, 'rows'), may hold values from -0.1875 to 0.1875
- out_proj: bfloat16 [1024, 1024], P('rows'), may hold values from -0.75 to 0.75
- norm_cross: bfloat16 [1024], replicated, may hold values from 0.099609375 to 1.8984375
- cross_query: bfloat16 [1024, 1024], P(None, 'rows'), may hold values from -0.1875 to 0.1875
- cross_key: bfloat16 [1024, 1024], P(None, 'rows'), may hold values from -0.125 to 0.125
- cross_value: bfloat16 [1024, 1024], P(None, 'rows'), may hold values from -0.125 to 0.125
- cross_out: bfloat16 [1024, 1024], P('rows'), may hold values from -0.375 to 0.375
- class_table: bfloat16 [1000, 1024], replicated, may hold values from -6 to 6
- class_pos: bfloat16 [16, 1024], replicated, may hold values from -6 to 6
- norm_mlp: bfloat16 [1024], replicated, may hold values from 0.099609375 to 1.8984375
- up_proj: bfloat16 [1024, 4096], P(None, 'rows'), may hold values from -0.1875 to 0.1875
- down_proj: bfloat16 [4096, 1024], P('rows'), may hold values from -0.125 to 0.125
- rgb_style: bfloat16 [512, 1024], replicated, may hold values from -0.125 to 0.125
- color_projection: bfloat16 [1024, 3], replicated, may hold values from -0.1875 to 0.1875
- color_bias: bfloat16 [3], replicated, may hold values from -2 to 2
Outputs:
- features: float32 [32, 16, 16, 1024], P(('dp', 'rows'))
- color_image: float32 [32, 3, 16, 16], P(('dp', 'rows'))
- images_grad: float32 [32, 8, 8, 1024], P(('dp', 'rows'))
- styles_grad: float32 [32, 512], P('dp')
- kernel_bank_grad: float32 [3, 3, 1024, 8, 1024], P(None, None, 'dp', None, 'rows')
- select_proj_grad: float32 [512, 8], replicated
- style_proj_grad: float32 [512, 1024], replicated
- conv_bias_grad: float32 [1024], replicated
- noise_gain_grad: float32 [1024], replicated
- norm_attn_grad: float32 [1024], replicated
- query_proj_grad: float32 [1024, 1024], P('dp', 'rows')
- key_proj_grad: float32 [1024, 1024], P('dp', 'rows')
- value_proj_grad: float32 [1024, 1024], P('dp', 'rows')
- out_proj_grad: float32 [1024, 1024], P('rows', 'dp')
- norm_cross_grad: float32 [1024], replicated
- cross_query_grad: float32 [1024, 1024], P('dp', 'rows')
- cross_key_grad: float32 [1024, 1024], P('dp', 'rows')
- cross_value_grad: float32 [1024, 1024], P('dp', 'rows')
- cross_out_grad: float32 [1024, 1024], P('rows', 'dp')
- class_table_grad: float32 [1000, 1024], replicated
- class_pos_grad: float32 [16, 1024], replicated
- norm_mlp_grad: float32 [1024], replicated
- up_proj_grad: float32 [1024, 4096], P('dp', 'rows')
- down_proj_grad: float32 [4096, 1024], P('rows', 'dp')
- rgb_style_grad: float32 [512, 1024], replicated
- rgb_proj_grad: float32 [1024, 3], replicated
- rgb_bias_grad: float32 [3], replicated
Inputs may be any that keep to these rules, and one draw needn't show every extreme that they name: Entry d belongs to device d of the dp and rows axes taken together (dp slowest) and counts the live samples in that device's first slots of 1; some entry is 1.
All inputs are finite; a program needn't handle non-finite values.
Results may differ from a plain program's by a relative error of at most 0.035.
Values may be sent and summed in bfloat16 or wider, within the bound.
No kernel may reach another device: no remote copies, remote signals or barrier semaphores. Data moves between devices by JAX's collectives and lax.ppermute only.
A program may use at most 512 MiB of HBM per device.

v0:
```python
import math

import jax
import jax.numpy as jnp
from jax import lax
from jax.sharding import PartitionSpec as P

HD = 64


HIGH_ACCURACY = lax.Precision.HIGHEST
FLOAT_KIND = jnp.float32
BRAIN = jnp.bfloat16


def matmul(former, latter):
    return jnp.dot(former, latter, preferred_element_type=FLOAT_KIND)


def contract(equation, former, latter):
    return jnp.einsum(equation, former, latter, preferred_element_type=FLOAT_KIND)


def accurate_mode(equation, former, latter):
    return jnp.einsum(equation, former, latter, precision=HIGH_ACCURACY)


def rms_forward(field, norm_gain):
    inverse = lax.rsqrt(jnp.mean(field * field, axis=-1, keepdims=True) + 1e-06)
    return (field * inverse * norm_gain, inverse)


def rms_backward(field, inverse, norm_gain, grad_out):
    scaled = grad_out * norm_gain
    grad_gain = jnp.sum(grad_out * field * inverse, axis=(0, 1))
    grad_in = inverse * scaled - field * inverse**3 * jnp.mean(
        scaled * field, axis=-1, keepdims=True
    )
    return (grad_in, grad_gain)


def silu_slope(field):
    sigmoid_value = jax.nn.sigmoid(field)
    return sigmoid_value * (1.0 + field * (1.0 - sigmoid_value))


def split_heads(field):
    return field.reshape(field.shape[0], field.shape[1], field.shape[2] // HD, HD)


def merge_heads(field):
    return field.reshape(field.shape[0], field.shape[1], field.shape[2] * field.shape[3])


def spread_group(field):
    return lax.all_gather(field, "rows", axis=0, tiled=True)


def collect_group(field):
    return lax.psum_scatter(field, "rows", scatter_dimension=0, tiled=True)


def spread_mlp(field):
    return lax.all_gather(field, "rows", axis=0, tiled=True)


def collect_mlp(field):
    return lax.psum_scatter(field, "rows", scatter_dimension=0, tiled=True)


def local(
    images,
    styles,
    labels,
    noise_map,
    counts,
    cot_features,
    cot_image,
    kernel_bank,
    select_proj,
    style_proj,
    conv_bias,
    noise_gain,
    norm_attn,
    query_proj,
    key_proj,
    value_proj,
    out_proj,
    norm_cross,
    cross_query,
    cross_key,
    cross_value,
    cross_out,
    class_table,
    class_pos,
    norm_mlp,
    up_proj,
    down_proj,
    rgb_style,
    color_projection,
    color_bias,
):
    own_count, low_rows, low_width, channels = images.shape
    group_count = styles.shape[0]
    own_place = lax.axis_index("rows")
    own_start = own_place * own_count
    rows_here = 2 * low_rows
    row_width = 2 * low_width
    places = rows_here * row_width
    kernels = kernel_bank.shape[3]
    slice_width = kernel_bank.shape[4]
    head_root = math.sqrt(HD)
    styles_float = styles.astype(FLOAT_KIND)
    mixing = jax.nn.softmax(matmul(styles, select_proj), axis=-1)
    scale_in = matmul(styles, style_proj) + 1.0
    color_scale = matmul(styles, rgb_style) + 1.0
    scale_square = scale_in * scale_in
    own_scale_in = lax.dynamic_slice_in_dim(scale_in, own_start, own_count, 0)
    own_scale_rgb = lax.dynamic_slice_in_dim(color_scale, own_start, own_count, 0)
    widened = jnp.repeat(jnp.repeat(images, 2, axis=1), 2, axis=2).astype(FLOAT_KIND)
    modulated = (widened * own_scale_in[:, None, None, :]).astype(BRAIN)
    gathered = lax.all_gather(modulated, "rows", axis=0, tiled=True)
    framed = jnp.pad(gathered, ((0, 0), (1, 1), (1, 1), (0, 0)))

    def tap_view(tap_index):
        return framed[
            :,
            tap_index // 3 : tap_index // 3 + rows_here,
            tap_index % 3 : tap_index % 3 + row_width,
            :,
        ].reshape(group_count, places, channels)

    def bank_tap(tap_index):
        return kernel_bank[tap_index // 3, tap_index % 3].astype(FLOAT_KIND)

    def mixed_tap(mix, tap_index):
        return accurate_mode("gk,cko->gco", mix, bank_tap(tap_index))

    energy = jnp.zeros((group_count, slice_width), FLOAT_KIND)
    conv_sum = jnp.zeros((group_count, places, slice_width), FLOAT_KIND)
    for tap_index in range(9):
        mixed = mixed_tap(mixing, tap_index)
        energy = energy + accurate_mode("gc,gco->go", scale_square, mixed * mixed)
        conv_sum = conv_sum + contract("gpc,gco->gpo", tap_view(tap_index), mixed.astype(BRAIN))
    demod_scale = lax.rsqrt(energy + 1e-08)
    conv_part = lax.all_to_all(
        conv_sum * demod_scale[:, None, :], "rows", split_axis=0, concat_axis=2, tiled=True
    )
    noise_flat = noise_map.reshape(own_count, places).astype(FLOAT_KIND)
    conv_out = (
        conv_part
        + noise_gain.astype(FLOAT_KIND) * noise_flat[:, :, None]
        + conv_bias.astype(FLOAT_KIND)
    )
    stream_one = jax.nn.silu(conv_out)
    gain_attn = norm_attn.astype(FLOAT_KIND)
    normed_attn, inverse_attn = rms_forward(stream_one, gain_attn)
    normed_group = spread_group(normed_attn.astype(BRAIN))
    query_heads = split_heads(matmul(normed_group, query_proj).astype(BRAIN))
    key_heads = split_heads(matmul(normed_group, key_proj).astype(BRAIN))
    value_heads = split_heads(matmul(normed_group, value_proj).astype(BRAIN))
    key_square = jnp.transpose(
        jnp.sum(jnp.square(key_heads.astype(FLOAT_KIND)), axis=-1), (0, 2, 1)
    )

    def self_scores():
        raw_scores = contract("gphd,gshd->ghps", query_heads, key_heads)
        return (2.0 * raw_scores - key_square[:, :, None, :]) / head_root

    scores = self_scores()
    highest = jnp.max(scores, axis=-1, keepdims=True)
    exponent = jnp.exp(scores - highest)
    row_mass = jnp.sum(exponent, axis=-1, keepdims=True)
    log_mass = highest + jnp.log(row_mass)
    weights_attn = (exponent / row_mass).astype(BRAIN)
    attended = merge_heads(contract("ghps,gshd->gphd", weights_attn, value_heads).astype(BRAIN))
    attn_branch = collect_group(matmul(attended, out_proj))
    stream_two = stream_one + attn_branch
    class_ids = jnp.arange(class_table.shape[0], dtype=jnp.int32)
    one_hot = (labels[:, None] == class_ids[None, :]).astype(BRAIN)
    class_rows = matmul(one_hot, class_table)
    context = (class_rows[:, None, :] + class_pos.astype(FLOAT_KIND)[None, :, :]).astype(BRAIN)
    gain_cross = norm_cross.astype(FLOAT_KIND)
    normed_cross, inverse_cross = rms_forward(stream_two, gain_cross)
    cross_group = spread_group(normed_cross.astype(BRAIN))
    cross_queries = split_heads(matmul(cross_group, cross_query).astype(BRAIN))
    cross_keys = split_heads(matmul(context, cross_key).astype(BRAIN))
    cross_values = split_heads(matmul(context, cross_value).astype(BRAIN))
    cross_prob = jax.nn.softmax(
        contract("gphd,gjhd->ghpj", cross_queries, cross_keys) / head_root, axis=-1
    )
    cross_weights = cross_prob.astype(BRAIN)
    cross_attended = merge_heads(
        contract("ghpj,gjhd->gphd", cross_weights, cross_values).astype(BRAIN)
    )
    cross_branch = collect_group(matmul(cross_attended, cross_out))
    stream_three = stream_two + cross_branch
    gain_mlp = norm_mlp.astype(FLOAT_KIND)
    normed_mlp, inverse_mlp = rms_forward(stream_three, gain_mlp)
    normed_mlp = normed_mlp.astype(BRAIN)
    mlp_in = spread_mlp(normed_mlp)
    up_use, down_use = (up_proj, down_proj)
    inner_act = matmul(mlp_in, up_use)
    activated = jax.nn.silu(inner_act).astype(BRAIN)
    mlp_branch = matmul(activated, down_use)
    mlp_branch = collect_mlp(mlp_branch)
    stream_four = stream_three + mlp_branch
    features = stream_four.reshape(own_count, rows_here, row_width, channels)
    color_single_float = color_projection.astype(FLOAT_KIND)
    colored_output = stream_four * own_scale_rgb[:, None, :]
    color_image = (
        accurate_mode("txk,kr->trx", colored_output, color_single_float)
        + color_bias.astype(FLOAT_KIND)[None, :, None]
    )
    color_image = color_image.reshape(own_count, 3, rows_here, row_width)
    own_live = lax.dynamic_index_in_dim(counts, own_place, 0, keepdims=False)
    live_mask = (jnp.arange(own_count, dtype=jnp.int32) < own_live).astype(FLOAT_KIND)
    image_gradient = cot_image.reshape(own_count, 3, places) * live_mask[:, None, None]
    grad_four = (
        cot_features.reshape(own_count, places, channels).astype(FLOAT_KIND)
        * live_mask[:, None, None]
    )
    colored_gradient = accurate_mode("qje,nj->qen", image_gradient, color_single_float)
    grad_four = grad_four + colored_gradient * own_scale_rgb[:, None, :]
    grad_scale_rgb_own = jnp.sum(colored_gradient * stream_four, axis=1)
    color_projection_gradient = accurate_mode("qbw,qhb->wh", colored_output, image_gradient)
    grad_rgb_bias = jnp.sum(image_gradient, axis=(0, 2))
    grad_branch = grad_four.astype(BRAIN)
    grad_branch = spread_mlp(grad_branch)
    grad_down = contract("gpf,gpc->fc", activated, grad_branch)
    grad_inner = (contract("gpc,fc->gpf", grad_branch, down_use) * silu_slope(inner_act)).astype(
        BRAIN
    )
    grad_up = contract("gpc,gpf->cf", mlp_in, grad_inner)
    grad_normed_mlp = contract("gpf,cf->gpc", grad_inner, up_use)
    grad_normed_mlp = collect_mlp(grad_normed_mlp)
    back_norm, grad_norm_mlp = rms_backward(stream_three, inverse_mlp, gain_mlp, grad_normed_mlp)
    grad_three = grad_four + back_norm
    grad_branch = spread_group(grad_three.astype(BRAIN))
    grad_cross_out = contract("gpc,gpd->cd", cross_attended, grad_branch)
    grad_cross_att = split_heads(contract("gpd,cd->gpc", grad_branch, cross_out).astype(BRAIN))
    grad_prob = contract("gphd,gjhd->ghpj", grad_cross_att, cross_values)
    grad_cross_values = merge_heads(
        contract("ghpj,gphd->gjhd", cross_weights, grad_cross_att).astype(BRAIN)
    )
    grad_scores = cross_prob * (grad_prob - jnp.sum(cross_prob * grad_prob, axis=-1, keepdims=True))
    grad_raw = (grad_scores / head_root).astype(BRAIN)
    grad_cross_queries = merge_heads(
        contract("ghpj,gjhd->gphd", grad_raw, cross_keys).astype(BRAIN)
    )
    grad_cross_keys = merge_heads(
        contract("ghpj,gphd->gjhd", grad_raw, cross_queries).astype(BRAIN)
    )
    grad_cross_query = contract("gpc,gpd->cd", cross_group, grad_cross_queries)
    grad_cross_key = contract("gjc,gjd->cd", context, grad_cross_keys)
    grad_cross_value = contract("gjc,gjd->cd", context, grad_cross_values)
    grad_context = contract("gjd,cd->gjc", grad_cross_keys, cross_key) + contract(
        "gjd,cd->gjc", grad_cross_values, cross_value
    )
    grad_class_pos = jnp.sum(grad_context, axis=0)
    grad_class_table = accurate_mode(
        "gk,gc->kc", one_hot.astype(FLOAT_KIND), jnp.sum(grad_context, axis=1)
    )
    grad_normed_cross = collect_group(contract("gpd,cd->gpc", grad_cross_queries, cross_query))
    back_norm, grad_norm_cross = rms_backward(
        stream_two, inverse_cross, gain_cross, grad_normed_cross
    )
    grad_two = grad_three + back_norm
    grad_branch = spread_group(grad_two.astype(BRAIN))
    grad_out_proj = contract("gpc,gpd->cd", attended, grad_branch)
    grad_attended = split_heads(contract("gpd,cd->gpc", grad_branch, out_proj).astype(BRAIN))
    probability = jnp.exp(self_scores() - log_mass)
    grad_prob = contract("gphd,gshd->ghps", grad_attended, value_heads)
    grad_scores = probability * (
        grad_prob - jnp.sum(probability * grad_prob, axis=-1, keepdims=True)
    )
    grad_raw = (grad_scores * (2.0 / head_root)).astype(BRAIN)
    grad_key_square = -jnp.sum(grad_scores, axis=2) / head_root
    grad_queries = merge_heads(contract("ghps,gshd->gphd", grad_raw, key_heads).astype(BRAIN))
    key_total = (
        contract("ghps,gphd->gshd", grad_raw, query_heads)
        + 2.0
        * key_heads.astype(FLOAT_KIND)
        * jnp.transpose(grad_key_square, (0, 2, 1))[:, :, :, None]
    )
    value_total = contract("ghps,gphd->gshd", weights_attn, grad_attended)
    grad_keys = merge_heads(key_total).astype(BRAIN)
    grad_values = merge_heads(value_total).astype(BRAIN)
    grad_query_proj = contract("gpc,gpd->cd", normed_group, grad_queries)
    grad_key_proj = contract("gpc,gpd->cd", normed_group, grad_keys)
    grad_value_proj = contract("gpc,gpd->cd", normed_group, grad_values)
    grad_normed = collect_group(
        contract("gpd,cd->gpc", grad_queries, query_proj)
        + contract("gpd,cd->gpc", grad_keys, key_proj)
        + contract("gpd,cd->gpc", grad_values, value_proj)
    )
    back_norm, grad_norm_attn = rms_backward(stream_one, inverse_attn, gain_attn, grad_normed)
    grad_one = grad_two + back_norm
    grad_conv = grad_one * silu_slope(conv_out)
    grad_conv_bias = jnp.sum(grad_conv, axis=(0, 1))
    grad_noise_gain = jnp.sum(grad_conv * noise_flat[:, :, None], axis=(0, 1))
    grad_part = lax.all_to_all(grad_conv, "rows", split_axis=2, concat_axis=0, tiled=True)
    grad_demod = jnp.sum(grad_part * conv_sum, axis=1)
    grad_energy = -0.5 * grad_demod * demod_scale**3
    grad_taps = (grad_part * demod_scale[:, None, :]).astype(BRAIN)
    bank_pieces = []
    grad_mixing = jnp.zeros((group_count, kernels), FLOAT_KIND)
    grad_square = jnp.zeros((group_count, channels), FLOAT_KIND)
    for tap_index in range(9):
        mixed = mixed_tap(mixing, tap_index)
        kernel_grad = contract("gpc,gpo->gco", tap_view(tap_index), grad_taps)
        grad_mixed = kernel_grad + 2.0 * scale_square[:, :, None] * mixed * grad_energy[:, None, :]
        bank_pieces.append(accurate_mode("gk,gco->cko", mixing, grad_mixed))
        grad_mixing = grad_mixing + accurate_mode("gco,cko->gk", grad_mixed, bank_tap(tap_index))
        grad_square = grad_square + jnp.sum(mixed * mixed * grad_energy[:, None, :], axis=2)
    grad_bank = jnp.stack(bank_pieces).reshape(3, 3, channels, kernels, slice_width)
    count = own_count * lax.axis_size("rows")
    spread = jnp.zeros((count, rows_here + 2, row_width + 2, channels), FLOAT_KIND)
    for tap_index in range(9):
        mixed_low = mixed_tap(mixing, tap_index).astype(BRAIN)
        piece = contract("gpo,gco->gpc", grad_taps, mixed_low).reshape(
            count, rows_here, row_width, channels
        )
        spread = spread.at[
            :,
            tap_index // 3 : tap_index // 3 + rows_here,
            tap_index % 3 : tap_index % 3 + row_width,
            :,
        ].add(piece)
    grad_modulated = lax.psum_scatter(
        spread[:, 1 : rows_here + 1, 1 : row_width + 1, :], "rows", scatter_dimension=0, tiled=True
    )
    grad_scale_own = jnp.sum(grad_modulated * widened, axis=(1, 2))
    grad_widened = grad_modulated * own_scale_in[:, None, None, :]
    images_raw = jnp.sum(
        grad_widened.reshape(own_count, low_rows, 2, low_width, 2, channels), axis=(2, 4)
    )
    zero_rows = jnp.zeros((group_count, channels), FLOAT_KIND)
    grad_scale_in = 2.0 * scale_in * grad_square + lax.dynamic_update_slice_in_dim(
        zero_rows, grad_scale_own, own_start, 0
    )
    grad_scale_rgb = lax.dynamic_update_slice_in_dim(zero_rows, grad_scale_rgb_own, own_start, 0)
    grad_logit = mixing * (grad_mixing - jnp.sum(mixing * grad_mixing, axis=-1, keepdims=True))
    grad_select = accurate_mode("gz,gk->zk", styles_float, grad_logit)
    grad_style_proj = accurate_mode("gz,gc->zc", styles_float, grad_scale_in)
    grad_rgb_style = accurate_mode("gz,gc->zc", styles_float, grad_scale_rgb)
    style_part = (
        accurate_mode("gk,zk->gz", grad_logit, select_proj.astype(FLOAT_KIND))
        + accurate_mode("gc,zc->gz", grad_scale_in, style_proj.astype(FLOAT_KIND))
        + accurate_mode("gc,zc->gz", grad_scale_rgb, rgb_style.astype(FLOAT_KIND))
    )
    style_summed = lax.psum(style_part, "rows")
    (
        grad_select,
        grad_style_proj,
        grad_rgb_style,
        grad_conv_bias,
        grad_noise_gain,
        grad_norm_attn,
        grad_norm_cross,
        grad_norm_mlp,
        grad_class_table,
        grad_class_pos,
        color_projection_gradient,
        grad_rgb_bias,
        count_sum,
    ) = lax.psum(
        (
            grad_select,
            grad_style_proj,
            grad_rgb_style,
            grad_conv_bias,
            grad_noise_gain,
            grad_norm_attn,
            grad_norm_cross,
            grad_norm_mlp,
            grad_class_table,
            grad_class_pos,
            color_projection_gradient,
            grad_rgb_bias,
            jnp.sum(counts.astype(FLOAT_KIND)),
        ),
        ("dp", "rows"),
    )
    sample_total = count_sum / lax.axis_size("rows")
    (
        grad_bank,
        grad_query_proj,
        grad_key_proj,
        grad_value_proj,
        grad_out_proj,
        grad_cross_query,
        grad_cross_key,
        grad_cross_value,
        grad_cross_out,
        grad_up,
        grad_down,
    ) = (
        lax.psum_scatter(grad_bank, "dp", scatter_dimension=2, tiled=True),
        lax.psum_scatter(grad_query_proj, "dp", scatter_dimension=0, tiled=True),
        lax.psum_scatter(grad_key_proj, "dp", scatter_dimension=0, tiled=True),
        lax.psum_scatter(grad_value_proj, "dp", scatter_dimension=0, tiled=True),
        lax.psum_scatter(grad_out_proj, "dp", scatter_dimension=1, tiled=True),
        lax.psum_scatter(grad_cross_query, "dp", scatter_dimension=0, tiled=True),
        lax.psum_scatter(grad_cross_key, "dp", scatter_dimension=0, tiled=True),
        lax.psum_scatter(grad_cross_value, "dp", scatter_dimension=0, tiled=True),
        lax.psum_scatter(grad_cross_out, "dp", scatter_dimension=1, tiled=True),
        lax.psum_scatter(grad_up, "dp", scatter_dimension=0, tiled=True),
        lax.psum_scatter(grad_down, "dp", scatter_dimension=1, tiled=True),
    )
    return (
        features,
        color_image,
        images_raw / sample_total,
        style_summed / sample_total,
        grad_bank / sample_total,
        grad_select / sample_total,
        grad_style_proj / sample_total,
        grad_conv_bias / sample_total,
        grad_noise_gain / sample_total,
        grad_norm_attn / sample_total,
        grad_query_proj / sample_total,
        grad_key_proj / sample_total,
        grad_value_proj / sample_total,
        grad_out_proj / sample_total,
        grad_norm_cross / sample_total,
        grad_cross_query / sample_total,
        grad_cross_key / sample_total,
        grad_cross_value / sample_total,
        grad_cross_out / sample_total,
        grad_class_table / sample_total,
        grad_class_pos / sample_total,
        grad_norm_mlp / sample_total,
        grad_up / sample_total,
        grad_down / sample_total,
        grad_rgb_style / sample_total,
        color_projection_gradient / sample_total,
        grad_rgb_bias / sample_total,
    )


def solution(mesh):
    placed = (
        P(("dp", "rows"), None, None, None),
        P("dp", None),
        P("dp"),
        P(("dp", "rows"), None, None),
        P("dp"),
        P(("dp", "rows"), None, None, None),
        P(("dp", "rows"), None, None, None),
        P(None, None, None, None, "rows"),
        P(),
        P(),
        P(),
        P(),
        P(),
        P(None, "rows"),
        P(None, "rows"),
        P(None, "rows"),
        P("rows", None),
        P(),
        P(None, "rows"),
        P(None, "rows"),
        P(None, "rows"),
        P("rows", None),
        P(),
        P(),
        P(),
        P(None, "rows"),
        P("rows", None),
        P(),
        P(),
        P(),
    )
    return jax.shard_map(
        local,
        mesh=mesh,
        in_specs=placed,
        out_specs=(
            P(("dp", "rows"), None, None, None),
            P(("dp", "rows"), None, None, None),
            P(("dp", "rows"), None, None, None),
            P("dp", None),
            P(None, None, "dp", None, "rows"),
            P(),
            P(),
            P(),
            P(),
            P(),
            P("dp", "rows"),
            P("dp", "rows"),
            P("dp", "rows"),
            P("rows", "dp"),
            P(),
            P("dp", "rows"),
            P("dp", "rows"),
            P("dp", "rows"),
            P("rows", "dp"),
            P(),
            P(),
            P(),
            P("dp", "rows"),
            P("rows", "dp"),
            P(),
            P(),
            P(),
        ),
        check_vma=False,
    )
```

profile of v0, /device:TPU:0, one launch (start us, length us, event | category | flops | bytes accessed | tf_op | source)
XLA Modules:
  0.0 3087.3 jit_solution(16564491557250231375)
XLA Ops:
  124.6 11.9 pad_slice_fusion
  162.2 14.3 all-to-all-done
  183.1 23.7 all-gather.11.cloned.1.call-done
  222.6 44.6 %reduce-scatter.22.cloned.1.call-done = f32[1,256,1024]{2,1,0:T(8,128)} async-done(((f32[4,256,1024]{2,1,0:T(8,128)}), f32[1,256,1024]{2,1,0:T(8,128)}) %reduce-scatter.22.cloned.1.call-update) | async-done | bytes 1048592 | tf_op jit(solution)/shard_map/reduce_scatter | solution.py:60
  276.4 17.3 all-gather.13.cloned.1.call-done
  305.8 43.3 %reduce-scatter.24.cloned.1.call-done = f32[1,256,1024]{2,1,0:T(8,128)} async-done(((f32[4,256,1024]{2,1,0:T(8,128)}), f32[1,256,1024]{2,1,0:T(8,128)}) %reduce-scatter.24.cloned.1.call-update) | async-done | bytes 1048592 | tf_op jit(solution)/shard_map/reduce_scatter | solution.py:60
  365.6 10.9 all-gather.15.cloned.1.call-done
  382.5 18.8 all-gather.21.cloned.1.call-done
  421.9 36.4 %reduce-scatter.28.cloned.1.call-done = f32[1,256,1024]{2,1,0:T(8,128)} async-done(((f32[4,256,1024]{2,1,0:T(8,128)}), f32[1,256,1024]{2,1,0:T(8,128)}) %reduce-scatter.28.cloned.1.call-update) | async-done | bytes 1048592 | tf_op jit(solution)/shard_map/reduce_scatter | solution.py:68
  461.0 44.6 %reduce-scatter.26.cloned.1.call-done = f32[1,256,1024]{2,1,0:T(8,128)} async-done(((f32[4,256,1024]{2,1,0:T(8,128)}), f32[1,256,1024]{2,1,0:T(8,128)}) %reduce-scatter.26.cloned.1.call-update) | async-done | bytes 1048592 | tf_op jit(solution)/shard_map/reduce_scatter | solution.py:68
  510.1 22.7 all-gather.17.cloned.1.call-done
  540.7 44.6 %reduce-scatter.30.cloned.1.call-done = f32[1,256,1024]{2,1,0:T(8,128)} async-done(((f32[4,256,1024]{2,1,0:T(8,128)}), f32[1,256,1024]{2,1,0:T(8,128)}) %reduce-scatter.30.cloned.1.call-update) | async-done | bytes 1048592 | tf_op jit(solution)/shard_map/reduce_scatter | solution.py:60
  590.4 22.5 all-gather.19.cloned.1.call-done
  648.4 44.6 %reduce-scatter.32.cloned.1.call-done = f32[1,256,1024]{2,1,0:T(8,128)} async-done(((f32[4,256,1024]{2,1,0:T(8,128)}), f32[1,256,1024]{2,1,0:T(8,128)}) %reduce-scatter.32.cloned.1.call-update) | async-done | bytes 1048592 | tf_op jit(solution)/shard_map/reduce_scatter | solution.py:60
  708.8 12.1 all-to-all-done.1
  755.1 22.2 scatter-add.31
  787.1 22.0 scatter-add.34
  822.7 20.7 scatter-add.36
  851.3 20.7 scatter-add.39
  885.6 20.7 scatter-add.41
  914.2 20.7 scatter-add.44
  990.8 20.3 multiply_reduce_fusion.7
  1044.2 13.3 bitcast_dynamic-update-slice_fusion.8
  1057.5 13.5 bitcast_dynamic-update-slice_fusion.7
  1071.0 13.3 bitcast_dynamic-update-slice_fusion.6
  1094.3 13.6 bitcast_dynamic-update-slice_fusion.5
  1107.9 13.3 bitcast_dynamic-update-slice_fusion.4
  1121.2 13.2 bitcast_dynamic-update-slice_fusion.3
  1134.4 13.5 bitcast_dynamic-update-slice_fusion.2
  1147.9 13.3 bitcast_dynamic-update-slice_fusion.1
  1161.2 13.3 bitcast_dynamic-update-slice_fusion
  1174.5 48.7 %copy.342 = f32[3,3,1024,8,256]{4,3,1,0,2:T(8,128)} copy(f32[3,3,1024,8,256]{4,3,2,1,0:T(8,128)} %bitcast.125) | data formatting | bytes 150994944
  1223.2 51.9 %copy.345 = f32[128,8,72,256]{3,1,2,0:T(8,128)} copy(f32[128,8,72,256]{3,2,1,0:T(8,128)} %bitcast.164) | data formatting | bytes 150994944
  1278.3 15.7 fusion.160
  1294.1 14.7 fusion.208
  1308.8 14.5 fusion.205
  1323.4 14.5 fusion.202
  1338.0 14.4 fusion.199
  1352.8 14.4 fusion.196
  1367.2 14.5 fusion.193
  1381.8 14.5 fusion.190
  1396.4 14.7 multiply_reduce_fusion.22
  1411.5 42.2 %all-reduce.2 = (f32[]{:T(128)}, f32[512,8]{0,1:T(8,128)S(1)}, f32[1024]{0:T(1024)S(1)}, f32[1024]{0:T(1024)S(1)}, f32[1024]{0:T(1024)S(1)}, /*index=5*/f32[1024...) all-reduce(f32[]{:T(128)} %convert_reduce_fusion, ...), channel_id=1, replica_groups=mesh['dp'=8,'rows'=4] {'dp','rows'}, use_global_device_ids=true, to_apply=%region_26.27 | all-reduce | flops 12292 | bytes 98336 | tf_op jit(solution)/shard_map/psum | solution.py:367
  1469.2 46.9 %reduce-scatter.36.cloned.1.call-done = f32[128,256]{1,0:T(8,128)} async-done(((f32[1024,256]{1,0:T(8,128)}), f32[128,256]{1,0:T(8,128)}) %reduce-scatter.36.cloned.1.call-update) | async-done | bytes 131088 | tf_op jit(solution)/shard_map/reduce_scatter | solution.py:400
  1517.7 90.0 %reduce-scatter.54.cloned.1.call-done = f32[1024,128]{1,0:T(8,128)} async-done(((f32[1024,1024]{1,0:T(8,128)}), f32[1024,128]{1,0:T(8,128)}) %reduce-scatter.54.cloned.1.call-update) | async-done | bytes 524304 | tf_op jit(solution)/shard_map/reduce_scatter | solution.py:409
  1609.6 89.5 %reduce-scatter.52.cloned.1.call-done = f32[128,1024]{1,0:T(8,128)} async-done(((f32[1024,1024]{1,0:T(8,128)}), f32[128,1024]{1,0:T(8,128)}) %reduce-scatter.52.cloned.1.call-update) | async-done | bytes 524304 | tf_op jit(solution)/shard_map/reduce_scatter | solution.py:408
  1714.7 172.7 %all-reduce.6.cloned.1.call-done = (f32[512,1024]{0,1:T(8,128)}, f32[1000,1024]{1,0:T(8,128)}, f32[16,1024]{1,0:T(8,128)}, f32[512,1024]{0,1:T(8,128)}) async-done(((f32[512,1024]{0,1:T(8,128)}, f32[1000,1024]{1,0:T(8,128)}, f32[16,1024]{1,0:T(8,128)}, f32[512,1024]{0,1:T(8,128)}), (f32[512,1024]{0,1:T(8,128)}, f32[1000,1024]{1,0:T(8,128)}, f32[16,1024]{1,0:T(8,128)}, ...) | async-done | bytes 8355856 | tf_op jit(solution)/shard_map/psum | solution.py:367
  1902.3 1166.9 %reduce-scatter.56.cloned.1.call-done = f32[128,18432]{1,0:T(8,128)} async-done(((f32[1024,18432]{1,0:T(8,128)}), f32[128,18432]{1,0:T(8,128)}) %reduce-scatter.56.cloned.1.call-update) | async-done | bytes 9437200
  (663 shorter events, 548.6 us)
Async XLA Ops:
  7.2 369.4 %copy-start = (bf16[1024,1024]{1,0:T(8,128)(2,1)S(1)}, bf16[1024,1024]{1,0:T(8,128)(2,1)}, u32[]{:S(2)}) copy-start(bf16[1024,1024]{1,0:T(8,128)(2,1)} %param.73) | copy-start | bytes 6291460
  7.2 117.4 %all-gather.9.cloned.1.call-start = ((), (), s32[]{:S(2)}) async-start(), calls=%async_computation.20 | async-start | bytes 2621440 | tf_op jit(solution)/shard_map/all_gather | solution.py:122
  15.6 97.1 %copy-start.99 = (f32[4,8]{1,0:T(4,128)}, f32[4,8]{1,0:T(4,128)S(1)}, u32[]{:S(2)}) copy-start(f32[4,8]{1,0:T(4,128)S(1)} %fusion.302) | copy-start | bytes 388
  158.1 18.3 all-to-all-start
  162.0 44.8 %all-gather.11.cloned.1.call-start = ((), (), s32[]{:S(2)}) async-start(), calls=%async_computation.21 | async-start | bytes 2621440 | tf_op jit(solution)/shard_map/all_gather | solution.py:56
  162.0 105.2 %copy-start.136 = (f32[1024]{0:T(1024)}, f32[1024]{0:T(1024)S(1)}, u32[]{:S(2)}) copy-start(f32[1024]{0:T(1024)S(1)} %convert_element_type.309) | copy-start | bytes 12292
  162.1 105.1 %copy-start.138 = (f32[1024]{0:T(1024)}, f32[1024]{0:T(1024)S(1)}, u32[]{:S(2)}) copy-start(f32[1024]{0:T(1024)S(1)} %convert_element_type.306) | copy-start | bytes 12292
  162.2 105.0 %copy-start.153 = (f32[256]{0:T(256)}, f32[256]{0:T(256)S(1)}, u32[]{:S(2)}) copy-start(f32[256]{0:T(256)S(1)} %reshape.1258) | copy-start | bytes 3076
  183.0 84.2 %reduce-scatter.22.cloned.1.call-start = ((), (), s32[]{:S(2)}) async-start(), calls=%async_computation.22 | async-start | bytes 5242880 | tf_op jit(solution)/shard_map/reduce_scatter | solution.py:60
  222.5 48.5 %copy-start.156 = (bf16[16,1024]{1,0:T(8,128)(2,1)S(1)}, bf16[16,1024]{1,0:T(8,128)(2,1)}, u32[]{:S(2)}) copy-start(bf16[16,1024]{1,0:T(8,128)(2,1)} %param.71) | copy-start | bytes 98308
  222.5 48.5 %copy-start.175 = (s32[4]{0:T(128)S(1)}, s32[4]{0:T(128)}, u32[]{:S(2)}) copy-start(s32[4]{0:T(128)} %param.50) | copy-start | bytes 52
  222.5 71.2 %all-gather.13.cloned.1.call-start = ((), (), s32[]{:S(2)}) async-start(), calls=%async_computation.23 | async-start | bytes 2621440 | tf_op jit(solution)/shard_map/all_gather | solution.py:56
  222.6 48.4 %copy-start.148 = (f32[1024]{0:T(1024)}, f32[1024]{0:T(1024)S(1)}, u32[]{:S(2)}) copy-start(f32[1024]{0:T(1024)S(1)} %convert_element_type.322) | copy-start | bytes 12292
  271.0 78.2 %reduce-scatter.24.cloned.1.call-start = ((), (), s32[]{:S(2)}) async-start(), calls=%async_computation.24 | async-start | bytes 5242880 | tf_op jit(solution)/shard_map/reduce_scatter | solution.py:60
  304.5 72.1 %all-gather.15.cloned.1.call-start = ((), (), s32[]{:S(2)}) async-start(), calls=%async_computation.25 | async-start | bytes 2621440 | tf_op jit(solution)/shard_map/all_gather | solution.py:64
  353.8 47.5 %all-gather.21.cloned.1.call-start = ((), (), s32[]{:S(2)}) async-start(), calls=%async_computation.43 | async-start | bytes 2621440 | tf_op jit(solution)/shard_map/all_gather | solution.py:64
  365.4 92.9 %reduce-scatter.28.cloned.1.call-start = ((), (), s32[]{:S(2)}) async-start(), calls=%async_computation.27 | async-start | bytes 5242880 | tf_op jit(solution)/shard_map/reduce_scatter | solution.py:68
  413.7 91.9 %reduce-scatter.26.cloned.1.call-start = ((), (), s32[]{:S(2)}) async-start(), calls=%async_computation.26 | async-start | bytes 5242880 | tf_op jit(solution)/shard_map/reduce_scatter | solution.py:68
  421.8 83.7 %copy-start.79 = (f32[1,16,16,1024]{3,2,1,0:T(8,128)S(1)}, f32[1,16,16,1024]{3,2,1,0:T(8,128)}, u32[]{:S(2)}) copy-start(f32[1,16,16,1024]{3,2,1,0:T(8,128)} %copy-done.78) | copy-start | bytes 3145732
  421.9 110.9 %all-gather.17.cloned.1.call-start = ((), (), s32[]{:S(2)}) async-start(), calls=%async_computation.28 | async-start | bytes 2621440 | tf_op jit(solution)/shard_map/all_gather | solution.py:56
  510.1 75.3 %reduce-scatter.30.cloned.1.call-start = ((), (), s32[]{:S(2)}) async-start(), calls=%async_computation.29 | async-start | bytes 5242880 | tf_op jit(solution)/shard_map/reduce_scatter | solution.py:60
  537.8 47.5 %copy-start.22 = (f32[1,256,1024]{2,1,0:T(8,128)S(1)}, f32[1,256,1024]{2,1,0:T(8,128)}, u32[]{:S(2)}) copy-start(f32[1,256,1024]{2,1,0:T(8,128)} %copy-done.21) | copy-start | bytes 3145732
  537.8 47.5 %copy-start.149 = (f32[1024]{0:T(1024)S(1)}, f32[1024]{0:T(1024)}, u32[]{:S(2)}) copy-start(f32[1024]{0:T(1024)} %copy-done.148) | copy-start | bytes 12292
  537.8 47.5 %copy-start.167 = (f32[256]{0:T(256)S(1)}, f32[256]{0:T(256)}, u32[]{:S(2)}) copy-start(f32[256]{0:T(256)} %copy-done.166) | copy-start | bytes 3076
  540.6 49.7 %copy-start.129 = (f32[4,4,256]{2,1,0:T(4,128)S(1)}, f32[4,4,256]{2,1,0:T(4,128)}, u32[]{:S(2)}) copy-start(f32[4,4,256]{2,1,0:T(4,128)} %copy-done.128) | copy-start | bytes 49156
  540.7 72.2 %all-gather.19.cloned.1.call-start = ((), (), s32[]{:S(2)}) async-start(), calls=%async_computation.30 | async-start | bytes 2621440 | tf_op jit(solution)/shard_map/all_gather | solution.py:56
  590.1 102.9 %reduce-scatter.32.cloned.1.call-start = ((), (), s32[]{:S(2)}) async-start(), calls=%async_computation.31 | async-start | bytes 5242880 | tf_op jit(solution)/shard_map/reduce_scatter | solution.py:60
  648.4 47.2 %copy-start.90 = (f32[1,256,1024]{2,1,0:T(8,128)S(1)}, f32[1,256,1024]{2,1,0:T(8,128)}, u32[]{:S(2)}) copy-start(f32[1,256,1024]{2,1,0:T(8,128)} %get-tuple-element.254) | copy-start | bytes 3145732
  702.9 18.0 all-to-all-start.1
  706.5 377.9 %reduce-scatter.34.cloned.1.call-start = ((), (), s32[]{:S(2)}) async-start(), calls=%async_computation.32 | async-start | bytes 5242880 | tf_op jit(solution)/shard_map/reduce_scatter | solution.py:330
  941.1 517.0 %reduce-scatter.38.cloned.1.call-start = ((), (), s32[]{:S(2)}) async-start(), calls=%async_computation.34 | async-start | bytes 1179648 | tf_op jit(solution)/shard_map/reduce_scatter | solution.py:401
  945.5 514.2 %reduce-scatter.40.cloned.1.call-start = ((), (), s32[]{:S(2)}) async-start(), calls=%async_computation.35 | async-start | bytes 1179648 | tf_op jit(solution)/shard_map/reduce_scatter | solution.py:402
  949.7 511.6 %reduce-scatter.44.cloned.1.call-start = ((), (), s32[]{:S(2)}) async-start(), calls=%async_computation.37 | async-start | bytes 1179648 | tf_op jit(solution)/shard_map/reduce_scatter | solution.py:404
  953.5 509.4 %reduce-scatter.46.cloned.1.call-start = ((), (), s32[]{:S(2)}) async-start(), calls=%async_computation.38 | async-start | bytes 1179648 | tf_op jit(solution)/shard_map/reduce_scatter | solution.py:405
  955.4 509.1 %reduce-scatter.48.cloned.1.call-start = ((), (), s32[]{:S(2)}) async-start(), calls=%async_computation.39 | async-start | bytes 1179648 | tf_op jit(solution)/shard_map/reduce_scatter | solution.py:406
  957.2 508.9 %reduce-scatter.50.cloned.1.call-start = ((), (), s32[]{:S(2)}) async-start(), calls=%async_computation.40 | async-start | bytes 1179648 | tf_op jit(solution)/shard_map/reduce_scatter | solution.py:407
  960.6 507.0 %reduce-scatter.42.cloned.1.call-start = ((), (), s32[]{:S(2)}) async-start(), calls=%async_computation.36 | async-start | bytes 1179648 | tf_op jit(solution)/shard_map/reduce_scatter | solution.py:403
  964.0 552.2 %reduce-scatter.36.cloned.1.call-start = ((), (), s32[]{:S(2)}) async-start(), calls=%async_computation.33 | async-start | bytes 1179648 | tf_op jit(solution)/shard_map/reduce_scatter | solution.py:400
  967.4 640.3 %reduce-scatter.54.cloned.1.call-start = ((), (), s32[]{:S(2)}) async-start(), calls=%async_computation.42 | async-start | bytes 4718592 | tf_op jit(solution)/shard_map/reduce_scatter | solution.py:409
  974.9 724.2 %reduce-scatter.52.cloned.1.call-start = ((), (), s32[]{:S(2)}) async-start(), calls=%async_computation.41 | async-start | bytes 4718592 | tf_op jit(solution)/shard_map/reduce_scatter | solution.py:408
  981.7 905.8 %all-reduce.6.cloned.1.call-start = ((), (), s32[]{:S(2)}) async-start(), calls=%async_computation.45 | async-start | bytes 16711680 | tf_op jit(solution)/shard_map/psum | solution.py:367
  1089.4 1979.9 %reduce-scatter.56.cloned.1.call-start = ((), (), s32[]{:S(2)}) async-start(), calls=%async_computation.44 | async-start | bytes 84934656
  1396.4 60.3 %copy-start.184 = (bf16[512,8]{0,1:T(8,128)(2,1)S(1)}, bf16[512,8]{0,1:T(8,128)(2,1)}, u32[]{:S(2)}) copy-start(bf16[512,8]{0,1:T(8,128)(2,1)} %param.56) | copy-start | bytes 24580
  1411.1 289.9 %copy-start.86 = (f32[1,16,16,1024]{3,2,1,0:T(8,128)S(1)}, f32[1,16,16,1024]{3,2,1,0:T(8,128)}, u32[]{:S(2)}) copy-start(f32[1,16,16,1024]{3,2,1,0:T(8,128)} %get-tuple-element.290) | copy-start | bytes 3145732
  1411.1 293.4 %copy-start.87 = (bf16[512,1024]{1,0:T(8,128)(2,1)S(1)}, bf16[512,1024]{1,0:T(8,128)(2,1)}, u32[]{:S(2)}) copy-start(bf16[512,1024]{1,0:T(8,128)(2,1)} %param.57) | copy-start | bytes 3145732
  1411.1 293.4 %copy-start.125 = (f32[4,1024]{1,0:T(4,128)S(1)}, f32[4,1024]{1,0:T(4,128)}, u32[]{:S(2)}) copy-start(f32[4,1024]{1,0:T(4,128)} %copy-done.124) | copy-start | bytes 49156
  1459.7 245.8 %copy-start.88 = (bf16[512,1024]{1,0:T(8,128)(2,1)S(1)}, bf16[512,1024]{1,0:T(8,128)(2,1)}, u32[]{:S(2)}) copy-start(bf16[512,1024]{1,0:T(8,128)(2,1)} %param.75) | copy-start | bytes 3145732
  1459.7 245.8 %copy-start.131 = (f32[4,1024]{1,0:T(4,128)S(1)}, f32[4,1024]{1,0:T(4,128)}, u32[]{:S(2)}) copy-start(f32[4,1024]{1,0:T(4,128)} %copy-done.130) | copy-start | bytes 49156
  (168 other events, 1679.1 us)
Sparse Core Ops, SparseCore 0:
  15.2 25.2 all-gather.8
  183.2 23.5 all-gather.10
  222.7 44.5 reduce-scatter.21
  271.1 22.5 all-gather.12
  304.6 44.4 reduce-scatter.23
  354.0 22.5 all-gather.14
  378.7 22.5 all-gather.20
  413.8 44.4 reduce-scatter.27
  461.0 44.4 reduce-scatter.25
  510.2 22.5 all-gather.16
  540.8 44.4 reduce-scatter.29
  590.2 22.5 all-gather.18
  648.5 44.4 reduce-scatter.31
  941.2 44.5 reduce-scatter.33
  989.4 63.5 reduce-scatter.37
  1056.2 62.4 reduce-scatter.39
  1122.4 62.5 reduce-scatter.43
  1188.2 62.5 reduce-scatter.45
  1254.6 62.5 reduce-scatter.47
  1320.5 62.8 reduce-scatter.49
  1387.1 62.9 reduce-scatter.41
  1453.5 62.5 reduce-scatter.35
  1520.2 87.4 reduce-scatter.53
  1611.2 87.8 reduce-scatter.51
  1708.0 179.3 all-reduce.5
  1891.7 1177.5 reduce-scatter.55
where the time goes:
time: 3100 us; the launch traced here: 3090 us
  waiting for transfers between devices  1970 us (64%)
  matrix products  568 us (18%)
  local copies, waits for them, and re-layouts  318 us (10%)
  other arithmetic  158 us (5%)
  blocking collectives  49.2 us (2%)
    unnamed x27, waiting for transfers between devices  1170 us
    dot_general x46, matrix products, accurate_mode(): return jnp.einsum(equation, former, latter, precision=HIGH_ACCURACY)  376 us
    reduce_scatter x4, waiting for transfers between devices, collect_group(): return lax.psum_scatter(field, 'rows', scatter_dimension=0, tiled=True)  177 us
    psum x1, waiting for transfers between devices, local(): lax.psum((grad_select, grad_style_proj, grad_rgb_style, grad_conv_bias, g...  173 us
    dot_general x59, matrix products, contract(): jnp.einsum(equation, former, latter, preferred_element_type=FLOAT_KIND)  151 us
    unnamed x382, local copies, waits for them, and re-layouts  143 us
    scatter-add x7, local copies, waits for them, and re-layouts, local(): spread = spread.at[:, tap_index // 3:tap_index // 3 + rows_here, tap_inde...  131 us
    reduce_scatter x1, waiting for transfers between devices, local(): lax.psum_scatter(grad_down, 'dp', scatter_dimension=1, tiled=True)  90 us
  transfers between devices with their start and end apart: 28, of which 19 were waited for; matrix products, arithmetic and copies ran while one was open for 21% of the time, Pallas kernels for 0%

commit v1 on v0

v1 whole, which is shorter than its diff:
```python
import functools
import math

import jax
import jax.numpy as jnp
from jax import lax
from jax.experimental import pallas as pl
from jax.experimental.pallas import tpu as pltpu
from jax.sharding import PartitionSpec as P

HD = 64
SUB = 32
BF = jnp.bfloat16
F = jnp.float32
VMEM_LIMIT = 56 * 2**20
EPS = 1e-6


def dot_nn(a, b):
    return lax.dot_general(a, b, (((1,), (0,)), ((), ())), preferred_element_type=F)


def dot_nt(a, b):
    return lax.dot_general(a, b, (((1,), (1,)), ((), ())), preferred_element_type=F)


def dot_tn(a, b):
    return lax.dot_general(a, b, (((0,), (0,)), ((), ())), preferred_element_type=F)


def params():
    return pltpu.CompilerParams(vmem_limit_bytes=VMEM_LIMIT)


def swap(x, axis, delta):
    n = lax.axis_size(axis)
    return lax.ppermute(x, axis, [(i, i ^ delta) for i in range(n)])


def spread(x):
    n = lax.axis_size("rows")
    blocks = [None] * n
    blocks[0] = x
    for j in range(2, n, 2):
        blocks[j] = swap(x, "rows", j)
    for j in range(0, n, 2):
        blocks[j + 1] = swap(blocks[j], "rows", 1)
    return blocks


def collect(blocks):
    n = len(blocks)
    total = None
    for j in list(range(2, n, 2)) + [0]:
        near = blocks[j].astype(F) + swap(blocks[j + 1].astype(BF), "rows", 1).astype(F)
        part = near if j == 0 else swap(near.astype(BF), "rows", j).astype(F)
        total = part if total is None else total + part
    return total


def double(x, axis, place):
    delta = 1
    while delta < lax.axis_size(axis):
        other = swap(x, axis, delta)
        high = (place & delta) != 0
        x = jnp.where(high, jnp.concatenate([other, x]), jnp.concatenate([x, other]))
        delta *= 2
    return x


def merge(sums, gathered, axis, place):
    rows = sums.shape[0]
    delta = 1
    while delta < lax.axis_size(axis):
        other = swap(jnp.concatenate([sums, gathered]), axis, delta)
        sums = sums + other[:rows]
        high = (place & delta) != 0
        theirs = other[rows:]
        gathered = jnp.where(
            high, jnp.concatenate([theirs, gathered]), jnp.concatenate([gathered, theirs])
        )
        delta *= 2
    return sums, gathered


def add_over(sums, axis):
    delta = 1
    while delta < lax.axis_size(axis):
        sums = sums + swap(sums, axis, delta)
        delta *= 2
    return sums


def ring_perm(n, step, flip):
    lines = n // 2
    return [(i, ((i // 2 + step) % lines) * 2 + ((i % 2) ^ flip)) for i in range(n)]


def ring_gather(x):
    n = lax.axis_size("dp")
    out = []
    held = x
    for step in range(n // 2):
        if step:
            held = lax.ppermute(held, "dp", ring_perm(n, 1, 0))
        out.append(held)
        out.append(lax.ppermute(held, "dp", ring_perm(n, 0, 1)))
    return out


def ring_source(n, place, slot):
    lines = n // 2
    return ((place // 2 - slot // 2) % lines) * 2 + ((place % 2) ^ (slot % 2))


def ring_target(n, place, slot):
    lines = n // 2
    return ((place // 2 + slot // 2) % lines) * 2 + ((place % 2) ^ (slot % 2))


def move_up(v, axis):
    shape = list(v.shape)
    shape[axis] = 1
    kept = lax.slice_in_dim(v, 0, v.shape[axis] - 1, axis=axis)
    return jnp.concatenate([jnp.zeros(shape, v.dtype), kept], axis=axis)


def move_down(v, axis):
    shape = list(v.shape)
    shape[axis] = 1
    kept = lax.slice_in_dim(v, 1, v.shape[axis], axis=axis)
    return jnp.concatenate([kept, jnp.zeros(shape, v.dtype)], axis=axis)


def band_mask(kernels):
    width = SUB * kernels
    row = lax.broadcasted_iota(jnp.int32, (SUB, width), 0)
    lane = lax.broadcasted_iota(jnp.int32, (SUB, width), 1)
    return (lane // kernels) == row


def conv_forward(xs, mix_row, scaled_mix, widen, bank, groups, side):
    rows, channels = xs.shape
    kernels, width = bank.shape[3], bank.shape[4]
    block = widen.shape[0]
    steps = channels // block
    parts = block // SUB
    span = SUB * kernels
    low = rows // groups

    def body(x_ref, m_ref, s_ref, w_ref, b_ref, out_ref, raw_ref, dem_ref, acc, en):
        step = pl.program_id(0)

        @pl.when(step == 0)
        def _():
            acc[...] = jnp.zeros_like(acc)
            en[...] = jnp.zeros_like(en)

        wide = dot_nn(x_ref[...], w_ref[...]).reshape(groups, low, block * kernels)
        a = (wide * m_ref[...]).astype(BF).reshape(rows, block * kernels)
        mask = band_mask(kernels)[None]
        left = []
        for u in range(parts):
            d = jnp.where(mask, s_ref[:, :, u * span : (u + 1) * span], 0.0).astype(BF)
            left.append(
                jnp.concatenate([a[:, u * span : (u + 1) * span], d.reshape(groups * SUB, span)])
            )
        energy = en[...]
        for t in range(9):
            b = b_ref[t // 3, t % 3].reshape(block * kernels, width)
            total = acc[t]
            for u in range(parts):
                p = dot_nn(left[u], b[u * span : (u + 1) * span])
                total = total + p[:rows]
                m = p[rows:]
                energy = energy + jnp.sum((m * m).reshape(groups, SUB // 8, 8, width), axis=1)
            acc[t] = total
        en[...] = energy

        @pl.when(step == steps - 1)
        def _():
            demod = lax.rsqrt(jnp.sum(en[...], axis=1, keepdims=True) + 1e-8)
            dem_ref[...] = demod
            for s in range(groups):
                v = [acc[t, s * low : (s + 1) * low].reshape(side, side, width) for t in range(9)]
                for py in range(2):
                    h = []
                    for tx in range(3):
                        if py == 0:
                            h.append(move_up(v[tx], 0) + v[3 + tx] + v[6 + tx])
                        else:
                            h.append(v[tx] + v[3 + tx] + move_down(v[6 + tx], 0))
                    for px in range(2):
                        if px == 0:
                            o = move_up(h[0], 1) + h[1] + h[2]
                        else:
                            o = h[0] + h[1] + move_down(h[2], 1)
                        o = o.reshape(low, width)
                        q = (py * 2 + px) * low
                        raw_ref[s, q : q + low] = o.astype(raw_ref.dtype)
                        out_ref[s, q : q + low] = (o * demod[s]).astype(BF)

    return pl.pallas_call(
        body,
        grid=(steps,),
        in_specs=[
            pl.BlockSpec((rows, block), lambda i: (0, i)),
            pl.BlockSpec((groups, 1, block * kernels), lambda i: (0, 0, 0)),
            pl.BlockSpec((groups, 1, block * kernels), lambda i: (0, 0, i)),
            pl.BlockSpec((block, block * kernels), lambda i: (0, 0)),
            pl.BlockSpec((3, 3, block, kernels, width), lambda i: (0, 0, i, 0, 0)),
        ],
        out_specs=[
            pl.BlockSpec((groups, 4 * low, width), lambda i: (0, 0, 0)),
            pl.BlockSpec((groups, 4 * low, width), lambda i: (0, 0, 0)),
            pl.BlockSpec((groups, 1, width), lambda i: (0, 0, 0)),
        ],
        out_shape=[
            jax.ShapeDtypeStruct((groups, 4 * low, width), BF),
            jax.ShapeDtypeStruct((groups, 4 * low, width), BF),
            jax.ShapeDtypeStruct((groups, 1, width), F),
        ],
        scratch_shapes=[pltpu.VMEM((9, rows, width), F), pltpu.VMEM((groups, 8, width), F)],
        compiler_params=params(),
        cost_estimate=pl.CostEstimate(
            flops=27 * rows * channels * kernels * width,
            bytes_accessed=18 * channels * kernels * width,
            transcendentals=0,
        ),
        name="conv_forward",
    )(xs, mix_row, scaled_mix, widen, bank)


def conv_back(gs, xs, mix_row, widen, bank, groups):
    _, rows, width = gs.shape
    channels, kernels = xs.shape[1], bank.shape[3]
    block = widen.shape[0]
    steps = channels // block
    low = rows // groups

    def body(g_ref, x_ref, m_ref, w_ref, b_ref, low_ref, mix_ref, acc):
        step = pl.program_id(0)

        @pl.when(step == 0)
        def _():
            acc[...] = jnp.zeros_like(acc)

        total = None
        for t in range(9):
            p = dot_nt(g_ref[t], b_ref[t // 3, t % 3].reshape(block * kernels, width))
            total = p if total is None else total + p
        wide = dot_nn(x_ref[...], w_ref[...])
        acc[...] += jnp.sum((wide * total).reshape(groups, low // 8, 8, block * kernels), axis=1)
        mixed = total.reshape(groups, low, block * kernels) * m_ref[...]
        low_ref[...] = dot_nt(mixed.astype(BF).reshape(rows, block * kernels), w_ref[...]).astype(BF)

        @pl.when(step == steps - 1)
        def _():
            mix_ref[...] = jnp.sum(acc[...], axis=1, keepdims=True)

    return pl.pallas_call(
        body,
        grid=(steps,),
        in_specs=[
            pl.BlockSpec((9, rows, width), lambda i: (0, 0, 0)),
            pl.BlockSpec((rows, block), lambda i: (0, i)),
            pl.BlockSpec((groups, 1, block * kernels), lambda i: (0, 0, 0)),
            pl.BlockSpec((block, block * kernels), lambda i: (0, 0)),
            pl.BlockSpec((3, 3, block, kernels, width), lambda i: (0, 0, i, 0, 0)),
        ],
        out_specs=[
            pl.BlockSpec((rows, block), lambda i: (0, i)),
            pl.BlockSpec((groups, 1, block * kernels), lambda i: (0, 0, 0)),
        ],
        out_shape=[
            jax.ShapeDtypeStruct((rows, channels), BF),
            jax.ShapeDtypeStruct((groups, 1, block * kernels), F),
        ],
        scratch_shapes=[pltpu.VMEM((groups, 8, block * kernels), F)],
        compiler_params=params(),
        cost_estimate=pl.CostEstimate(
            flops=18 * rows * channels * kernels * width,
            bytes_accessed=18 * channels * kernels * width,
            transcendentals=0,
        ),
        name="conv_back",
    )(gs, xs, mix_row, widen, bank)


def bank_energy(scaled_mix, ge, bank, first, bands):
    samples = scaled_mix.shape[0]
    kernels, width = bank.shape[3], bank.shape[4]
    span = SUB * kernels
    chunk = min(samples, 32)
    chunks = samples // chunk
    kind = BF if chunks == 1 else F

    def body(first_ref, s_ref, g_ref, b_ref, e_ref, diag_ref):
        part = pl.program_id(1)
        mask = band_mask(kernels)[None]
        d = jnp.where(mask, s_ref[...], 0.0).astype(BF).reshape(chunk * SUB, span)
        d_turned = d.T
        acc = None
        for t in range(9):
            b = b_ref[t // 3, t % 3].reshape(span, width)
            m = dot_nn(d, b)
            w = (m.reshape(chunk, SUB, width) * g_ref[...]).reshape(chunk * SUB, width).astype(BF)
            e = dot_nn(d_turned, w).reshape(SUB, kernels, width)
            if chunks == 1:
                e_ref[t // 3, t % 3] = e.astype(kind)
            else:
                e_ref[t // 3, t % 3] = e + jnp.where(part == 0, 0.0, e_ref[t // 3, t % 3])
            p = dot_nt(w, b)
            acc = p if acc is None else acc + p
        kept = jnp.where(mask, acc.reshape(chunk, SUB, span), 0.0)
        diag_ref[...] = jnp.sum(kept, axis=1, keepdims=True)

    return pl.pallas_call(
        body,
        grid_spec=pltpu.PrefetchScalarGridSpec(
            num_scalar_prefetch=1,
            grid=(bands, chunks),
            in_specs=[
                pl.BlockSpec((chunk, 1, span), lambda i, c, s: (c, 0, i)),
                pl.BlockSpec((chunk, 1, width), lambda i, c, s: (c, 0, 0)),
                pl.BlockSpec((3, 3, SUB, kernels, width), lambda i, c, s: (0, 0, s[0] + i, 0, 0)),
            ],
            out_specs=[
                pl.BlockSpec((3, 3, SUB, kernels, width), lambda i, c, s: (0, 0, i, 0, 0)),
                pl.BlockSpec((chunk, 1, span), lambda i, c, s: (c, 0, i)),
            ],
        ),
        out_shape=[
            jax.ShapeDtypeStruct((3, 3, bands * SUB, kernels, width), kind),
            jax.ShapeDtypeStruct((samples, 1, bands * span), F),
        ],
        compiler_params=params(),
        cost_estimate=pl.CostEstimate(
            flops=54 * bands * samples * SUB * span * width,
            bytes_accessed=36 * bands * span * width,
            transcendentals=0,
        ),
        name="bank_energy",
    )(first, scaled_mix, ge, bank)


def bank_main(at, gs, energy):
    _, points, width = gs.shape
    band, kernels = energy.shape[2], energy.shape[3]

    def body(a_ref, g_ref, e_ref, o_ref):
        p = dot_nn(a_ref[...], g_ref[0]).reshape(band, kernels, width)
        o_ref[0, 0] = p + e_ref[0, 0].astype(F)

    return pl.pallas_call(
        body,
        grid=(9,),
        in_specs=[
            pl.BlockSpec((band * kernels, points), lambda t: (0, 0)),
            pl.BlockSpec((1, points, width), lambda t: (t, 0, 0)),
            pl.BlockSpec((1, 1, band, kernels, width), lambda t: (t // 3, t % 3, 0, 0, 0)),
        ],
        out_specs=pl.BlockSpec((1, 1, band, kernels, width), lambda t: (t // 3, t % 3, 0, 0, 0)),
        out_shape=jax.ShapeDtypeStruct((3, 3, band, kernels, width), F),
        compiler_params=params(),
        cost_estimate=pl.CostEstimate(
            flops=18 * band * kernels * points * width,
            bytes_accessed=18 * points * width + 54 * band * kernels * width,
            transcendentals=0,
        ),
        name="bank_main",
    )(at, gs, energy)


def tap_sums(grads, side):
    samples, _, width = grads.shape
    g = grads.astype(F).reshape(samples, 2, 2, side, side, width)
    lines = [g[:, 1] + move_down(g[:, 0], 2), g[:, 0] + g[:, 1], g[:, 0] + move_up(g[:, 1], 2)]
    out = []
    for v in lines:
        out.append(v[:, 1] + move_down(v[:, 0], 2))
        out.append(v[:, 0] + v[:, 1])
        out.append(v[:, 0] + move_up(v[:, 1], 2))
    return jnp.stack(out).astype(BF).reshape(9, samples * side * side, width)


def rms(field, gain):
    inverse = lax.rsqrt(jnp.mean(field * field, axis=-1, keepdims=True) + EPS)
    return field * inverse * gain, inverse


def rms_back(field, gain, grad_out):
    inverse = lax.rsqrt(jnp.mean(field * field, axis=-1, keepdims=True) + EPS)
    scaled = grad_out * gain
    grad_gain = jnp.sum(grad_out * field * inverse, axis=0, keepdims=True)
    mean = jnp.mean(scaled * field, axis=-1, keepdims=True)
    return inverse * scaled - field * inverse**3 * mean, grad_gain


def sigmoid(v):
    return 1.0 / (1.0 + jnp.exp(-v))


def silu_slope(v):
    q = sigmoid(v)
    return q * (1.0 + v * (1.0 - q))


def self_prob(q, k):
    kf = k.astype(F)
    square = jnp.sum(kf * kf, axis=1, keepdims=True)
    scores = (2.0 * dot_nt(k, q) - square) * (1.0 / math.sqrt(HD))
    e = jnp.exp(scores - jnp.max(scores, axis=0, keepdims=True))
    return e * (1.0 / jnp.sum(e, axis=0, keepdims=True))


def cross_prob(q, k):
    scores = dot_nt(k, q) * (1.0 / math.sqrt(HD))
    e = jnp.exp(scores - jnp.max(scores, axis=0, keepdims=True))
    return e * (1.0 / jnp.sum(e, axis=0, keepdims=True))


def middle_forward(conv, noise, noise_gain, bias, g_attn, g_cross, g_mlp, wqkv, wo, cq, co, ckv):
    points, channels = conv.shape
    n = len(wqkv)
    share = cq[0].shape[1]
    tokens = ckv[0].shape[0]

    def body(conv_ref, noise_ref, ng_ref, cb_ref, ga_ref, gc_ref, gm_ref, *rest):
        wqkv_r, wo_r, cq_r, co_r, ckv_r = (rest[i * n : (i + 1) * n] for i in range(5))
        two_ref, three_ref, mlp_ref, qkv_ref, att_ref, xq_ref, xatt_ref = rest[5 * n :]
        out = conv_ref[...].astype(F) + ng_ref[...] * noise_ref[...] + cb_ref[...]
        one = out * sigmoid(out)
        normed = rms(one, ga_ref[...])[0].astype(BF)
        two = one
        for j in range(n):
            qkv = dot_nn(normed, wqkv_r[j][...]).astype(BF)
            qkv_ref[j] = qkv
            heads = []
            for h in range(share // HD):
                q, k, v = (qkv[:, i * share + h * HD : i * share + (h + 1) * HD] for i in range(3))
                heads.append(dot_tn(self_prob(q, k).astype(BF), v).astype(BF))
            att_ref[j] = jnp.concatenate(heads, axis=1)
            two = two + dot_nn(att_ref[j], wo_r[j][...])
        two_ref[...] = two
        normed = rms(two, gc_ref[...])[0].astype(BF)
        three = two_ref[...]
        for j in range(n):
            xq = dot_nn(normed, cq_r[j][...]).astype(BF)
            xq_ref[j] = xq
            kv = ckv_r[j][...]
            heads = []
            for h in range(share // HD):
                q = xq[:, h * HD : (h + 1) * HD]
                k = kv[:, h * HD : (h + 1) * HD]
                v = kv[:, share + h * HD : share + (h + 1) * HD]
                heads.append(dot_tn(cross_prob(q, k).astype(BF), v).astype(BF))
            xatt_ref[j] = jnp.concatenate(heads, axis=1)
            three = three + dot_nn(xatt_ref[j], co_r[j][...])
        three_ref[...] = three
        mlp_ref[...] = rms(three, gm_ref[...])[0].astype(BF)

    return pl.pallas_call(
        body,
        out_shape=[
            jax.ShapeDtypeStruct((points, channels), F),
            jax.ShapeDtypeStruct((points, channels), F),
            jax.ShapeDtypeStruct((points, channels), BF),
            jax.ShapeDtypeStruct((n, points, 3 * share), BF),
            jax.ShapeDtypeStruct((n, points, share), BF),
            jax.ShapeDtypeStruct((n, points, share), BF),
            jax.ShapeDtypeStruct((n, points, share), BF),
        ],
        compiler_params=params(),
        cost_estimate=pl.CostEstimate(
            flops=14 * points * channels * channels,
            bytes_accessed=24 * channels * channels,
            transcendentals=points * points * channels // HD,
        ),
        name="middle_forward",
    )(conv, noise, noise_gain, bias, g_attn, g_cross, g_mlp, *wqkv, *wo, *cq, *co, *ckv)


def cross_backward(grad_norm, grad_four, three, two, g_mlp, g_cross, xq, xatt, cq, co, ckv):
    points, channels = three.shape
    n, _, share = xq.shape
    tokens = ckv[0].shape[0]

    def body(gn_ref, g4_ref, three_ref, two_ref, gm_ref, gc_ref, xq_ref, xatt_ref, *rest):
        cq_r, co_r, ckv_r = (rest[i * n : (i + 1) * n] for i in range(3))
        two_out, gmlp_out, gcross_out, dcq_ref, dco_ref, dkv_ref, held = rest[3 * n :]
        back, gain = rms_back(three_ref[...], gm_ref[...], gn_ref[...])
        gmlp_out[...] = gain
        grad_three = g4_ref[...] + back
        gb = grad_three.astype(BF)
        normed = rms(two_ref[...], gc_ref[...])[0].astype(BF)
        grad_norm2 = jnp.zeros((points, channels), F)
        for j in range(n):
            ga = dot_nt(gb, co_r[j][...]).astype(BF)
            dco_ref[j] = dot_tn(gb, xatt_ref[j]).astype(BF)
            kv = ckv_r[j][...]
            gq, gk, gv = [], [], []
            for h in range(share // HD):
                q = xq_ref[j, :, h * HD : (h + 1) * HD]
                k = kv[:, h * HD : (h + 1) * HD]
                v = kv[:, share + h * HD : share + (h + 1) * HD]
                g = ga[:, h * HD : (h + 1) * HD]
                p = cross_prob(q, k)
                gp = dot_nt(v, g)
                gs = p * (gp - jnp.sum(p * gp, axis=0, keepdims=True))
                raw = (gs * (1.0 / math.sqrt(HD))).astype(BF)
                gq.append(dot_tn(raw, k).astype(BF))
                gk.append(dot_nn(raw, q).astype(BF))
                gv.append(dot_nn(p.astype(BF), g).astype(BF))
            held[j] = jnp.concatenate(gq, axis=1)
            dkv_ref[j] = jnp.concatenate(gk + gv, axis=1)
            dcq_ref[j] = dot_tn(normed, held[j]).astype(BF)
            grad_norm2 = grad_norm2 + dot_nt(held[j], cq_r[j][...])
        back, gain = rms_back(two_ref[...], gc_ref[...], grad_norm2)
        gcross_out[...] = gain
        two_out[...] = grad_three + back

    return pl.pallas_call(
        body,
        out_shape=[
            jax.ShapeDtypeStruct((points, channels), F),
            jax.ShapeDtypeStruct((1, channels), F),
            jax.ShapeDtypeStruct((1, channels), F),
            jax.ShapeDtypeStruct((n, channels, share), BF),
            jax.ShapeDtypeStruct((n, channels, share), BF),
            jax.ShapeDtypeStruct((n, tokens, 2 * share), BF),
        ],
        scratch_shapes=[pltpu.VMEM((n, points, share), BF)],
        compiler_params=params(),
        cost_estimate=pl.CostEstimate(
            flops=8 * points * channels * channels,
            bytes_accessed=12 * channels * channels,
            transcendentals=points * channels,
        ),
        name="cross_backward",
    )(grad_norm, grad_four, three, two, g_mlp, g_cross, xq, xatt, *cq, *co, *ckv)


def attn_backward(grad_two, conv, noise, noise_gain, bias, g_attn, qkv, att, wqkv, wo):
    points, channels = grad_two.shape
    n, _, share = att.shape

    def body(g2_ref, conv_ref, noise_ref, ng_ref, cb_ref, ga_ref, qkv_ref, att_ref, *rest):
        wqkv_r, wo_r = rest[:n], rest[n : 2 * n]
        gc_ref, sums_ref, dqkv_ref, dwo_ref, held = rest[2 * n :]
        grad_two = g2_ref[...]
        gb = grad_two.astype(BF)
        out = conv_ref[...].astype(F) + ng_ref[...] * noise_ref[...] + cb_ref[...]
        one = out * sigmoid(out)
        normed = rms(one, ga_ref[...])[0].astype(BF)
        grad_norm = jnp.zeros((points, channels), F)
        for j in range(n):
            ga = dot_nt(gb, wo_r[j][...]).astype(BF)
            dwo_ref[j] = dot_tn(gb, att_ref[j]).astype(BF)
            gq, gk, gv = [], [], []
            for h in range(share // HD):
                q, k, v = (
                    qkv_ref[j, :, i * share + h * HD : i * share + (h + 1) * HD] for i in range(3)
                )
                g = ga[:, h * HD : (h + 1) * HD]
                p = self_prob(q, k)
                gp = dot_nt(v, g)
                gs = p * (gp - jnp.sum(p * gp, axis=0, keepdims=True))
                square = jnp.sum(gs, axis=1, keepdims=True) * (-1.0 / math.sqrt(HD))
                raw = (gs * (2.0 / math.sqrt(HD))).astype(BF)
                gq.append(dot_tn(raw, k).astype(BF))
                gk.append((dot_nn(raw, q) + 2.0 * k.astype(F) * square).astype(BF))
                gv.append(dot_nn(p.astype(BF), g).astype(BF))
            held[j] = jnp.concatenate(gq + gk + gv, axis=1)
            dqkv_ref[j] = dot_tn(normed, held[j]).astype(BF)
            grad_norm = grad_norm + dot_nt(held[j], wqkv_r[j][...])
        back, gain = rms_back(one, ga_ref[...], grad_norm)
        grad_conv = (grad_two + back) * silu_slope(out)
        gc_ref[...] = grad_conv.astype(BF)
        sums_ref[0:1] = gain
        sums_ref[1:2] = jnp.sum(grad_conv, axis=0, keepdims=True)
        sums_ref[2:3] = jnp.sum(grad_conv * noise_ref[...], axis=0, keepdims=True)

    return pl.pallas_call(
        body,
        out_shape=[
            jax.ShapeDtypeStruct((points, channels), BF),
            jax.ShapeDtypeStruct((3, channels), F),
            jax.ShapeDtypeStruct((n, channels, 3 * share), BF),
            jax.ShapeDtypeStruct((n, channels, share), BF),
        ],
        scratch_shapes=[pltpu.VMEM((n, points, 3 * share), BF)],
        compiler_params=params(),
        cost_estimate=pl.CostEstimate(
            flops=24 * points * channels * channels,
            bytes_accessed=24 * channels * channels,
            transcendentals=points * points * channels // HD,
        ),
        name="attn_backward",
    )(grad_two, conv, noise, noise_gain, bias, g_attn, qkv, att, *wqkv, *wo)


def local(
    images,
    styles,
    labels,
    noise_map,
    counts,
    cot_features,
    cot_image,
    kernel_bank,
    select_proj,
    style_proj,
    conv_bias,
    noise_gain,
    norm_attn,
    query_proj,
    key_proj,
    value_proj,
    out_proj,
    norm_cross,
    cross_query,
    cross_key,
    cross_value,
    cross_out,
    class_table,
    class_pos,
    norm_mlp,
    up_proj,
    down_proj,
    rgb_style,
    color_projection,
    color_bias,
):
    n, n_dp = lax.axis_size("rows"), lax.axis_size("dp")
    r, d = lax.axis_index("rows"), lax.axis_index("dp")
    side, channels = images.shape[1], images.shape[3]
    low = side * side
    points = 4 * low
    kernels, width = kernel_bank.shape[3], kernel_bank.shape[4]
    tokens = class_pos.shape[0]
    share = query_proj.shape[1]
    band = channels // n_dp
    samples = n * n_dp

    def by_phase(field):
        rest = field.shape[2:]
        split = field.reshape((side, 2, side, 2) + rest)
        order = (1, 3, 0, 2) + tuple(range(4, 4 + len(rest)))
        return split.transpose(order).reshape((points,) + rest)

    group_order = jnp.arange(n, dtype=jnp.int32) ^ r
    slots = jnp.arange(n_dp, dtype=jnp.int32)
    ring_order = ring_source(n_dp, d, slots)
    ring_back = ((d // 2 - slots // 2) % (n_dp // 2)) * 2 + ((d % 2) ^ (slots % 2))

    def row(v):
        return v.astype(F).reshape(1, -1)

    def style_values(codes):
        mixing = jax.nn.softmax(
            jnp.dot(codes, select_proj, preferred_element_type=F), axis=-1
        )
        scale = jnp.dot(codes, style_proj, preferred_element_type=F) + 1.0
        return mixing, scale

    def scaled_rows(mixing, scale):
        return (scale[:, :, None] * mixing[:, None, :]).reshape(scale.shape[0], 1, -1)

    codes = jnp.take(styles, group_order, axis=0)
    mixing, scale_in = style_values(codes)
    own_scale = scale_in[0]
    own_images = images[0].reshape(low, channels)
    modulated = (own_images.astype(F) * own_scale).astype(BF)
    xs = jnp.concatenate(spread(modulated))
    block = min(channels, 128)
    widen = (
        jnp.arange(block * kernels, dtype=jnp.int32)[None, :] // kernels
        == jnp.arange(block, dtype=jnp.int32)[:, None]
    ).astype(BF)
    mix_row = jnp.tile(mixing, (1, block))[:, None, :]
    conv_part, conv_raw, demod = conv_forward(
        xs, mix_row, scaled_rows(mixing, scale_in), widen, kernel_bank, n, side
    )

    wqkv = spread(jnp.concatenate([query_proj, key_proj, value_proj], axis=1))
    wo = spread(out_proj)
    cq = spread(cross_query)
    co = spread(cross_out)

    class_rows = jnp.take(class_table, jnp.take(labels, group_order), axis=0)
    context = (class_rows.astype(F)[:, None, :] + class_pos.astype(F)[None]).astype(BF)
    flat_context = context.reshape(n * tokens, channels)
    ckv = jnp.dot(
        flat_context,
        jnp.concatenate([cross_key, cross_value], axis=1),
        preferred_element_type=F,
    ).astype(BF)
    ckv = ckv.reshape(n, tokens, 2 * share)
    ckv = [ckv[0]] + [swap(ckv[j], "rows", j) for j in range(1, n)]

    live = counts.astype(F)
    total = add_over(jnp.broadcast_to(jnp.sum(live), (8, 128)), "dp")[0, 0]
    own_live = lax.dynamic_index_in_dim(live, r, 0, keepdims=False) / total
    color_scale = (
        jnp.dot(codes[:1], rgb_style, preferred_element_type=F) + 1.0
    )
    grad_image = by_phase(cot_image[0].transpose(1, 2, 0)) * own_live
    colors = color_projection.astype(F)
    tinted = jnp.dot(grad_image, colors.T, precision=lax.Precision.HIGHEST)
    grad_four = by_phase(cot_features[0]).astype(F) * own_live + tinted * color_scale
    grad_four_group = spread(grad_four.astype(BF))

    parts = [conv_part[0]] + [swap(conv_part[j], "rows", j) for j in range(1, n)]
    parts = jnp.stack(parts)
    conv = jnp.concatenate(
        [lax.dynamic_index_in_dim(parts, r ^ j, 0, keepdims=False) for j in range(n)], axis=1
    )
    noise = by_phase(noise_map[0]).astype(F).reshape(points, 1)
    rows_of = (row(noise_gain), row(conv_bias), row(norm_attn))
    two, three, normed_mlp, qkv, att, xq, xatt = middle_forward(
        conv, noise, *rows_of, row(norm_cross), row(norm_mlp), wqkv, wo, cq, co, ckv
    )

    mlp_in = spread(normed_mlp)
    forward, backward, acts, inners = [], [], [], []
    for j in range(n):
        inner = jnp.dot(mlp_in[j], up_proj, preferred_element_type=F)
        gate = sigmoid(inner)
        act = (inner * gate).astype(BF)
        grad_act = lax.dot_general(
            grad_four_group[j], down_proj, (((1,), (1,)), ((), ())), preferred_element_type=F
        )
        grad_inner = (grad_act * (gate * (1.0 + inner * (1.0 - gate)))).astype(BF)
        backward.append(dot_nt(grad_inner, up_proj).astype(BF))
        forward.append(jnp.dot(act, down_proj, preferred_element_type=F).astype(BF))
        acts.append(act)
        inners.append(grad_inner)
    grad_norm = collect(backward)
    four = three + collect(forward)
    d_up = sum(dot_tn(mlp_in[j], inners[j]) for j in range(n))
    d_down = sum(dot_tn(grad_four_group[j], acts[j]) for j in range(n))

    features = four.reshape(2, 2, side, side, channels).transpose(2, 0, 3, 1, 4)
    features = features.reshape(1, 2 * side, 2 * side, channels)
    tint = color_scale.T * colors
    color_image = jnp.dot(four, tint, precision=lax.Precision.HIGHEST) + color_bias.astype(F)
    color_image = color_image.reshape(2, 2, side, side, 3).transpose(4, 2, 0, 3, 1)
    color_image = color_image.reshape(1, 3, 2 * side, 2 * side)
    four_image = lax.dot_general(
        four, grad_image, (((0,), (0,)), ((), ())), precision=lax.Precision.HIGHEST
    )
    grad_colors = four_image * color_scale.T
    grad_scale_rgb = jnp.sum(four_image * colors, axis=1)
    grad_color_bias = jnp.sum(grad_image, axis=0)

    grad_two, d_norm_mlp, d_norm_cross, dcq, dco, dkv = cross_backward(
        grad_norm, grad_four, three, two, row(norm_mlp), row(norm_cross), xq, xatt, cq, co, ckv
    )
    grad_conv, late_sums, dqkv, dwo = attn_backward(
        grad_two, conv, noise, *rows_of, qkv, att, wqkv, wo
    )

    dkv = [dkv[0]] + [swap(dkv[j], "rows", j) for j in range(1, n)]
    dkv = jnp.concatenate(dkv)
    d_ck_cv = dot_tn(flat_context, dkv).astype(BF)
    grad_context = dot_nt(dkv[:, :share], cross_key) + dot_nt(dkv[:, share:], cross_value)
    grad_context = grad_context.reshape(n, tokens, channels)
    token_sum = jnp.take(jnp.sum(grad_context, axis=1), group_order, axis=0)

    rgb_rows = jnp.where((jnp.arange(n) == r)[:, None], grad_scale_rgb[None], 0.0)
    bias_row = jnp.pad(grad_color_bias, (0, channels - 3))[None]
    early = jnp.concatenate(
        [jnp.sum(grad_context, axis=0), d_norm_mlp, d_norm_cross, grad_colors.T, bias_row]
    )
    held = add_over(jnp.concatenate([early, token_sum, rgb_rows]), "rows")
    count = early.shape[0]
    early, per_sample = merge(held[:count], held[count:], "dp", d)
    per_sample = per_sample.reshape(n_dp, 2, n, channels)
    token_all = per_sample[:, 0].reshape(samples, channels)
    rgb_all = per_sample[:, 1].reshape(samples, channels)
    styles_all = double(styles, "dp", d)
    labels_all = double(labels, "dp", d)

    shares = [
        lax.dynamic_slice_in_dim(grad_conv, (r ^ j) * width, width, axis=1) for j in range(n)
    ]
    shares = jnp.stack([shares[0]] + [swap(shares[j], "rows", j) for j in range(1, n)])
    grad_part = shares.astype(F)
    grad_demod = jnp.sum(grad_part * conv_raw.astype(F), axis=1, keepdims=True)
    grad_energy = -0.5 * grad_demod * demod**3
    grad_taps = (grad_part * demod).astype(BF)

    ge_all = jnp.concatenate(ring_gather(grad_energy[:, 0])).reshape(samples, 1, width)
    taps_all = jnp.stack(ring_gather(grad_taps)).reshape(samples, points, width)

    xs_points = xs.reshape(n * low, n_dp, band)
    band_blocks = []
    for slot in range(n_dp):
        target = ring_target(n_dp, d, slot)
        piece = lax.dynamic_slice_in_dim(xs, target * band, band, axis=1)
        if slot:
            piece = lax.ppermute(piece, "dp", ring_perm(n_dp, slot // 2, slot % 2))
        band_blocks.append(piece)
    x_turned = jnp.concatenate(band_blocks).T
    codes_all = jnp.take(styles_all.reshape(n_dp, n, -1), ring_order, axis=0)
    codes_all = jnp.take(codes_all, group_order, axis=1).reshape(samples, -1)
    mixing_all, scale_all = style_values(codes_all)
    scale_band = lax.dynamic_slice_in_dim(scale_all, d * band, band, axis=1)
    first = (d * (band // SUB)).astype(jnp.int32).reshape(1)
    energy, diag = bank_energy(
        scaled_rows(mixing_all, scale_band), 2.0 * ge_all, kernel_bank, first, band // SUB
    )
    diag = diag.reshape(samples, band, kernels)
    scale_energy = jnp.sum(diag * mixing_all[:, None, :], axis=2)
    mixing_energy = jnp.sum(diag * scale_band[:, :, None], axis=1)
    at = x_turned.astype(F)[:, None, :] * jnp.repeat(mixing_all.T, low, axis=1)[None]
    at = at.astype(BF).reshape(band * kernels, samples * low)
    grad_bank = bank_main(at, tap_sums(taps_all, side), energy)

    gs = tap_sums(grad_taps, side)
    low_part, mix_part = conv_back(gs, xs, mix_row, widen, kernel_bank, n)
    low_part = low_part.reshape(n, low, channels)
    grad_low = collect([low_part[j] for j in range(n)])
    grad_images = (grad_low * own_scale).reshape(1, side, side, channels)
    scale_low = jnp.sum(grad_low * own_images.astype(F), axis=0)
    mixing_conv = jnp.sum(mix_part.reshape(n, block, kernels), axis=1)

    def ordered(field):
        rest = field.shape[1:]
        field = jnp.take(field.reshape((n_dp, n) + rest), ring_back, axis=0)
        return jnp.take(field, group_order, axis=1).reshape((samples,) + rest)

    scale_rows = jnp.where((jnp.arange(n) == r)[:, None], scale_low[None], 0.0)
    energy_rows = ordered(scale_energy).reshape(n, channels)
    mixing_rows = jnp.take(mixing_conv, group_order, axis=0).reshape(1, -1)
    mixing_rows = jnp.pad(mixing_rows, ((0, 0), (0, channels - mixing_rows.shape[1])))
    mixing_sum = ordered(mixing_energy).reshape(1, -1)
    mixing_sum = jnp.pad(mixing_sum, ((0, 0), (0, -mixing_sum.shape[1] % channels)))
    mixing_sum = mixing_sum.reshape(-1, channels)
    sums = jnp.concatenate([late_sums, mixing_sum])
    count = sums.shape[0]
    held = add_over(jnp.concatenate([sums, scale_rows, energy_rows, mixing_rows]), "rows")
    sums, per_sample = merge(held[:count], held[count:], "dp", d)
    late_sums, mixing_sum = sums[:3], sums[3:]
    per_sample = per_sample.reshape(n_dp, 2 * n + 1, channels)
    scale_grad = per_sample[:, :n].reshape(samples, channels)
    bands_grad = per_sample[:, n : 2 * n].reshape(n_dp, samples, band).transpose(1, 0, 2)
    scale_grad = scale_grad + bands_grad.reshape(samples, channels)
    mixing_grad = per_sample[:, 2 * n, : n * kernels].reshape(samples, kernels)
    mixing_grad = mixing_grad + mixing_sum.reshape(-1)[: samples * kernels].reshape(samples, kernels)
    mixing_flat = style_values(styles_all)[0]
    grad_logit = mixing_flat * (
        mixing_grad - jnp.sum(mixing_flat * mixing_grad, axis=-1, keepdims=True)
    )

    def style_weight(grad):
        return dot_tn(styles_all, grad.astype(BF))

    def own_group(field):
        return lax.dynamic_slice_in_dim(field, d * n, n, axis=0)

    styles_grad = (
        dot_nt(own_group(grad_logit).astype(BF), select_proj)
        + dot_nt(own_group(scale_grad).astype(BF), style_proj)
        + dot_nt(own_group(rgb_all).astype(BF), rgb_style)
    )
    class_ids = jnp.arange(class_table.shape[0], dtype=jnp.int32)
    one_hot = (labels_all[:, None] == class_ids[None, :]).astype(F)
    d_table = lax.dot_general(
        one_hot, token_all, (((0,), (0,)), ((), ())), precision=lax.Precision.HIGHEST
    )

    def scatter(grads):
        return lax.psum_scatter(grads, "dp", scatter_dimension=0, tiled=True).astype(F)

    g_mlp = scatter(jnp.concatenate([d_up.astype(BF), d_down.astype(BF)], axis=1))
    wide = up_proj.shape[1]
    g_cross = [collect([dcq[j] for j in range(n)]), collect([dco[j] for j in range(n)])]
    g_cross = scatter(jnp.concatenate([g.astype(BF) for g in g_cross] + [d_ck_cv], axis=1))
    g_attn = [collect([dqkv[j] for j in range(n)]), collect([dwo[j] for j in range(n)])]
    g_attn = scatter(jnp.concatenate([g.astype(BF) for g in g_attn], axis=1))

    def column(grads, i):
        return grads[:, i * share : (i + 1) * share]

    return (
        features,
        color_image,
        grad_images,
        styles_grad,
        grad_bank,
        style_weight(grad_logit),
        style_weight(scale_grad),
        late_sums[1],
        late_sums[2],
        late_sums[0],
        column(g_attn, 0),
        column(g_attn, 1),
        column(g_attn, 2),
        column(g_attn, 3).T,
        early[tokens + 1],
        column(g_cross, 0),
        column(g_cross, 2),
        column(g_cross, 3),
        column(g_cross, 1).T,
        d_table,
        early[:tokens],
        early[tokens],
        g_mlp[:, :wide],
        g_mlp[:, wide:].T,
        style_weight(rgb_all),
        early[tokens + 2 : tokens + 5].T,
        early[tokens + 5, :3],
    )


def solution(mesh):
    whole = P()
    columns = P(None, "rows")
    lines = P("rows", None)
    both = P(("dp", "rows"), None, None, None)
    placed = (
        both,
        P("dp", None),
        P("dp"),
        P(("dp", "rows"), None, None),
        P("dp"),
        both,
        both,
        P(None, None, None, None, "rows"),
        whole,
        whole,
        whole,
        whole,
        whole,
        columns,
        columns,
        columns,
        lines,
        whole,
        columns,
        columns,
        columns,
        lines,
        whole,
        whole,
        whole,
        columns,
        lines,
        whole,
        whole,
        whole,
    )
    given = (
        both,
        both,
        both,
        P("dp", None),
        P(None, None, "dp", None, "rows"),
        whole,
        whole,
        whole,
        whole,
        whole,
        P("dp", "rows"),
        P("dp", "rows"),
        P("dp", "rows"),
        P("rows", "dp"),
        whole,
        P("dp", "rows"),
        P("dp", "rows"),
        P("dp", "rows"),
        P("rows", "dp"),
        whole,
        whole,
        whole,
        P("dp", "rows"),
        P("rows", "dp"),
        whole,
        whole,
        whole,
    )
    return jax.shard_map(local, mesh=mesh, in_specs=placed, out_specs=given, check_vma=False)
```

time: 3100 us -> 709 us (0.23)
  waiting for transfers between devices: 1970 us -> 192 us
  matrix products: 568 us -> 51.4 us
  local copies, waits for them, and re-layouts: 318 us -> 138 us
  Pallas kernels: 0 us -> 135 us
  other arithmetic: 158 us -> 87.6 us
  starting transfers between devices: 9.44 us -> 74.9 us
  blocking collectives: 49.2 us -> 0 us
    unnamed x27 -> x5, waiting for transfers between devices: 1170 us -> 0.05 us
    dot_general x119 -> x44, matrix products: 562 us -> 51.4 us  [the longest x12 15.6 us: dot_tn(): lax.dot_general(a, b, (((0,), (0,)), ((), ())), preferred_element_type=F)]
    reduce_scatter x17 -> x1, waiting for transfers between devices: 485 us -> 22.5 us  [scatter(): lax.psum_scatter(grads, 'dp', scatter_dimension=0, tiled=True).astype(F)]
    psum x1 -> x0, waiting for transfers between devices: 173 us -> none  [local(): lax.psum((grad_select, grad_style_proj, grad_rgb_style, grad_conv_bias, g...]
    ppermute x0 -> x94, waiting for transfers between devices: none -> 170 us  [the longest x73 119 us: swap(): return lax.ppermute(x, axis, [(i, i ^ delta) for i in range(n)])]
    pallas_call x0 -> x7, Pallas kernels: none -> 135 us  [the longest x1 22.5 us: attn_backward(): pl.pallas_call(body, out_shape=[jax.ShapeDtypeStruct((points, channels),...]
    scatter-add x7 -> x0, local copies, waits for them, and re-layouts: 131 us -> none  [local(): spread = spread.at[:, tap_index // 3:tap_index // 3 + rows_here, tap_inde...]
    all_gather x7 -> x0, waiting for transfers between devices: 116 us -> none  [the longest x4 86.1 us: spread_group(): return lax.all_gather(field, 'rows', axis=0, tiled=True)]
  transfers between devices with their start and end apart: 28 -> 97, of which waited for: 19 -> 35; matrix products, arithmetic and copies ran while one was open for 21% -> 35% of each run, Pallas kernels for 0% -> 17%
where the time goes in v1:
time: 709 us; the launch traced here: 697 us
  waiting for transfers between devices  192 us (27%)
  local copies, waits for them, and re-layouts  138 us (19%)
  Pallas kernels  135 us (19%)
  other arithmetic  87.6 us (12%)
  starting transfers between devices  74.9 us (11%)
  matrix products  51.4 us (7%)
  between operations  17.7 us (2%)
    ppermute x73, waiting for transfers between devices, swap(): return lax.ppermute(x, axis, [(i, i ^ delta) for i in range(n)])  119 us
    unnamed x283, local copies, waits for them, and re-layouts  63.4 us
    ppermute x73, starting transfers between devices, swap(): return lax.ppermute(x, axis, [(i, i ^ delta) for i in range(n)])  51.4 us
    ppermute x6, waiting for transfers between devices, ring_gather(): held = lax.ppermute(held, 'dp', ring_perm(n, 1, 0))  30.4 us
    pallas_call x1, Pallas kernels, attn_backward(): pl.pallas_call(body, out_shape=[jax.ShapeDtypeStruct((points, channels),...  22.5 us
    reduce_scatter x1, waiting for transfers between devices, scatter(): lax.psum_scatter(grads, 'dp', scatter_dimension=0, tiled=True).astype(F)  22.5 us
    pallas_call x1, Pallas kernels, conv_forward(): pl.pallas_call(body, grid=(steps,), in_specs=[pl.BlockSpec((rows, block),...  22.2 us
    pallas_call x1, Pallas kernels, conv_back(): pl.pallas_call(body, grid=(steps,), in_specs=[pl.BlockSpec((9, rows, widt...  20 us
  transfers between devices with their start and end apart: 97, of which 35 were waited for; matrix products, arithmetic and copies ran while one was open for 35% of the time, Pallas kernels for 17%

profile of v1, /device:TPU:0, one launch (start us, length us, event | category | flops | bytes accessed | tf_op | source)
XLA Modules:
  0.0 697.2 jit_solution(12705837818544303128)
XLA Ops:
  12.0 3.0 collective-permute-start.1
  27.0 3.4 mul.443.s_ref
  51.0 2.6 collective-permute-start.93
  59.9 3.0 collective-permute-start.29
  73.3 2.7 collective-permute-start.44
  88.2 22.2 %conv_forward.1 = (bf16[4,256,256]{2,1,0:T(8,128)(2,1)}, bf16[4,256,256]{2,1,0:T(8,128)(2,1)}, f32[4,1,256]{2,1,0:T(1,128)}) custom-call(bf16[256,1024]{1,0:T(8,128)(2,1)} %copy-done.12, f32[4,1,1024]{2,1,0:T(1,128)} %tile.10.m_ref, f32[4,1,8192]{2,1,0:T(1,128)} %mul.443.s_ref, bf16[128,1024]{1,0:T(8,128)(2,1)} %fusion.31.w_ref, ...), custom_call_target="tpu_custom_call" | custom-call | flops 14495514624 | bytes 37748736 | tf_op jit(solution)/shard_map/conv_forward/pallas_call | solution.py:203
  123.1 2.9 collective-permute-start.71
  140.9 4.1 collective-permute-done.10.rest_6_
  147.0 9.2 %collective-permute-done.13.rest_10_.rest_2_ = bf16[1024,256]{1,0:T(8,128)(2,1)} collective-permute-done((bf16[1024,256]{1,0:T(8,128)(2,1)}, bf16[1024,256]{1,0:T(8,128)(2,1)}, u32[]{:S(2)}, u32[]{:S(2)}) %collective-permute-start.13) | collective-permute-done | bytes 524320 | tf_op jit(solution)/shard_map/ppermute | solution.py:37
  156.6 10.8 %collective-permute-done.16.rest_14_.rest_6_ = bf16[256,1024]{1,0:T(8,128)(2,1)} collective-permute-done((bf16[256,1024]{1,0:T(8,128)(2,1)}, bf16[256,1024]{1,0:T(8,128)(2,1)}, u32[]{:S(2)}, u32[]{:S(2)}) %collective-permute-start.16) | collective-permute-done | bytes 524320 | tf_op jit(solution)/shard_map/ppermute | solution.py:37
  172.0 2.5 copy.206
  175.0 7.1 %collective-permute-done.30 = bf16[256,1024]{1,0:T(8,128)(2,1)} collective-permute-done((bf16[256,1024]{1,0:T(8,128)(2,1)}, bf16[256,1024]{1,0:T(8,128)(2,1)}, u32[]{:S(2)}, u32[]{:S(2)}) %collective-permute-start.30) | collective-permute-done | bytes 524320 | tf_op jit(solution)/shard_map/ppermute | solution.py:37
  182.1 4.0 fusion.a_ref
  189.9 20.0 %middle_forward.1 = (f32[256,1024]{1,0:T(8,128)}, f32[256,1024]{1,0:T(8,128)}, bf16[256,1024]{1,0:T(8,128)(2,1)}, bf16[4,256,768]{2,1,0:T(8,128)(2,1)}, bf16[4,2...) custom-call(bf16[256,1024]{1,0:T(8,128)(2,1)} %pad_maximum_fusion.5.conv_ref, ...), custom_call_target="tpu_custom_call" | custom-call | flops 3758096384 | bytes 25165824 | tf_op jit(solution)/shard_map/middle_forward/pallas_call | solution.py:463
  214.4 10.6 %collective-permute-done.21 = bf16[256,1024]{1,0:T(8,128)(2,1)S(1)} collective-permute-done((bf16[256,1024]{1,0:T(8,128)(2,1)}, bf16[256,1024]{1,0:T(8,128)(2,1)S(1)}, u32[]{:S(2)}, u32[]{:S(2)}) %collective-permute-start.21) | collective-permute-done | bytes 524320 | tf_op jit(solution)/shard_map/ppermute | solution.py:37
  238.3 10.8 %collective-permute-done.33 = bf16[256,1024]{1,0:T(8,128)(2,1)S(1)} collective-permute-done((bf16[256,1024]{1,0:T(8,128)(2,1)S(1)}, bf16[256,1024]{1,0:T(8,128)(2,1)S(1)}, u32[]{:S(2)}, u32[]{:S(2)}) %collective-permute-start.33) | collective-permute-done | bytes 524320 | tf_op jit(solution)/shard_map/ppermute | solution.py:37
  250.3 14.2 %cross_backward.1 = (f32[256,1024]{1,0:T(8,128)}, f32[1,1024]{1,0:T(1,128)}, f32[1,1024]{1,0:T(1,128)}, bf16[4,1024,256]{2,1,0:T(8,128)(2,1)}, bf16[4,1024,256]{...) custom-call(f32[256,1024]{1,0:T(8,128)} %add_add_fusion.gn_ref, f32[256,1024]{1,0:T(8,128)} %get-tuple-element.289.g4_ref, ...), custom_call_target="tpu_custom_call" | custom-call | flops 2147483648 | bytes 12582912 | tf_op jit(solution)/shard_map/cross_backward/pallas_call | solution.py:523
  267.4 2.8 fusion.84
  275.1 10.2 %collective-permute-done.58 = bf16[16,512]{1,0:T(8,128)(2,1)S(1)} collective-permute-done((bf16[16,512]{1,0:T(8,128)(2,1)S(1)}, bf16[16,512]{1,0:T(8,128)(2,1)S(1)}, u32[]{:S(2)}, u32[]{:S(2)}) %collective-permute-start.58) | collective-permute-done | bytes 16416 | tf_op jit(solution)/shard_map/ppermute | solution.py:37
  290.9 7.7 %collective-permute-done.89 = bf16[1024,256]{1,0:T(8,128)(2,1)} collective-permute-done((bf16[1024,256]{1,0:T(8,128)(2,1)}, bf16[1024,256]{1,0:T(8,128)(2,1)}, u32[]{:S(2)}, u32[]{:S(2)}) %collective-permute-start.89) | collective-permute-done | bytes 524320 | tf_op jit(solution)/shard_map/ppermute | solution.py:37
  304.5 2.6 copy.216
  321.8 2.5 pad_maximum_fusion
  324.3 6.6 copy.218
  335.5 22.5 %attn_backward.1 = (bf16[256,1024]{1,0:T(8,128)(2,1)}, f32[3,1024]{1,0:T(4,128)}, bf16[4,1024,768]{2,1,0:T(8,128)(2,1)}, bf16[4,1024,256]{2,1,0:T(8,128)(2,1)}) custom-call(f32[256,1024]{1,0:T(8,128)} %get-tuple-element.57.g2_ref, bf16[256,1024]{1,0:T(8,128)(2,1)} %pad_maximum_fusion.5.conv_ref, f32[256,1]{1,0:T(8,128)} %reshape.1127.noise_ref, ...), custom_call_target="tpu_custom_call" | custom-call | flops 6442450944 | bytes 25165824 | tf_op jit(solution)/shard_map/attn_backward/pallas_call | solution.py:584
  358.0 4.1 slice_bitcast_fusion.7
  384.3 20.0 %conv_back.1 = (bf16[256,1024]{1,0:T(8,128)(2,1)}, f32[4,1,1024]{2,1,0:T(1,128)}) custom-call(bf16[9,256,256]{2,1,0:T(8,128)(2,1)} %copy-done.38, bf16[256,1024]{1,0:T(8,128)(2,1)} %copy-done.12, f32[4,1,1024]{2,1,0:T(1,128)} %tile.10.m_ref, bf16[128,1024]{1,0:T(8,128)(2,1)} %fusion.31.w_ref, bf16[3,3,1024,8,256]{4,3,2,1,0:T(8,128)(2,1)} %b_ref.5), custom_call_target="tpu_custom_call" | custom-call | flops 9663676416 | bytes 37748736 | tf_op jit(solution)/shard_map/conv_back/pallas_call | solution.py:261
  412.4 5.9 collective-permute-done.48
  419.5 2.4 collective-permute-done.49
  422.1 5.4 collective-permute-done.50
  428.7 2.4 collective-permute-done.51
  431.8 18.9 %bank_energy.1 = (bf16[3,3,128,8,256]{4,3,2,1,0:T(8,128)(2,1)}, f32[32,1,1024]{2,1,0:T(1,128)}) custom-call(s32[1]{0:T(128)} %bitcast.58.first_ref, f32[32,1,1024]{2,1,0:T(1,128)} %copy.195.s_ref, f32[32,1,256]{2,1,0:T(1,128)} %broadcast_multiply_fusion.1.g_ref, bf16[3,3,1024,8,256]{4,3,2,1,0:T(8,128)(2,1)} %b_ref.5), custom_call_target="tpu_custom_call" | custom-call | flops 14495514624 | bytes 9437184 | tf_op jit(solution)/shard_map/bank_energy/pallas_call | solution.py:318
  456.6 4.6 collective-permute-done.40
  468.2 2.8 collective-permute-done.53
  481.3 6.1 collective-permute-done.72
  489.4 7.3 %collective-permute-done.73 = bf16[4,256,256]{2,1,0:T(8,128)(2,1)} collective-permute-done((bf16[4,256,256]{2,1,0:T(8,128)(2,1)S(1)}, bf16[4,256,256]{2,1,0:T(8,128)(2,1)}, u32[]{:S(2)}, u32[]{:S(2)}) %collective-permute-start.73) | collective-permute-done | bytes 524320 | tf_op jit(solution)/shard_map/ppermute | solution.py:105
  501.7 6.7 collective-permute-done.56
  519.2 19.4 %collective-permute-done.64 = f32[54,1024]{1,0:T(8,128)S(1)} collective-permute-done((f32[54,1024]{1,0:T(8,128)S(1)}, f32[54,1024]{1,0:T(8,128)S(1)}, u32[]{:S(2)}, u32[]{:S(2)}) %collective-permute-start.64) | collective-permute-done | bytes 221216 | tf_op jit(solution)/shard_map/ppermute | solution.py:37
  539.8 3.9 fusion.34
  550.7 11.9 %collective-permute-done.77 = bf16[4,256,256]{2,1,0:T(8,128)(2,1)S(1)} collective-permute-done((bf16[4,256,256]{2,1,0:T(8,128)(2,1)S(1)}, bf16[4,256,256]{2,1,0:T(8,128)(2,1)S(1)}, u32[]{:S(2)}, u32[]{:S(2)}) %collective-permute-start.77) | collective-permute-done | bytes 524320 | tf_op jit(solution)/shard_map/ppermute | solution.py:105
  563.4 3.4 fusion.3
  570.1 5.4 collective-permute-done.78
  576.4 3.3 fusion.86
  587.2 12.0 %pad_add_fusion = (f32[32,2,8,8,256]{4,3,2,0,1:T(8,128)}, f32[32,2,8,8,256]{4,3,2,0,1:T(8,128)}, f32[32,2,8,8,256]{4,3,2,0,1:T(8,128)}) fusion(f32[32,2,7,8,256]{4,3,2,0,1:T(8,128)} %slice.562, f32[32,1,2,8,8,256]{5,4,3,2,1,0:T(8,128)} %copy-done.8, f32[32,1,2,8,8,256]{5,4,3,2,1,0:T(8,128)} %copy-done.7, f32[32,2,7,8,256]{4,3,2,0,1:T(8,128)} %slice.553), kind=kLoop, calls=%fused_computation.18 | loop fusion | flops 3145728 | bytes 28311552 | tf_op jit(solution)/shard_map/add | solution.py:378
  599.2 4.5 slice_bitcast_fusion.1
  616.3 3.0 fusion.2
  625.6 3.5 add_convert_fusion.5
  637.7 17.2 %bank_main.1 = f32[3,3,128,8,256]{4,3,2,1,0:T(8,128)} custom-call(bf16[1024,2048]{1,0:T(8,128)(2,1)} %fusion.a_ref, bf16[9,2048,256]{2,1,0:T(8,128)(2,1)} %constant_dynamic-update-slice_fusion.28.g_ref, bf16[3,3,128,8,256]{4,3,2,1,0:T(8,128)(2,1)} %get-tuple-element.70.e_ref), custom_call_target="tpu_custom_call" | custom-call | flops 9663676416 | bytes 23592960 | tf_op jit(solution)/shard_map/bank_main/pallas_call | solution.py:355
  664.3 22.5 %reduce-scatter.8.cloned.1.call-done = bf16[128,1024]{1,0:T(8,128)(2,1)} async-done(((bf16[1024,1024]{1,0:T(8,128)(2,1)}), bf16[128,1024]{1,0:T(8,128)(2,1)}) %reduce-scatter.8.cloned.1.call-update) | async-done | bytes 262160 | tf_op jit(solution)/shard_map/reduce_scatter | solution.py:875
  (731 shorter events, 294.8 us)
Async XLA Ops:
  7.2 647.6 %reduce-scatter.10.cloned.1.call-start = ((), (), s32[]{:S(2)}) async-start(), calls=%async_computation.4 | async-start | bytes 2359296
  12.0 69.4 %collective-permute-start.1 = (bf16[64,1024]{1,0:T(8,128)(2,1)}, bf16[64,1024]{1,0:T(8,128)(2,1)}, u32[]{:S(2)}, u32[]{:S(2)}) collective-permute-start(bf16[64,1024]{1,0:T(8,128)(2,1)} %fusion.32), channel_id=1, source_target_pairs={{0,2},{1,3},{2,0},{3,1},{4,6},{5,7},{6,4},{7,5},{8,10},{9,11},{10,... | collective-permute-start | bytes 393224 | tf_op jit(solution)/shard_map/ppermute | solution.py:37
  14.9 68.2 %collective-permute-start = (bf16[64,1024]{1,0:T(8,128)(2,1)}, bf16[64,1024]{1,0:T(8,128)(2,1)}, u32[]{:S(2)}, u32[]{:S(2)}) collective-permute-start(bf16[64,1024]{1,0:T(8,128)(2,1)} %fusion.32), channel_id=1, source_target_pairs={{0,1},{1,0},{2,3},{3,2},{4,5},{5,4},{6,7},{7,6},{8,9},{9,8},{10,11... | collective-permute-start | bytes 393224 | tf_op jit(solution)/shard_map/ppermute | solution.py:37
  14.9 45.0 %collective-permute-start.42 = (bf16[4,512]{1,0:T(4,128)(2,1)}, bf16[4,512]{1,0:T(4,128)(2,1)S(1)}, u32[]{:S(2)}, u32[]{:S(2)}) collective-permute-start(bf16[4,512]{1,0:T(4,128)(2,1)} %param.31), channel_id=1, source_target_pairs={{0,4},{4,0},{8,12},{12,8},{16,20},{20,16},{24,28},{28,24},{1,5},{5... | collective-permute-start | bytes 12296 | tf_op jit(solution)/shard_map/ppermute | solution.py:37
  16.4 26.7 %collective-permute-start.91 = (s32[4]{0:T(128)}, s32[4]{0:T(128)S(1)}, u32[]{:S(2)}, u32[]{:S(2)}) collective-permute-start(s32[4]{0:T(128)} %param.32), channel_id=1, source_target_pairs={{0,4},{4,0},{8,12},{12,8},{16,20},{20,16},{24,28},{28,24},{1,5},{5... | collective-permute-start | bytes 56 | tf_op jit(solution)/shard_map/ppermute | solution.py:37
  23.2 64.5 %collective-permute-start.18 = (bf16[16,512]{1,0:T(8,128)(2,1)}, bf16[16,512]{1,0:T(8,128)(2,1)S(1)}, u32[]{:S(2)}, u32[]{:S(2)}) collective-permute-start(bf16[16,512]{1,0:T(8,128)(2,1)} %get-tuple-element.277), channel_id=1, source_target_pairs={{0,1},{1,0},{2,3},{3,2},{4,5},{5,4},{6,7},{7,6},{8,9},{9,8},{10,11... | collective-permute-start | bytes 49160 | tf_op jit(solution)/shard_map/ppermute | solution.py:37
  59.1 51.3 %collective-permute-start.19 = (bf16[16,512]{1,0:T(8,128)(2,1)}, bf16[16,512]{1,0:T(8,128)(2,1)}, u32[]{:S(2)}, u32[]{:S(2)}) collective-permute-start(bf16[16,512]{1,0:T(8,128)(2,1)} %get-tuple-element.276), channel_id=1, source_target_pairs={{0,2},{1,3},{2,0},{3,1},{4,6},{5,7},{6,4},{7,5},{8,10},{9,11},{10,... | collective-permute-start | bytes 49160 | tf_op jit(solution)/shard_map/ppermute | solution.py:37
  78.3 34.4 %collective-permute-start.20 = (bf16[16,512]{1,0:T(8,128)(2,1)}, bf16[16,512]{1,0:T(8,128)(2,1)}, u32[]{:S(2)}, u32[]{:S(2)}) collective-permute-start(bf16[16,512]{1,0:T(8,128)(2,1)} %get-tuple-element.275), channel_id=1, source_target_pairs={{0,3},{1,2},{2,1},{3,0},{4,7},{5,6},{6,5},{7,4},{8,11},{9,10},{10,... | collective-permute-start | bytes 49160 | tf_op jit(solution)/shard_map/ppermute | solution.py:37
  83.1 62.3 %collective-permute-start.7 = (bf16[1024,768]{1,0:T(8,128)(2,1)}, bf16[1024,768]{1,0:T(8,128)(2,1)}, u32[]{:S(2)}, u32[]{:S(2)}) collective-permute-start(bf16[1024,768]{1,0:T(8,128)(2,1)} %constant_dynamic-update-slice_fusion.rest_0_), channel_id=1, source_target_pairs={{0,2},{1,3},{2,0},{3,1},{4,6},{5,7},{6,4},{7,5},{8,10},{9,11},{10,... | collective-permute-start | bytes 4718600 | tf_op jit(solution)/shard_map/ppermute | solution.py:37
  86.2 28.1 %collective-permute-start.65 = (bf16[256,128]{1,0:T(8,128)(2,1)S(1)}, bf16[256,128]{1,0:T(8,128)(2,1)S(1)}, u32[]{:S(2)}, u32[]{:S(2)}) collective-permute-start(bf16[256,128]{1,0:T(8,128)(2,1)S(1)} %get-tuple-element.230), channel_id=1, source_target_pairs={{0,4},{4,0},{8,12},{12,8},{16,20},{20,16},{24,28},{28,24},{1,5},{5... | collective-permute-start | bytes 196616 | tf_op jit(solution)/shard_map/ppermute | solution.py:803
  87.7 28.9 %collective-permute-start.66 = (bf16[256,128]{1,0:T(8,128)(2,1)S(1)}, bf16[256,128]{1,0:T(8,128)(2,1)S(1)}, u32[]{:S(2)}, u32[]{:S(2)}) collective-permute-start(bf16[256,128]{1,0:T(8,128)(2,1)S(1)} %get-tuple-element.229), channel_id=1, source_target_pairs={{0,8},{4,12},{8,16},{12,20},{16,24},{20,28},{24,0},{28,4},{1,9},{5... | collective-permute-start | bytes 196616 | tf_op jit(solution)/shard_map/ppermute | solution.py:803
  130.0 15.0 %collective-permute-start.10 = (bf16[256,1024]{1,0:T(8,128)(2,1)}, bf16[256,1024]{1,0:T(8,128)(2,1)}, u32[]{:S(2)}, u32[]{:S(2)}) collective-permute-start(bf16[256,1024]{1,0:T(8,128)(2,1)} %rest_4_.5), channel_id=1, source_target_pairs={{0,2},{1,3},{2,0},{3,1},{4,6},{5,7},{6,4},{7,5},{8,10},{9,11},{10,... | collective-permute-start | bytes 1572872 | tf_op jit(solution)/shard_map/ppermute | solution.py:37
  132.8 23.4 %collective-permute-start.13 = (bf16[1024,256]{1,0:T(8,128)(2,1)}, bf16[1024,256]{1,0:T(8,128)(2,1)}, u32[]{:S(2)}, u32[]{:S(2)}) collective-permute-start(bf16[1024,256]{1,0:T(8,128)(2,1)} %rest_0_.1), channel_id=1, source_target_pairs={{0,2},{1,3},{2,0},{3,1},{4,6},{5,7},{6,4},{7,5},{8,10},{9,11},{10,... | collective-permute-start | bytes 1572872 | tf_op jit(solution)/shard_map/ppermute | solution.py:37
  133.5 34.0 %collective-permute-start.12 = (bf16[1024,256]{1,0:T(8,128)(2,1)}, bf16[1024,256]{1,0:T(8,128)(2,1)}, u32[]{:S(2)}, u32[]{:S(2)}) collective-permute-start(bf16[1024,256]{1,0:T(8,128)(2,1)} %rest_0_.1), channel_id=1, source_target_pairs={{0,1},{1,0},{2,3},{3,2},{4,5},{5,4},{6,7},{7,6},{8,9},{9,8},{10,11... | collective-permute-start | bytes 1572872 | tf_op jit(solution)/shard_map/ppermute | solution.py:37
  134.1 33.4 %collective-permute-start.16 = (bf16[256,1024]{1,0:T(8,128)(2,1)}, bf16[256,1024]{1,0:T(8,128)(2,1)}, u32[]{:S(2)}, u32[]{:S(2)}) collective-permute-start(bf16[256,1024]{1,0:T(8,128)(2,1)} %rest_4_.4), channel_id=1, source_target_pairs={{0,2},{1,3},{2,0},{3,1},{4,6},{5,7},{6,4},{7,5},{8,10},{9,11},{10,... | collective-permute-start | bytes 1572872 | tf_op jit(solution)/shard_map/ppermute | solution.py:37
  145.0 43.9 %collective-permute-start.6 = (bf16[1024,768]{1,0:T(8,128)(2,1)}, bf16[1024,768]{1,0:T(8,128)(2,1)}, u32[]{:S(2)}, u32[]{:S(2)}) collective-permute-start(bf16[1024,768]{1,0:T(8,128)(2,1)} %constant_dynamic-update-slice_fusion.rest_0_), channel_id=1, source_target_pairs={{0,1},{1,0},{2,3},{3,2},{4,5},{5,4},{6,7},{7,6},{8,9},{9,8},{10,11... | collective-permute-start | bytes 4718600 | tf_op jit(solution)/shard_map/ppermute | solution.py:37
  145.4 43.5 %collective-permute-start.8 = (bf16[1024,768]{1,0:T(8,128)(2,1)}, bf16[1024,768]{1,0:T(8,128)(2,1)}, u32[]{:S(2)}, u32[]{:S(2)}) collective-permute-start(bf16[1024,768]{1,0:T(8,128)(2,1)} %collective-permute-done.7.rest_2_), channel_id=1, source_target_pairs={{0,1},{1,0},{2,3},{3,2},{4,5},{5,4},{6,7},{7,6},{8,9},{9,8},{10,11... | collective-permute-start | bytes 4718600 | tf_op jit(solution)/shard_map/ppermute | solution.py:37
  156.2 18.3 %collective-permute-start.15 = (bf16[256,1024]{1,0:T(8,128)(2,1)}, bf16[256,1024]{1,0:T(8,128)(2,1)}, u32[]{:S(2)}, u32[]{:S(2)}) collective-permute-start(bf16[256,1024]{1,0:T(8,128)(2,1)} %rest_4_.4), channel_id=1, source_target_pairs={{0,1},{1,0},{2,3},{3,2},{4,5},{5,4},{6,7},{7,6},{8,9},{9,8},{10,11... | collective-permute-start | bytes 1572872 | tf_op jit(solution)/shard_map/ppermute | solution.py:37
  167.6 14.5 %collective-permute-start.30 = (bf16[256,1024]{1,0:T(8,128)(2,1)}, bf16[256,1024]{1,0:T(8,128)(2,1)}, u32[]{:S(2)}, u32[]{:S(2)}) collective-permute-start(bf16[256,1024]{1,0:T(8,128)(2,1)} %get-tuple-element.288), channel_id=1, source_target_pairs={{0,2},{1,3},{2,0},{3,1},{4,6},{5,7},{6,4},{7,5},{8,10},{9,11},{10,... | collective-permute-start | bytes 1572872 | tf_op jit(solution)/shard_map/ppermute | solution.py:37
  174.7 14.1 %collective-permute-start.14 = (bf16[1024,256]{1,0:T(8,128)(2,1)}, bf16[1024,256]{1,0:T(8,128)(2,1)S(1)}, u32[]{:S(2)}, u32[]{:S(2)}) collective-permute-start(bf16[1024,256]{1,0:T(8,128)(2,1)} %collective-permute-done.13.rest_10_.rest_2_), channel_id=1, source_target_pairs={{0,1},{1,0},{2,3},{3,2},{4,5},{5,4},{6,7},{7,6},{8,9},{9,8},{10,11... | collective-permute-start | bytes 1572872 | tf_op jit(solution)/shard_map/ppermute | solution.py:37
  188.2 37.5 %collective-permute-start.34 = (bf16[256,1024]{1,0:T(8,128)(2,1)S(1)}, bf16[256,1024]{1,0:T(8,128)(2,1)S(1)}, u32[]{:S(2)}, u32[]{:S(2)}) collective-permute-start(bf16[256,1024]{1,0:T(8,128)(2,1)S(1)} %copy-done.29), channel_id=1, source_target_pairs={{0,1},{1,0},{2,3},{3,2},{4,5},{5,4},{6,7},{7,6},{8,9},{9,8},{10,11... | collective-permute-start | bytes 1572872 | tf_op jit(solution)/shard_map/ppermute | solution.py:37
  188.8 40.1 %collective-permute-start.31 = (bf16[256,1024]{1,0:T(8,128)(2,1)}, bf16[256,1024]{1,0:T(8,128)(2,1)S(1)}, u32[]{:S(2)}, u32[]{:S(2)}) collective-permute-start(bf16[256,1024]{1,0:T(8,128)(2,1)} %collective-permute-done.30), channel_id=1, source_target_pairs={{0,1},{1,0},{2,3},{3,2},{4,5},{5,4},{6,7},{7,6},{8,9},{9,8},{10,11... | collective-permute-start | bytes 1572872 | tf_op jit(solution)/shard_map/ppermute | solution.py:37
  209.9 15.1 %collective-permute-start.25 = (bf16[256,1024]{1,0:T(8,128)(2,1)}, bf16[256,1024]{1,0:T(8,128)(2,1)S(1)}, u32[]{:S(2)}, u32[]{:S(2)}) collective-permute-start(bf16[256,1024]{1,0:T(8,128)(2,1)} %get-tuple-element.53), channel_id=1, source_target_pairs={{0,1},{1,0},{2,3},{3,2},{4,5},{5,4},{6,7},{7,6},{8,9},{9,8},{10,11... | collective-permute-start | bytes 1572872 | tf_op jit(solution)/shard_map/ppermute | solution.py:37
  210.3 14.7 %collective-permute-start.21 = (bf16[256,1024]{1,0:T(8,128)(2,1)}, bf16[256,1024]{1,0:T(8,128)(2,1)S(1)}, u32[]{:S(2)}, u32[]{:S(2)}) collective-permute-start(bf16[256,1024]{1,0:T(8,128)(2,1)} %get-tuple-element.53), channel_id=1, source_target_pairs={{0,2},{1,3},{2,0},{3,1},{4,6},{5,7},{6,4},{7,5},{8,10},{9,11},{10,... | collective-permute-start | bytes 1572872 | tf_op jit(solution)/shard_map/ppermute | solution.py:37
  234.7 14.4 %collective-permute-start.33 = (bf16[256,1024]{1,0:T(8,128)(2,1)S(1)}, bf16[256,1024]{1,0:T(8,128)(2,1)S(1)}, u32[]{:S(2)}, u32[]{:S(2)}) collective-permute-start(bf16[256,1024]{1,0:T(8,128)(2,1)S(1)} %add_convert_fusion.11), channel_id=1, source_target_pairs={{0,2},{1,3},{2,0},{3,1},{4,6},{5,7},{6,4},{7,5},{8,10},{9,11},{10,... | collective-permute-start | bytes 1572872 | tf_op jit(solution)/shard_map/ppermute | solution.py:37
  270.2 17.5 %collective-permute-start.87 = (bf16[1024,256]{1,0:T(8,128)(2,1)S(1)}, bf16[1024,256]{1,0:T(8,128)(2,1)S(1)}, u32[]{:S(2)}, u32[]{:S(2)}) collective-permute-start(bf16[1024,256]{1,0:T(8,128)(2,1)S(1)} %get-tuple-element.210), channel_id=1, source_target_pairs={{0,1},{1,0},{2,3},{3,2},{4,5},{5,4},{6,7},{7,6},{8,9},{9,8},{10,11... | collective-permute-start | bytes 1572872 | tf_op jit(solution)/shard_map/ppermute | solution.py:37
  270.8 17.0 %collective-permute-start.86 = (bf16[1024,256]{1,0:T(8,128)(2,1)S(1)}, bf16[1024,256]{1,0:T(8,128)(2,1)S(1)}, u32[]{:S(2)}, u32[]{:S(2)}) collective-permute-start(bf16[1024,256]{1,0:T(8,128)(2,1)S(1)} %fusion.23), channel_id=1, source_target_pairs={{0,2},{1,3},{2,0},{3,1},{4,6},{5,7},{6,4},{7,5},{8,10},{9,11},{10,... | collective-permute-start | bytes 1572872 | tf_op jit(solution)/shard_map/ppermute | solution.py:37
  274.7 16.1 %collective-permute-start.90 = (bf16[1024,256]{1,0:T(8,128)(2,1)}, bf16[1024,256]{1,0:T(8,128)(2,1)}, u32[]{:S(2)}, u32[]{:S(2)}) collective-permute-start(bf16[1024,256]{1,0:T(8,128)(2,1)} %get-tuple-element.212), channel_id=1, source_target_pairs={{0,1},{1,0},{2,3},{3,2},{4,5},{5,4},{6,7},{7,6},{8,9},{9,8},{10,11... | collective-permute-start | bytes 1572872 | tf_op jit(solution)/shard_map/ppermute | solution.py:37
  307.1 351.9 %reduce-scatter.12.cloned.1.call-start = ((), (), s32[]{:S(2)}) async-start(), calls=%async_computation.5 | async-start | bytes 4718592
  311.5 53.0 %collective-permute-start.26 = (bf16[256,1024]{1,0:T(8,128)(2,1)}, bf16[256,1024]{1,0:T(8,128)(2,1)}, u32[]{:S(2)}, u32[]{:S(2)}) collective-permute-start(bf16[256,1024]{1,0:T(8,128)(2,1)} %convolution_convert_fusion.5), channel_id=1, source_target_pairs={{0,1},{1,0},{2,3},{3,2},{4,5},{5,4},{6,7},{7,6},{8,9},{9,8},{10,11... | collective-permute-start | bytes 1572872 | tf_op jit(solution)/shard_map/ppermute | solution.py:37
  330.9 355.9 %reduce-scatter.8.cloned.1.call-start = ((), (), s32[]{:S(2)}) async-start(), calls=%async_computation.3 | async-start | bytes 2359296 | tf_op jit(solution)/shard_map/reduce_scatter | solution.py:875
  334.6 31.0 %collective-permute-start.24 = (bf16[256,1024]{1,0:T(8,128)(2,1)S(1)}, bf16[256,1024]{1,0:T(8,128)(2,1)S(1)}, u32[]{:S(2)}, u32[]{:S(2)}) collective-permute-start(bf16[256,1024]{1,0:T(8,128)(2,1)S(1)} %add_convert_fusion.12), channel_id=1, source_target_pairs={{0,2},{1,3},{2,0},{3,1},{4,6},{5,7},{6,4},{7,5},{8,10},{9,11},{10,... | collective-permute-start | bytes 1572872 | tf_op jit(solution)/shard_map/ppermute | solution.py:37
  362.1 201.3 %collective-permute-start.79 = (bf16[1024,768]{1,0:T(8,128)(2,1)}, bf16[1024,768]{1,0:T(8,128)(2,1)}, u32[]{:S(2)}, u32[]{:S(2)}) collective-permute-start(bf16[1024,768]{1,0:T(8,128)(2,1)} %get-tuple-element.187), channel_id=1, source_target_pairs={{0,1},{1,0},{2,3},{3,2},{4,5},{5,4},{6,7},{7,6},{8,9},{9,8},{10,11... | collective-permute-start | bytes 4718600 | tf_op jit(solution)/shard_map/ppermute | solution.py:37
  362.1 254.1 %collective-permute-start.81 = (bf16[1024,768]{1,0:T(8,128)(2,1)}, bf16[1024,768]{1,0:T(8,128)(2,1)}, u32[]{:S(2)}, u32[]{:S(2)}) collective-permute-start(bf16[1024,768]{1,0:T(8,128)(2,1)} %get-tuple-element.188), channel_id=1, source_target_pairs={{0,1},{1,0},{2,3},{3,2},{4,5},{5,4},{6,7},{7,6},{8,9},{9,8},{10,11... | collective-permute-start | bytes 4718600 | tf_op jit(solution)/shard_map/ppermute | solution.py:37
  377.2 99.3 %collective-permute-start.82 = (bf16[1024,256]{1,0:T(8,128)(2,1)}, bf16[1024,256]{1,0:T(8,128)(2,1)}, u32[]{:S(2)}, u32[]{:S(2)}) collective-permute-start(bf16[1024,256]{1,0:T(8,128)(2,1)} %get-tuple-element.213), channel_id=1, source_target_pairs={{0,1},{1,0},{2,3},{3,2},{4,5},{5,4},{6,7},{7,6},{8,9},{9,8},{10,11... | collective-permute-start | bytes 1572872 | tf_op jit(solution)/shard_map/ppermute | solution.py:37
  380.1 27.7 %collective-permute-start.45 = (f32[4,256]{1,0:T(4,128)S(1)}, f32[4,256]{1,0:T(4,128)}, u32[]{:S(2)}, u32[]{:S(2)}) collective-permute-start(f32[4,256]{1,0:T(4,128)S(1)} %bitcast.433), channel_id=1, source_target_pairs={{0,4},{4,0},{8,12},{12,8},{16,20},{20,16},{24,28},{28,24},{1,5},{5... | collective-permute-start | bytes 12296 | tf_op jit(solution)/shard_map/ppermute | solution.py:107
  381.2 27.4 %collective-permute-start.46 = (f32[4,256]{1,0:T(4,128)S(1)}, f32[4,256]{1,0:T(4,128)}, u32[]{:S(2)}, u32[]{:S(2)}) collective-permute-start(f32[4,256]{1,0:T(4,128)S(1)} %bitcast.434), channel_id=1, source_target_pairs={{0,8},{4,12},{8,16},{12,20},{16,24},{20,28},{24,0},{28,4},{1,9},{5... | collective-permute-start | bytes 12296 | tf_op jit(solution)/shard_map/ppermute | solution.py:105
  407.7 47.4 %collective-permute-start.39 = (bf16[64,1024]{1,0:T(8,128)(2,1)S(1)}, bf16[64,1024]{1,0:T(8,128)(2,1)S(1)}, u32[]{:S(2)}, u32[]{:S(2)}) collective-permute-start(bf16[64,1024]{1,0:T(8,128)(2,1)S(1)} %get-tuple-element.234), channel_id=1, source_target_pairs={{0,1},{1,0},{2,3},{3,2},{4,5},{5,4},{6,7},{7,6},{8,9},{9,8},{10,11... | collective-permute-start | bytes 393224 | tf_op jit(solution)/shard_map/ppermute | solution.py:37
  431.1 25.4 %collective-permute-start.41 = (bf16[64,1024]{1,0:T(8,128)(2,1)}, bf16[64,1024]{1,0:T(8,128)(2,1)}, u32[]{:S(2)}, u32[]{:S(2)}) collective-permute-start(bf16[64,1024]{1,0:T(8,128)(2,1)} %get-tuple-element.235), channel_id=1, source_target_pairs={{0,1},{1,0},{2,3},{3,2},{4,5},{5,4},{6,7},{7,6},{8,9},{9,8},{10,11... | collective-permute-start | bytes 393224 | tf_op jit(solution)/shard_map/ppermute | solution.py:37
  480.3 34.7 %collective-permute-start.84 = (bf16[1024,256]{1,0:T(8,128)(2,1)}, bf16[1024,256]{1,0:T(8,128)(2,1)}, u32[]{:S(2)}, u32[]{:S(2)}) collective-permute-start(bf16[1024,256]{1,0:T(8,128)(2,1)} %get-tuple-element.214), channel_id=1, source_target_pairs={{0,1},{1,0},{2,3},{3,2},{4,5},{5,4},{6,7},{7,6},{8,9},{9,8},{10,11... | collective-permute-start | bytes 1572872 | tf_op jit(solution)/shard_map/ppermute | solution.py:37
  481.2 15.4 %collective-permute-start.73 = (bf16[4,256,256]{2,1,0:T(8,128)(2,1)S(1)}, bf16[4,256,256]{2,1,0:T(8,128)(2,1)}, u32[]{:S(2)}, u32[]{:S(2)}) collective-permute-start(bf16[4,256,256]{2,1,0:T(8,128)(2,1)S(1)} %copy-done.44), channel_id=1, source_target_pairs={{0,8},{4,12},{8,16},{12,20},{16,24},{20,28},{24,0},{28,4},{1,9},{5... | collective-permute-start | bytes 1572872 | tf_op jit(solution)/shard_map/ppermute | solution.py:105
  487.4 28.9 %collective-permute-start.83 = (bf16[1024,256]{1,0:T(8,128)(2,1)S(1)}, bf16[1024,256]{1,0:T(8,128)(2,1)}, u32[]{:S(2)}, u32[]{:S(2)}) collective-permute-start(bf16[1024,256]{1,0:T(8,128)(2,1)S(1)} %fusion.26), channel_id=1, source_target_pairs={{0,2},{1,3},{2,0},{3,1},{4,6},{5,7},{6,4},{7,5},{8,10},{9,11},{10,... | collective-permute-start | bytes 1572872 | tf_op jit(solution)/shard_map/ppermute | solution.py:37
  513.7 35.2 %collective-permute-start.74 = (bf16[4,256,256]{2,1,0:T(8,128)(2,1)}, bf16[4,256,256]{2,1,0:T(8,128)(2,1)S(1)}, u32[]{:S(2)}, u32[]{:S(2)}) collective-permute-start(bf16[4,256,256]{2,1,0:T(8,128)(2,1)} %collective-permute-done.73), channel_id=1, source_target_pairs={{0,4},{4,0},{8,12},{12,8},{16,20},{20,16},{24,28},{28,24},{1,5},{5... | collective-permute-start | bytes 1572872 | tf_op jit(solution)/shard_map/ppermute | solution.py:107
  515.0 31.7 %collective-permute-start.75 = (bf16[4,256,256]{2,1,0:T(8,128)(2,1)}, bf16[4,256,256]{2,1,0:T(8,128)(2,1)S(1)}, u32[]{:S(2)}, u32[]{:S(2)}) collective-permute-start(bf16[4,256,256]{2,1,0:T(8,128)(2,1)} %collective-permute-done.73), channel_id=1, source_target_pairs={{0,8},{4,12},{8,16},{12,20},{16,24},{20,28},{24,0},{28,4},{1,9},{5... | collective-permute-start | bytes 1572872 | tf_op jit(solution)/shard_map/ppermute | solution.py:105
  516.3 22.2 %collective-permute-start.64 = (f32[54,1024]{1,0:T(8,128)S(1)}, f32[54,1024]{1,0:T(8,128)S(1)}, u32[]{:S(2)}, u32[]{:S(2)}) collective-permute-start(f32[54,1024]{1,0:T(8,128)S(1)} %pad_maximum_fusion.7), channel_id=1, source_target_pairs={{0,16},{4,20},{8,24},{12,28},{16,0},{20,4},{24,8},{28,12},{1,17},{... | collective-permute-start | bytes 663560 | tf_op jit(solution)/shard_map/ppermute | solution.py:37
  546.7 15.9 %collective-permute-start.77 = (bf16[4,256,256]{2,1,0:T(8,128)(2,1)S(1)}, bf16[4,256,256]{2,1,0:T(8,128)(2,1)S(1)}, u32[]{:S(2)}, u32[]{:S(2)}) collective-permute-start(bf16[4,256,256]{2,1,0:T(8,128)(2,1)S(1)} %collective-permute-done.75), channel_id=1, source_target_pairs={{0,8},{4,12},{8,16},{12,20},{16,24},{20,28},{24,0},{28,4},{1,9},{5... | collective-permute-start | bytes 1572872 | tf_op jit(solution)/shard_map/ppermute | solution.py:105
  548.1 20.4 %collective-permute-start.76 = (bf16[4,256,256]{2,1,0:T(8,128)(2,1)S(1)}, bf16[4,256,256]{2,1,0:T(8,128)(2,1)S(1)}, u32[]{:S(2)}, u32[]{:S(2)}) collective-permute-start(bf16[4,256,256]{2,1,0:T(8,128)(2,1)S(1)} %collective-permute-done.75), channel_id=1, source_target_pairs={{0,4},{4,0},{8,12},{12,8},{16,20},{20,16},{24,28},{28,24},{1,5},{5... | collective-permute-start | bytes 1572872 | tf_op jit(solution)/shard_map/ppermute | solution.py:107
  566.9 49.4 %collective-permute-start.80 = (bf16[1024,768]{1,0:T(8,128)(2,1)}, bf16[1024,768]{1,0:T(8,128)(2,1)}, u32[]{:S(2)}, u32[]{:S(2)}) collective-permute-start(bf16[1024,768]{1,0:T(8,128)(2,1)} %fusion.3), channel_id=1, source_target_pairs={{0,2},{1,3},{2,0},{3,1},{4,6},{5,7},{6,4},{7,5},{8,10},{9,11},{10,... | collective-permute-start | bytes 4718600 | tf_op jit(solution)/shard_map/ppermute | solution.py:37
  (167 other events, 1768.4 us)
Sparse Core Ops, SparseCore 0:
  307.2 67.0 reduce-scatter.9
  377.9 87.0 reduce-scatter.11
  621.0 65.7 reduce-scatter.7

commit v2 on v1

v2 whole, which is shorter than its diff:
```python
import functools
import math

import jax
import jax.numpy as jnp
from jax import lax
from jax.experimental import pallas as pl
from jax.experimental.pallas import tpu as pltpu
from jax.sharding import PartitionSpec as P

HD = 64
SUB = 32
BF = jnp.bfloat16
F = jnp.float32
VMEM_LIMIT = 56 * 2**20
EPS = 1e-6


def dot_nn(a, b):
    return lax.dot_general(a, b, (((1,), (0,)), ((), ())), preferred_element_type=F)


def dot_nt(a, b):
    return lax.dot_general(a, b, (((1,), (1,)), ((), ())), preferred_element_type=F)


def dot_tn(a, b):
    return lax.dot_general(a, b, (((0,), (0,)), ((), ())), preferred_element_type=F)


def params():
    return pltpu.CompilerParams(vmem_limit_bytes=VMEM_LIMIT)


def swap(x, axis, delta):
    n = lax.axis_size(axis)
    return lax.ppermute(x, axis, [(i, i ^ delta) for i in range(n)])


def spread(x):
    n = lax.axis_size("rows")
    blocks = [None] * n
    blocks[0] = x
    for j in range(2, n, 2):
        blocks[j] = swap(x, "rows", j)
    for j in range(0, n, 2):
        blocks[j + 1] = swap(blocks[j], "rows", 1)
    return blocks


def near_sums(blocks):
    out = []
    for j in range(0, len(blocks), 2):
        near = blocks[j].astype(F) + swap(blocks[j + 1], "rows", 1).astype(F)
        out.append(near.astype(BF))
    return out


def far_sum(near):
    total = near[0].astype(F)
    for j in range(1, len(near)):
        total = total + swap(near[j], "rows", 2 * j).astype(F)
    return total


def collect(blocks):
    return far_sum(near_sums(blocks))


def double(x, axis, place):
    delta = 1
    while delta < lax.axis_size(axis):
        other = swap(x, axis, delta)
        high = (place & delta) != 0
        x = jnp.where(high, jnp.concatenate([other, x]), jnp.concatenate([x, other]))
        delta *= 2
    return x


def merge_step(sums, gathered, axis, place, delta):
    rows = sums.shape[0]
    other = swap(jnp.concatenate([sums, gathered]), axis, delta)
    high = (place & delta) != 0
    theirs = other[rows:]
    gathered = jnp.where(
        high, jnp.concatenate([theirs, gathered]), jnp.concatenate([gathered, theirs])
    )
    return sums + other[:rows], gathered


def add_over(sums, axis):
    delta = 1
    while delta < lax.axis_size(axis):
        sums = sums + swap(sums, axis, delta)
        delta *= 2
    return sums


def tree(parts):
    while len(parts) > 1:
        parts = [a + b for a, b in zip(parts[::2], parts[1::2])]
    return parts[0]


def everyone(x, axis):
    return [x] + [swap(x, axis, j) for j in range(1, lax.axis_size(axis))]


def in_order(blocks, place):
    stacked = jnp.stack(blocks)
    return jnp.take(stacked, jnp.arange(len(blocks), dtype=jnp.int32) ^ place, axis=0)


def ring_perm(n, step, flip):
    lines = n // 2
    return [(i, ((i // 2 + step) % lines) * 2 + ((i % 2) ^ flip)) for i in range(n)]


def ring_gather(x):
    n = lax.axis_size("dp")
    out = []
    held = x
    for step in range(n // 2):
        if step:
            held = lax.ppermute(held, "dp", ring_perm(n, 1, 0))
        out.append(held)
        out.append(lax.ppermute(held, "dp", ring_perm(n, 0, 1)))
    return out


def ring_source(n, place, slot):
    lines = n // 2
    return ((place // 2 - slot // 2) % lines) * 2 + ((place % 2) ^ (slot % 2))


def ring_target(n, place, slot):
    lines = n // 2
    return ((place // 2 + slot // 2) % lines) * 2 + ((place % 2) ^ (slot % 2))


def scatter_side(grads):
    n = lax.axis_size("dp")
    side = lax.axis_index("dp") % 2
    bands = grads.reshape(n // 2, 2, grads.shape[0] // n, grads.shape[1])
    mine = lax.dynamic_index_in_dim(bands, side, 1, keepdims=False)
    theirs = lax.dynamic_index_in_dim(bands, 1 - side, 1, keepdims=False)
    return mine, lax.ppermute(theirs, "dp", ring_perm(n, 0, 1))


def scatter_lines(mine, theirs):
    n = lax.axis_size("dp")
    lines = n // 2
    line = lax.axis_index("dp") // 2
    half = (mine.astype(F) + theirs.astype(F)).astype(BF)
    pieces = [lax.dynamic_index_in_dim(half, line, 0, keepdims=False)]
    for step in range(1, lines):
        piece = lax.dynamic_index_in_dim(half, (line + step) % lines, 0, keepdims=False)
        pieces.append(lax.ppermute(piece, "dp", ring_perm(n, step, 0)))
    return pieces


def tie(*values):
    return lax.optimization_barrier(values)


def move_up(v, axis):
    shape = list(v.shape)
    shape[axis] = 1
    kept = lax.slice_in_dim(v, 0, v.shape[axis] - 1, axis=axis)
    return jnp.concatenate([jnp.zeros(shape, v.dtype), kept], axis=axis)


def move_down(v, axis):
    shape = list(v.shape)
    shape[axis] = 1
    kept = lax.slice_in_dim(v, 1, v.shape[axis], axis=axis)
    return jnp.concatenate([kept, jnp.zeros(shape, v.dtype)], axis=axis)


def band_mask(kernels):
    width = SUB * kernels
    row = lax.broadcasted_iota(jnp.int32, (SUB, width), 0)
    lane = lax.broadcasted_iota(jnp.int32, (SUB, width), 1)
    return (lane // kernels) == row


def split_dot(a, b):
    high = a.astype(BF)
    rest = (a - high.astype(F)).astype(BF)
    return dot_nn(high, b) + dot_nn(rest, b)


def widen_mask(block, kernels):
    row = lax.broadcasted_iota(jnp.int32, (block, block * kernels), 0)
    lane = lax.broadcasted_iota(jnp.int32, (block, block * kernels), 1)
    return jnp.where(lane // kernels == row, 1.0, 0.0).astype(BF)


def tile_mask(block, kernels):
    row = lax.broadcasted_iota(jnp.int32, (kernels, block * kernels), 0)
    lane = lax.broadcasted_iota(jnp.int32, (kernels, block * kernels), 1)
    return jnp.where(lane % kernels == row, 1.0, 0.0).astype(BF)


def conv_forward(codes, select, style, images, bank, side):
    groups = len(images)
    low, channels = images[0].shape
    rows = groups * low
    kernels, width = bank.shape[3], bank.shape[4]
    pad, depth = codes.shape
    block = min(channels, 128)
    steps = channels // block
    parts = block // SUB
    span = SUB * kernels

    def body(c_ref, sel_ref, sty_ref, *rest):
        x_refs = rest[:groups]
        b_ref, out_ref, raw_ref, dem_ref, xs_ref, mix_ref, sc_ref = rest[groups : groups + 7]
        acc, en, scale, mix_row, widen = rest[groups + 7 :]
        step = pl.program_id(0)

        @pl.when(step == 0)
        def _():
            acc[...] = jnp.zeros_like(acc)
            en[...] = jnp.zeros_like(en)
            logits = dot_nn(c_ref[...], sel_ref[...])
            e = jnp.exp(logits - jnp.max(logits, axis=1, keepdims=True))
            mixing = e / jnp.sum(e, axis=1, keepdims=True)
            mix_ref[...] = mixing
            mix_row[...] = split_dot(mixing, tile_mask(block, kernels))
            scale[...] = dot_nn(c_ref[...], sty_ref[...]) + 1.0
            sc_ref[...] = scale[...]
            widen[...] = widen_mask(block, kernels)

        here = scale[:, pl.ds(pl.multiple_of(step * block, block), block)]
        wide_scale = split_dot(here, widen[...]) * mix_row[...]
        mask = band_mask(kernels)
        xs = []
        for s in range(groups):
            xs.append((x_refs[s][...].astype(F) * here[s : s + 1]).astype(BF))
            xs_ref[s * low : (s + 1) * low] = xs[s]
        a = []
        for s in range(groups):
            a.append((dot_nn(xs[s], widen[...]) * mix_row[s : s + 1]).astype(BF))
        left = []
        for u in range(parts):
            cut = slice(u * span, (u + 1) * span)
            pieces = [v[:, cut] for v in a]
            for s in range(groups):
                pieces.append(jnp.where(mask, wide_scale[s : s + 1, cut], 0.0).astype(BF))
            left.append(jnp.concatenate(pieces))
        energy = en[...]
        for t in range(9):
            b = b_ref[t // 3, t % 3].reshape(block * kernels, width)
            total = acc[t]
            for u in range(parts):
                p = dot_nn(left[u], b[u * span : (u + 1) * span])
                total = total + p[:rows]
                m = p[rows:]
                energy = energy + jnp.sum((m * m).reshape(groups, SUB // 8, 8, width), axis=1)
            acc[t] = total
        en[...] = energy

        @pl.when(step == steps - 1)
        def _():
            demod = lax.rsqrt(jnp.sum(en[...], axis=1, keepdims=True) + 1e-8)
            dem_ref[...] = demod
            for s in range(groups):
                v = [acc[t, s * low : (s + 1) * low].reshape(side, side, width) for t in range(9)]
                for py in range(2):
                    h = []
                    for tx in range(3):
                        if py == 0:
                            h.append(move_up(v[tx], 0) + v[3 + tx] + v[6 + tx])
                        else:
                            h.append(v[tx] + v[3 + tx] + move_down(v[6 + tx], 0))
                    for px in range(2):
                        if px == 0:
                            o = move_up(h[0], 1) + h[1] + h[2]
                        else:
                            o = h[0] + h[1] + move_down(h[2], 1)
                        o = o.reshape(low, width)
                        q = (py * 2 + px) * low
                        raw_ref[s, q : q + low] = o.astype(raw_ref.dtype)
                        out_ref[s, q : q + low] = (o * demod[s]).astype(BF)

    return pl.pallas_call(
        body,
        grid=(steps,),
        in_specs=[
            pl.BlockSpec((pad, depth), lambda i: (0, 0)),
            pl.BlockSpec((depth, kernels), lambda i: (0, 0)),
            pl.BlockSpec((depth, channels), lambda i: (0, 0)),
        ]
        + [pl.BlockSpec((low, block), lambda i: (0, i))] * groups
        + [pl.BlockSpec((3, 3, block, kernels, width), lambda i: (0, 0, i, 0, 0))],
        out_specs=[
            pl.BlockSpec((groups, 4 * low, width), lambda i: (0, 0, 0)),
            pl.BlockSpec((groups, 4 * low, width), lambda i: (0, 0, 0)),
            pl.BlockSpec((groups, 1, width), lambda i: (0, 0, 0)),
            pl.BlockSpec((rows, block), lambda i: (0, i)),
            pl.BlockSpec((pad, kernels), lambda i: (0, 0)),
            pl.BlockSpec((pad, channels), lambda i: (0, 0)),
        ],
        out_shape=[
            jax.ShapeDtypeStruct((groups, 4 * low, width), BF),
            jax.ShapeDtypeStruct((groups, 4 * low, width), BF),
            jax.ShapeDtypeStruct((groups, 1, width), F),
            jax.ShapeDtypeStruct((rows, channels), BF),
            jax.ShapeDtypeStruct((pad, kernels), F),
            jax.ShapeDtypeStruct((pad, channels), F),
        ],
        scratch_shapes=[
            pltpu.VMEM((9, rows, width), F),
            pltpu.VMEM((groups, 8, width), F),
            pltpu.VMEM((pad, channels), F),
            pltpu.VMEM((pad, block * kernels), F),
            pltpu.VMEM((block, block * kernels), BF),
        ],
        compiler_params=params(),
        cost_estimate=pl.CostEstimate(
            flops=27 * rows * channels * kernels * width,
            bytes_accessed=18 * channels * kernels * width,
            transcendentals=0,
        ),
        name="conv_forward",
    )(codes, select, style, *images, bank)


def conv_back(gs, xs, mixing, bank, groups):
    _, rows, width = gs.shape
    channels, kernels = xs.shape[1], bank.shape[3]
    pad = mixing.shape[0]
    block = min(channels, 128)
    steps = channels // block
    low = rows // groups

    def body(g_ref, x_ref, m_ref, b_ref, low_ref, mix_ref, acc, mix_row, widen):
        step = pl.program_id(0)

        @pl.when(step == 0)
        def _():
            acc[...] = jnp.zeros_like(acc)
            mix_row[...] = split_dot(m_ref[...], tile_mask(block, kernels))
            widen[...] = widen_mask(block, kernels)

        total = None
        for t in range(9):
            p = dot_nt(g_ref[t], b_ref[t // 3, t % 3].reshape(block * kernels, width))
            total = p if total is None else total + p
        wide = dot_nn(x_ref[...], widen[...])
        acc[...] += jnp.sum((wide * total).reshape(groups, low // 8, 8, block * kernels), axis=1)
        for s in range(groups):
            cut = slice(s * low, (s + 1) * low)
            mixed = (total[cut] * mix_row[s : s + 1]).astype(BF)
            low_ref[s] = dot_nt(mixed, widen[...]).astype(BF)

        @pl.when(step == steps - 1)
        def _():
            sums = jnp.sum(acc[...], axis=1)
            mix_ref[...] = lax.dot_general(
                sums,
                tile_mask(block, kernels).astype(F),
                (((1,), (1,)), ((), ())),
                precision=lax.Precision.HIGHEST,
                preferred_element_type=F,
            )

    return pl.pallas_call(
        body,
        grid=(steps,),
        in_specs=[
            pl.BlockSpec((9, rows, width), lambda i: (0, 0, 0)),
            pl.BlockSpec((rows, block), lambda i: (0, i)),
            pl.BlockSpec((pad, kernels), lambda i: (0, 0)),
            pl.BlockSpec((3, 3, block, kernels, width), lambda i: (0, 0, i, 0, 0)),
        ],
        out_specs=[
            pl.BlockSpec((groups, low, block), lambda i: (0, 0, i)),
            pl.BlockSpec((groups, kernels), lambda i: (0, 0)),
        ],
        out_shape=[
            jax.ShapeDtypeStruct((groups, low, channels), BF),
            jax.ShapeDtypeStruct((groups, kernels), F),
        ],
        scratch_shapes=[
            pltpu.VMEM((groups, 8, block * kernels), F),
            pltpu.VMEM((pad, block * kernels), F),
            pltpu.VMEM((block, block * kernels), BF),
        ],
        compiler_params=params(),
        cost_estimate=pl.CostEstimate(
            flops=18 * rows * channels * kernels * width,
            bytes_accessed=18 * channels * kernels * width,
            transcendentals=0,
        ),
        name="conv_back",
    )(gs, xs, mixing, bank)


def bank_energy(place, mixing, scale, ge, bank, group):
    samples, kernels = mixing.shape
    band = scale.shape[1]
    width = bank.shape[4]
    span = SUB * kernels
    bands = band // SUB
    chunk = min(samples, 32)
    chunks = samples // chunk
    kind = BF if chunks == 1 else F

    def body(place_ref, m_ref, s_ref, g_ref, b_ref, e_ref, se_ref, me_ref, rows, wides, diag):
        u, part = pl.program_id(0), pl.program_id(1)
        cut = pl.ds(pl.multiple_of(part * chunk, chunk), chunk)

        @pl.when((u == 0) & (part == 0))
        def _():
            rows[...] = split_dot(m_ref[...], tile_mask(band, kernels))
            wides[...] = split_dot(s_ref[...], widen_mask(band, kernels))

        lanes = pl.ds(pl.multiple_of(u * span, span), span)
        scaled = rows[cut, lanes] * wides[cut, lanes]
        mask = band_mask(kernels)[None]
        d = jnp.where(mask, scaled[:, None, :], 0.0).astype(BF).reshape(chunk * SUB, span)
        d_turned = d.T
        ge = 2.0 * g_ref[...]
        acc = None
        for t in range(9):
            b = b_ref[t // 3, t % 3].reshape(span, width)
            m = dot_nn(d, b)
            w = (m.reshape(chunk, SUB, width) * ge).reshape(chunk * SUB, width).astype(BF)
            e = dot_nn(d_turned, w).reshape(SUB, kernels, width)
            if chunks == 1:
                e_ref[t // 3, t % 3] = e.astype(kind)
            else:
                e_ref[t // 3, t % 3] = e + jnp.where(part == 0, 0.0, e_ref[t // 3, t % 3])
            p = dot_nt(w, b)
            acc = p if acc is None else acc + p
        kept = jnp.where(mask, acc.reshape(chunk, SUB, span), 0.0)
        diag[cut, lanes] = jnp.sum(kept, axis=1)

        @pl.when((u == bands - 1) & (part == chunks - 1))
        def _():
            exact = dict(precision=lax.Precision.HIGHEST, preferred_element_type=F)
            over = (((1,), (1,)), ((), ()))
            se = lax.dot_general(diag[...] * rows[...], widen_mask(band, kernels).astype(F), over, **exact)
            me = lax.dot_general(diag[...] * wides[...], tile_mask(band, kernels).astype(F), over, **exact)
            for s in range(samples):
                to = pl.ds(s // group * group + lax.bitwise_xor(place_ref[0], s % group), 1)
                se_ref[to] = se[s : s + 1]
                me_ref[to] = me[s : s + 1]

    return pl.pallas_call(
        body,
        grid_spec=pltpu.PrefetchScalarGridSpec(
            num_scalar_prefetch=1,
            grid=(bands, chunks),
            in_specs=[
                pl.BlockSpec((samples, kernels), lambda i, c, s: (0, 0)),
                pl.BlockSpec((samples, band), lambda i, c, s: (0, 0)),
                pl.BlockSpec((chunk, 1, width), lambda i, c, s: (c, 0, 0)),
                pl.BlockSpec(
                    (3, 3, SUB, kernels, width), lambda i, c, s: (0, 0, s[1] * bands + i, 0, 0)
                ),
            ],
            out_specs=[
                pl.BlockSpec((3, 3, SUB, kernels, width), lambda i, c, s: (0, 0, i, 0, 0)),
                pl.BlockSpec((samples, band), lambda i, c, s: (0, 0)),
                pl.BlockSpec((samples, kernels), lambda i, c, s: (0, 0)),
            ],
            scratch_shapes=[
                pltpu.VMEM((samples, band * kernels), F),
                pltpu.VMEM((samples, band * kernels), F),
                pltpu.VMEM((samples, band * kernels), F),
            ],
        ),
        out_shape=[
            jax.ShapeDtypeStruct((3, 3, band, kernels, width), kind),
            jax.ShapeDtypeStruct((samples, band), F),
            jax.ShapeDtypeStruct((samples, kernels), F),
        ],
        compiler_params=params(),
        cost_estimate=pl.CostEstimate(
            flops=54 * bands * samples * SUB * span * width,
            bytes_accessed=36 * bands * span * width,
            transcendentals=0,
        ),
        name="bank_energy",
    )(place, mixing, scale, ge, bank)


def line_sums(g, tap, axis):
    if tap == 0:
        return g[1] + move_down(g[0], axis)
    if tap == 1:
        return g[0] + g[1]
    return g[0] + move_up(g[1], axis)


def bank_main(tap_row, before, sources, scale, at, taps, energy, side):
    blocks = len(taps)
    groups, points, width = taps[0].shape
    low = side * side
    held = blocks * groups * low
    band, kernels = energy.shape[2], energy.shape[3]

    def body(src_ref, scale_ref, a_ref, *rest):
        g_refs = rest[:blocks]
        e_ref = rest[blocks]
        o_ref, lines, sums = rest[-3:]
        tx = pl.program_id(0)

        @pl.when(tx == 0)
        def _():
            for b in range(blocks):
                for s in range(groups):
                    g = g_refs[b][s].astype(F).reshape(2, 2, side, side, width)
                    at_row = pl.multiple_of((src_ref[b] * groups + s) * low, low)
                    for px in range(2):
                        v = line_sums((g[0, px], g[1, px]), tap_row, 0)
                        lines[px, pl.ds(at_row, low)] = v.reshape(low, width)

        for tap in range(3):

            @pl.when(tx == tap)
            def _():
                for b in range(blocks * groups):
                    cut = slice(b * low, (b + 1) * low)
                    pair = [lines[px, cut].reshape(side, side, width) for px in range(2)]
                    sums[cut] = line_sums(pair, tap, 1).reshape(low, width).astype(BF)

        p = dot_nn(a_ref[...], sums[...]).reshape(band, kernels, width)
        o_ref[0, 0] = (p + e_ref[0, 0].astype(F)) * scale_ref[0]

    whole = [] if before is None else [before]
    tap_block = pl.BlockSpec((1, 1, band, kernels, width), lambda t: (tap_row, t, 0, 0, 0))
    return pl.pallas_call(
        body,
        grid=(3,),
        in_specs=[smem(), smem(), pl.BlockSpec((band * kernels, held), lambda t: (0, 0))]
        + [pl.BlockSpec((groups, points, width), lambda t: (0, 0, 0))] * blocks
        + [tap_block]
        + [pl.BlockSpec(memory_space=pl.ANY)] * len(whole),
        out_specs=tap_block,
        out_shape=jax.ShapeDtypeStruct((3, 3, band, kernels, width), F),
        input_output_aliases={4 + blocks: 0} if whole else {},
        scratch_shapes=[pltpu.VMEM((2, held, width), F), pltpu.VMEM((held, width), BF)],
        compiler_params=params(),
        cost_estimate=pl.CostEstimate(
            flops=6 * band * kernels * held * width,
            bytes_accessed=6 * held * width + 18 * band * kernels * width,
            transcendentals=0,
        ),
        name="bank_main",
    )(sources, scale, at, *taps, energy, *whole)


def tap_sums(grads, demod, raw, side):
    groups = len(grads)
    _, points, width = raw.shape
    low = side * side

    def body(d_ref, r_ref, *rest):
        g_refs = rest[:groups]
        taps_ref, sums_ref, en_ref = rest[groups:]
        for s in range(groups):
            part = g_refs[s][:points].astype(F)
            demod = d_ref[s]
            grad_demod = jnp.sum(part * r_ref[s].astype(F), axis=0, keepdims=True)
            en_ref[s] = -0.5 * grad_demod * demod * demod * demod
            taps_ref[s] = (part * demod).astype(BF)
            g = taps_ref[s].astype(F).reshape(2, 2, side, side, width)
            for ty in range(3):
                lines = [line_sums((g[0, px], g[1, px]), ty, 0) for px in range(2)]
                for tx in range(3):
                    v = line_sums(lines, tx, 1).reshape(low, width).astype(BF)
                    sums_ref[3 * ty + tx, s * low : (s + 1) * low] = v

    return pl.pallas_call(
        body,
        out_shape=[
            jax.ShapeDtypeStruct((groups, points, width), BF),
            jax.ShapeDtypeStruct((9, groups * low, width), BF),
            jax.ShapeDtypeStruct((groups, 1, width), F),
        ],
        compiler_params=params(),
        name="tap_sums",
    )(demod, raw, *grads)


def rms(field, gain):
    inverse = lax.rsqrt(jnp.mean(field * field, axis=-1, keepdims=True) + EPS)
    return field * inverse * gain, inverse


def rms_back(field, gain, grad_out):
    inverse = lax.rsqrt(jnp.mean(field * field, axis=-1, keepdims=True) + EPS)
    scaled = grad_out * gain
    grad_gain = jnp.sum(grad_out * field * inverse, axis=0, keepdims=True)
    mean = jnp.mean(scaled * field, axis=-1, keepdims=True)
    return inverse * scaled - field * inverse**3 * mean, grad_gain


def sigmoid(v):
    return 1.0 / (1.0 + jnp.exp(-v))


def silu_slope(v):
    q = sigmoid(v)
    return q * (1.0 + v * (1.0 - q))


def self_prob(q, k):
    kf = k.astype(F)
    square = jnp.sum(kf * kf, axis=1, keepdims=True)
    scores = (2.0 * dot_nt(k, q) - square) * (1.0 / math.sqrt(HD))
    e = jnp.exp(scores - jnp.max(scores, axis=0, keepdims=True))
    return e * (1.0 / jnp.sum(e, axis=0, keepdims=True))


def cross_prob(q, k):
    scores = dot_nt(k, q) * (1.0 / math.sqrt(HD))
    e = jnp.exp(scores - jnp.max(scores, axis=0, keepdims=True))
    return e * (1.0 / jnp.sum(e, axis=0, keepdims=True))


def side_slot(own_ref, send_ref, j, start, width):
    at = start + j // 2 * width
    return (send_ref if j % 2 else own_ref), slice(at, at + width)


def smem():
    return pl.BlockSpec(memory_space=pltpu.SMEM)


def vmem(count):
    return [pl.BlockSpec(memory_space=pltpu.VMEM)] * count


def attn_forward(place, conv_parts, noise, gains, wqkv, wo):
    n = len(wo)
    points, width = conv_parts[0].shape
    share, channels = wo[0].shape

    def body(place_ref, noise_ref, gains_ref, *rest):
        part_r, wqkv_r, wo_r = (rest[i * n : (i + 1) * n] for i in range(3))
        conv_ref, two_ref, qkv_ref, own_ref, send_ref = rest[3 * n :]
        here = place_ref[0]
        for j in range(n):
            start = pl.multiple_of(lax.bitwise_xor(here, j) * width, width)
            conv_ref[:, pl.ds(start, width)] = part_r[j][...]
        out = conv_ref[...].astype(F) + gains_ref[0:1] * noise_ref[...] + gains_ref[1:2]
        one = out * sigmoid(out)
        normed = rms(one, gains_ref[2:3])[0].astype(BF)
        own_ref[:, :channels] = normed
        send_ref[:, :channels] = normed
        two_ref[...] = one
        for j in range(n):
            qkv_ref[j] = dot_nn(normed, wqkv_r[j][...]).astype(BF)
            heads = []
            for h in range(share // HD):
                q, k, v = (
                    qkv_ref[j, :, i * share + h * HD : i * share + (h + 1) * HD] for i in range(3)
                )
                heads.append(dot_tn(self_prob(q, k).astype(BF), v).astype(BF))
            side_ref, cut = side_slot(own_ref, send_ref, j, channels, share)
            side_ref[:, cut] = jnp.concatenate(heads, axis=1)
            two_ref[...] += dot_nn(side_ref[:, cut], wo_r[j][...])

    return pl.pallas_call(
        body,
        in_specs=[smem()] + vmem(2 + 3 * n),
        out_shape=[
            jax.ShapeDtypeStruct((points, channels), BF),
            jax.ShapeDtypeStruct((points, channels), F),
            jax.ShapeDtypeStruct((n, points, 3 * share), BF),
        ]
        + [jax.ShapeDtypeStruct((points, channels + n // 2 * share), BF)] * 2,
        compiler_params=params(),
        cost_estimate=pl.CostEstimate(
            flops=10 * points * channels * channels,
            bytes_accessed=16 * channels * channels,
            transcendentals=points * points * channels // HD,
        ),
        name="attn_forward",
    )(place, noise, gains, *conv_parts, *wqkv, *wo)


def cross_forward(two, gains, cq, co, ckv):
    points, channels = two.shape
    n = len(cq)
    share = cq[0].shape[1]

    def body(two_ref, gains_ref, *rest):
        cq_r, co_r, ckv_r = (rest[i * n : (i + 1) * n] for i in range(3))
        three_ref, mlp_ref, xq_ref, own_ref, send_ref = rest[3 * n :]
        normed = rms(two_ref[...], gains_ref[3:4])[0].astype(BF)
        own_ref[:, :channels] = normed
        send_ref[:, :channels] = normed
        three_ref[...] = two_ref[...]
        for j in range(n):
            xq_ref[j] = dot_nn(normed, cq_r[j][...]).astype(BF)
            heads = []
            for h in range(share // HD):
                q = xq_ref[j, :, h * HD : (h + 1) * HD]
                k = ckv_r[j][:, h * HD : (h + 1) * HD]
                v = ckv_r[j][:, share + h * HD : share + (h + 1) * HD]
                heads.append(dot_tn(cross_prob(q, k).astype(BF), v).astype(BF))
            side_ref, cut = side_slot(own_ref, send_ref, j, channels, share)
            side_ref[:, cut] = jnp.concatenate(heads, axis=1)
            three_ref[...] += dot_nn(side_ref[:, cut], co_r[j][...])
        mlp_ref[...] = rms(three_ref[...], gains_ref[4:5])[0].astype(BF)

    return pl.pallas_call(
        body,
        out_shape=[
            jax.ShapeDtypeStruct((points, channels), F),
            jax.ShapeDtypeStruct((points, channels), BF),
            jax.ShapeDtypeStruct((n, points, share), BF),
        ]
        + [jax.ShapeDtypeStruct((points, channels + n // 2 * share), BF)] * 2,
        compiler_params=params(),
        cost_estimate=pl.CostEstimate(
            flops=5 * points * channels * channels,
            bytes_accessed=8 * channels * channels,
            transcendentals=points * channels,
        ),
        name="cross_forward",
    )(two, gains, *cq, *co, *ckv)


def mlp_core(inputs, grad_out, up, down):
    count = len(inputs)
    points, channels = inputs[0].shape
    hidden = up.shape[1]
    tile = min(hidden, 256)
    steps = hidden // tile
    rows = count * points

    def body(*refs):
        x_r, g_r = refs[:count], refs[count : 2 * count]
        up_ref, down_ref, act_ref, gi_ref = refs[2 * count : 2 * count + 4]
        back_r = refs[2 * count + 4 : 3 * count + 4]
        x_all, g_all, acc = refs[3 * count + 4 :]
        step = pl.program_id(0)

        @pl.when(step == 0)
        def _():
            for j in range(count):
                x_all[j * points : (j + 1) * points] = x_r[j][...]
                g_all[j * points : (j + 1) * points] = g_r[j][...]
            acc[...] = jnp.zeros_like(acc)

        inner = dot_nn(x_all[...], up_ref[...])
        gate = sigmoid(inner)
        act_ref[...] = (inner * gate).astype(BF)
        grad_act = dot_nt(g_all[...], down_ref[...])
        gi_ref[...] = (grad_act * (gate * (1.0 + inner * (1.0 - gate)))).astype(BF)
        acc[...] += dot_nt(gi_ref[...], up_ref[...])

        @pl.when(step == steps - 1)
        def _():
            for j in range(count):
                back_r[j][...] = acc[j * points : (j + 1) * points].astype(BF)

    block = pl.BlockSpec((points, channels), lambda i: (0, 0))
    return pl.pallas_call(
        body,
        grid=(steps,),
        in_specs=[block] * (2 * count)
        + [
            pl.BlockSpec((channels, tile), lambda i: (0, i)),
            pl.BlockSpec((tile, channels), lambda i: (i, 0)),
        ],
        out_specs=[pl.BlockSpec((rows, tile), lambda i: (0, i))] * 2 + [block] * count,
        out_shape=[jax.ShapeDtypeStruct((rows, hidden), BF)] * 2
        + [jax.ShapeDtypeStruct((points, channels), BF)] * count,
        scratch_shapes=[
            pltpu.VMEM((rows, channels), BF),
            pltpu.VMEM((rows, channels), BF),
            pltpu.VMEM((rows, channels), F),
        ],
        compiler_params=params(),
        cost_estimate=pl.CostEstimate(
            flops=6 * rows * channels * hidden,
            bytes_accessed=4 * channels * hidden,
            transcendentals=rows * hidden,
        ),
        name="mlp_core",
    )(*inputs, *grad_out, up, down)


def mlp_rest(inputs, grad_out, grad_inner, acts, down):
    n = len(inputs)
    points, channels = inputs[0].shape
    hidden = acts[0].shape[1]
    tile = min(hidden, 256)
    groups = len(acts)
    each = n // groups

    def body(down_ref, *rest):
        x_r, go_r = rest[:n], rest[n : 2 * n]
        gi_r, act_r = rest[2 * n : 2 * n + groups], rest[2 * n + groups : 2 * n + 2 * groups]
        outs, dw_ref = rest[2 * n + 2 * groups : 3 * n + 2 * groups], rest[3 * n + 2 * groups]
        turned = rest[3 * n + 2 * groups + 1]
        for j in range(n):
            cut = slice(j % each * points, (j % each + 1) * points)
            outs[j][...] = dot_nn(act_r[j // each][cut], down_ref[...]).astype(BF)
        for side, refs, other in ((0, x_r, gi_r), (1, go_r, act_r)):
            for j in range(n):
                turned[:, j * points : (j + 1) * points] = refs[j][...].T
            for c in range(hidden // tile):
                cut = slice(c * tile, (c + 1) * tile)
                total = None
                for g in range(groups):
                    span = each * points
                    p = dot_nn(turned[:, g * span : (g + 1) * span], other[g][:, cut])
                    total = p if total is None else total + p
                at = side * hidden + c * tile
                dw_ref[:, at : at + tile] = total.astype(BF)

    return pl.pallas_call(
        body,
        out_shape=[jax.ShapeDtypeStruct((points, channels), BF)] * n
        + [jax.ShapeDtypeStruct((channels, 2 * hidden), BF)],
        scratch_shapes=[pltpu.VMEM((channels, n * points), BF)],
        compiler_params=params(),
        cost_estimate=pl.CostEstimate(
            flops=6 * n * points * channels * hidden,
            bytes_accessed=16 * channels * hidden,
            transcendentals=0,
        ),
        name="mlp_rest",
    )(down, *inputs, *grad_out, *grad_inner, *acts)


def cross_backward(grad_norm, grad_four, three, two, gains, xq, cq, co, ckv):
    points, channels = three.shape
    n, _, share = xq.shape
    tokens = ckv[0].shape[0]

    def body(gn_ref, g4_ref, three_ref, two_ref, in_ref, xq_ref, *rest):
        cq_r, co_r, ckv_r = (rest[i * n : (i + 1) * n] for i in range(3))
        two_out, gains_ref, own_ref, send_ref = rest[3 * n : 3 * n + 4]
        dkv_r = rest[3 * n + 4 : 4 * n + 4]
        back, gain = rms_back(three_ref[...], in_ref[4:5], gn_ref[...])
        gains_ref[0:1] = gain
        grad_three = g4_ref[...] + back
        gb = grad_three.astype(BF)
        own_ref[:, :channels] = gb
        send_ref[:, :channels] = gb
        grad_norm2 = jnp.zeros((points, channels), F)
        for j in range(n):
            ga = dot_nt(gb, co_r[j][...]).astype(BF)
            kv = ckv_r[j][...]
            gq, gk, gv = [], [], []
            for h in range(share // HD):
                q = xq_ref[j, :, h * HD : (h + 1) * HD]
                k = kv[:, h * HD : (h + 1) * HD]
                v = kv[:, share + h * HD : share + (h + 1) * HD]
                g = ga[:, h * HD : (h + 1) * HD]
                p = cross_prob(q, k)
                gp = dot_nt(v, g)
                gs = p * (gp - jnp.sum(p * gp, axis=0, keepdims=True))
                raw = (gs * (1.0 / math.sqrt(HD))).astype(BF)
                gq.append(dot_tn(raw, k).astype(BF))
                gk.append(dot_nn(raw, q).astype(BF))
                gv.append(dot_nn(p.astype(BF), g).astype(BF))
            side_ref, cut = side_slot(own_ref, send_ref, j, 2 * channels, share)
            side_ref[:, cut] = jnp.concatenate(gq, axis=1)
            dkv_r[j][...] = jnp.concatenate(gk + gv, axis=1)
            grad_norm2 = grad_norm2 + dot_nt(side_ref[:, cut], cq_r[j][...])
        back, gain = rms_back(two_ref[...], in_ref[3:4], grad_norm2)
        gains_ref[1:2] = gain
        two_out[...] = grad_three + back
        gb = two_out[...].astype(BF)
        own_ref[:, channels : 2 * channels] = gb
        send_ref[:, channels : 2 * channels] = gb

    return pl.pallas_call(
        body,
        out_shape=[
            jax.ShapeDtypeStruct((points, channels), F),
            jax.ShapeDtypeStruct((2, channels), F),
        ]
        + [jax.ShapeDtypeStruct((points, 2 * channels + n // 2 * share), BF)] * 2
        + [jax.ShapeDtypeStruct((tokens, 2 * share), BF)] * n,
        compiler_params=params(),
        cost_estimate=pl.CostEstimate(
            flops=8 * points * channels * channels,
            bytes_accessed=12 * channels * channels,
            transcendentals=points * channels,
        ),
        name="cross_backward",
    )(grad_norm, grad_four, three, two, gains, xq, *cq, *co, *ckv)


def attn_backward(place, grad_two, conv, noise, gains, qkv, token_grads, wqkv, wo, width):
    points, channels = grad_two.shape
    n = len(wo)
    share = wo[0].shape[0]
    tokens = token_grads[0].shape[0]

    def body(place_ref, g2_ref, conv_ref, noise_ref, gains_ref, qkv_ref, *rest):
        wqkv_r, wo_r, token_r = (rest[i * n : (i + 1) * n] for i in range(3))
        sums_ref = rest[3 * n]
        share_r = rest[3 * n + 1 : 4 * n + 1]
        own_ref, send_ref, gc_ref = rest[4 * n + 1 :]
        here = place_ref[0]
        grad_two = g2_ref[...]
        gb = grad_two.astype(BF)
        out = conv_ref[...].astype(F) + gains_ref[0:1] * noise_ref[...] + gains_ref[1:2]
        one = out * sigmoid(out)
        grad_norm = jnp.zeros((points, channels), F)
        for j in range(n):
            ga = dot_nt(gb, wo_r[j][...]).astype(BF)
            gq, gk, gv = [], [], []
            for h in range(share // HD):
                q, k, v = (
                    qkv_ref[j, :, i * share + h * HD : i * share + (h + 1) * HD] for i in range(3)
                )
                g = ga[:, h * HD : (h + 1) * HD]
                p = self_prob(q, k)
                gp = dot_nt(v, g)
                gs = p * (gp - jnp.sum(p * gp, axis=0, keepdims=True))
                square = jnp.sum(gs, axis=1, keepdims=True) * (-1.0 / math.sqrt(HD))
                raw = (gs * (2.0 / math.sqrt(HD))).astype(BF)
                gq.append(dot_tn(raw, k).astype(BF))
                gk.append((dot_nn(raw, q) + 2.0 * k.astype(F) * square).astype(BF))
                gv.append(dot_nn(p.astype(BF), g).astype(BF))
            side_ref, cut = side_slot(own_ref, send_ref, j, 0, 3 * share)
            side_ref[:, cut] = jnp.concatenate(gq + gk + gv, axis=1)
            grad_norm = grad_norm + dot_nt(side_ref[:, cut], wqkv_r[j][...])
        back, gain = rms_back(one, gains_ref[2:3], grad_norm)
        grad_conv = (grad_two + back) * silu_slope(out)
        gc_ref[...] = grad_conv.astype(BF)
        for j in range(n):
            start = pl.multiple_of(lax.bitwise_xor(here, j) * width, width)
            share_r[j][:points] = gc_ref[:, pl.ds(start, width)]
            for i in range(2):
                rows = slice(points + i * tokens, points + (i + 1) * tokens)
                share_r[j][rows] = token_r[j][:, i * width : (i + 1) * width]
        sums_ref[0:1] = gain
        sums_ref[1:2] = jnp.sum(grad_conv, axis=0, keepdims=True)
        sums_ref[2:3] = jnp.sum(grad_conv * noise_ref[...], axis=0, keepdims=True)

    return pl.pallas_call(
        body,
        out_shape=[
            jax.ShapeDtypeStruct((3, channels), F),
        ]
        + [jax.ShapeDtypeStruct((points + 2 * tokens, width), BF)] * n
        + [jax.ShapeDtypeStruct((points, n // 2 * 3 * share), BF)] * 2,
        in_specs=[smem()] + vmem(5 + 3 * n),
        scratch_shapes=[pltpu.VMEM((points, channels), BF)],
        compiler_params=params(),
        cost_estimate=pl.CostEstimate(
            flops=24 * points * channels * channels,
            bytes_accessed=24 * channels * channels,
            transcendentals=points * points * channels // HD,
        ),
        name="attn_backward",
    )(place, grad_two, conv, noise, gains, qkv, *wqkv, *wo, *token_grads)


def turn(turned, blocks, start, channels):
    points = blocks[0].shape[0]
    for i, block in enumerate(blocks):
        turned[:, i * points : (i + 1) * points] = block[:, start : start + channels].T


def pair_product(turned, blocks, cut):
    points = blocks[0].shape[0]
    total = None
    for i, block in enumerate(blocks):
        p = dot_nn(turned[:, i * points : (i + 1) * points], block[:, cut])
        total = p if total is None else total + p
    return total.astype(BF)


def cross_weights(attn_pair, cross_pair, grad_pair, count, share):
    points = attn_pair[0].shape[0]
    channels = attn_pair[0].shape[1] - count * share

    def body(*refs):
        attn, cross, grad = refs[:2], refs[2:4], refs[4:6]
        both, out = refs[6 : 6 + count], refs[6 + count : 6 + 2 * count]
        turned = refs[-1]
        turn(turned, cross, 0, channels)
        for i in range(count):
            cut = slice(2 * channels + i * share, 2 * channels + (i + 1) * share)
            both[i][:, :share] = pair_product(turned, grad, cut)
        turn(turned, grad, 0, channels)
        for i in range(count):
            cut = slice(channels + i * share, channels + (i + 1) * share)
            both[i][:, share:] = pair_product(turned, cross, cut)
        turn(turned, grad, channels, channels)
        for i in range(count):
            cut = slice(channels + i * share, channels + (i + 1) * share)
            out[i][...] = pair_product(turned, attn, cut)

    return pl.pallas_call(
        body,
        out_shape=[jax.ShapeDtypeStruct((channels, 2 * share), BF)] * count
        + [jax.ShapeDtypeStruct((channels, share), BF)] * count,
        scratch_shapes=[pltpu.VMEM((channels, 2 * points), BF)],
        compiler_params=params(),
        cost_estimate=pl.CostEstimate(
            flops=12 * count * points * channels * share,
            bytes_accessed=20 * points * channels,
            transcendentals=0,
        ),
        name="cross_weights",
    )(*attn_pair, *cross_pair, *grad_pair)


def attn_weights(attn_pair, grad_pair, count, share):
    points = attn_pair[0].shape[0]
    channels = attn_pair[0].shape[1] - count * share

    def body(*refs):
        attn, grad = refs[:2], refs[2:4]
        out, turned = refs[4 : 4 + 3 * count], refs[-1]
        turn(turned, attn, 0, channels)
        for i in range(count):
            for k in range(3):
                cut = slice((3 * i + k) * share, (3 * i + k + 1) * share)
                out[k * count + i][...] = pair_product(turned, grad, cut)

    return pl.pallas_call(
        body,
        out_shape=[jax.ShapeDtypeStruct((channels, share), BF)] * (3 * count),
        scratch_shapes=[pltpu.VMEM((channels, 2 * points), BF)],
        compiler_params=params(),
        cost_estimate=pl.CostEstimate(
            flops=12 * count * points * channels * share,
            bytes_accessed=16 * points * channels,
            transcendentals=0,
        ),
        name="attn_weights",
    )(*attn_pair, *grad_pair)


def band_prepare(place, received, codes, select, style, points_low):
    n_dp, _, band = received.shape
    samples, depth = codes.shape
    kernels = select.shape[1]
    low = n_dp * points_low // samples
    columns = samples * low
    step = 8

    def body(place_ref, x_ref, c_ref, sel_ref, sty_ref, at_ref, mix_ref, scale_ref, turned):
        logits = dot_nn(c_ref[...], sel_ref[...])
        e = jnp.exp(logits - jnp.max(logits, axis=1, keepdims=True))
        mixing = e / jnp.sum(e, axis=1, keepdims=True)
        mix_ref[...] = mixing
        scale_ref[...] = dot_nn(c_ref[...], sty_ref[...]) + 1.0
        for b in range(n_dp):
            turned[:, b * points_low : (b + 1) * points_low] = x_ref[b, :points_low].astype(F).T
        row = lax.broadcasted_iota(jnp.int32, (samples, columns), 0)
        lane = lax.broadcasted_iota(jnp.int32, (samples, columns), 1)
        repeat = jnp.where(lane // low == row, 1.0, 0.0).astype(BF)
        high = mixing.astype(BF)
        rest = (mixing - high.astype(F)).astype(BF)
        wide = dot_tn(high, repeat) + dot_tn(rest, repeat)
        for i in range(band // step):
            x = turned[i * step : (i + 1) * step]
            a = (x[:, None, :] * wide[None]).reshape(step * kernels, columns)
            at_ref[i * step * kernels : (i + 1) * step * kernels] = a.astype(BF)

    return pl.pallas_call(
        body,
        in_specs=[smem()] + vmem(4),
        out_shape=[
            jax.ShapeDtypeStruct((band * kernels, columns), BF),
            jax.ShapeDtypeStruct((samples, kernels), F),
            jax.ShapeDtypeStruct((samples, band), F),
        ],
        scratch_shapes=[pltpu.VMEM((band, columns), F)],
        compiler_params=params(),
        name="band_prepare",
    )(place, received, codes, select, style)


def side_outputs(place, three, branch, image_grad, color_scale, colors, bias, context, shares, ck, cv, gains, late, count_sums, count_all, side):
    points, channels = three.shape
    n, parts = len(shares), len(branch)
    share = ck.shape[1]
    tokens = context.shape[0] // n
    low = side * side
    exact = dict(precision=lax.Precision.HIGHEST, preferred_element_type=F)

    def body(place_ref, three_ref, gi_ref, cs_ref, col_ref, bias_ref, ctx_ref, ck_ref, cv_ref, gains_ref, late_ref, *rest):
        branch_r, share_r = rest[:parts], rest[parts : parts + n]
        feat_ref, color_ref, dkv_ref, pack_ref, four_ref, keys, values = rest[parts + n :]
        here = place_ref[0]
        four = three_ref[...]
        for b in branch_r:
            four = four + b[...].astype(F)
        four_ref[...] = four
        row = lax.broadcasted_iota(jnp.int32, (points, points), 0)
        lane = lax.broadcasted_iota(jnp.int32, (points, points), 1)
        phase, spot = lane // low, lane % low
        line = 2 * (spot // side) + phase // 2
        target = 2 * side * line + 2 * (spot % side) + phase % 2
        order = jnp.where(row == target, 1.0, 0.0)
        moved = lax.dot_general(order, four, (((1,), (0,)), ((), ())), **exact)
        feat_ref[...] = moved.reshape(1, 2 * side, 2 * side, channels)
        scale, col = cs_ref[...], col_ref[...]
        tint = col * scale
        color_ref[...] = bias_ref[...] + lax.dot_general(
            tint, four_ref[...], (((1,), (1,)), ((), ())), **exact
        )
        gi = gi_ref[...]
        image = lax.dot_general(gi, four_ref[...], (((0,), (0,)), ((), ())), **exact)
        for j in range(n):
            cut = slice(j * tokens, (j + 1) * tokens)
            keys[cut] = share_r[j][points : points + tokens]
            values[cut] = share_r[j][points + tokens : points + 2 * tokens]
        turned = ctx_ref[...]
        dkv_ref[:, :share] = dot_tn(turned, keys[...]).astype(BF)
        dkv_ref[:, share:] = dot_tn(turned, values[...]).astype(BF)
        grad = dot_nt(keys[...], ck_ref[...]) + dot_nt(values[...], cv_ref[...])
        pack_ref[...] = jnp.zeros_like(pack_ref)
        total = None
        for j in range(n):
            part = grad[j * tokens : (j + 1) * tokens]
            total = part if total is None else total + part
            row = count_sums + 2 * n + lax.bitwise_xor(here, j)
            pack_ref[pl.ds(row, 1)] = jnp.sum(part, axis=0, keepdims=True)
        pack_ref[:tokens] = total
        pack_ref[tokens : tokens + 2] = gains_ref[...]
        pack_ref[tokens + 2 : tokens + 5] = image * scale
        lane = lax.broadcasted_iota(jnp.int32, (1, channels), 1)
        row = jnp.zeros((1, channels), F)
        for c in range(3):
            row = jnp.where(lane == c, jnp.sum(gi[:, c : c + 1]), row)
        pack_ref[tokens + 5 : tokens + 6] = row
        pack_ref[tokens + 6 : tokens + 9] = late_ref[...]
        pack_ref[pl.ds(count_sums + 3 * n + here, 1)] = jnp.sum(image * col, axis=0, keepdims=True)

    return pl.pallas_call(
        body,
        in_specs=[smem()] + vmem(10 + parts + n),
        out_shape=[
            jax.ShapeDtypeStruct((1, 2 * side, 2 * side, channels), F),
            jax.ShapeDtypeStruct((3, points), F),
            jax.ShapeDtypeStruct((channels, 2 * share), BF),
            jax.ShapeDtypeStruct((count_all, channels), F),
        ],
        scratch_shapes=[
            pltpu.VMEM((points, channels), F),
            pltpu.VMEM((n * tokens, share), BF),
            pltpu.VMEM((n * tokens, share), BF),
        ],
        compiler_params=params(),
        name="side_outputs",
    )(place, three, image_grad, color_scale, colors, bias, context, ck, cv, gains, late, *branch, *shares)


def late_sums_kernel(place, scale, pack, low_parts, images, own_scale, energy, mixing_sum, mixing, count_sums, at_sum):
    low, channels = images.shape
    parts = len(low_parts)
    n, kernels = mixing.shape
    rows = mixing_sum.shape[0]

    def body(place_ref, scale_ref, pack_ref, im_ref, own_ref, en_ref, ms_ref, mix_ref, *rest):
        low_r, (out_ref, grad_ref) = rest[:parts], rest[parts:]
        here = place_ref[0]
        total = low_r[0][...].astype(F)
        for v in low_r[1:]:
            total = total + v[...].astype(F)
        grad_ref[...] = total * (own_ref[...] * scale_ref[0])
        out_ref[...] = pack_ref[...]
        line = jnp.sum(total * im_ref[...].astype(F), axis=0, keepdims=True)
        out_ref[pl.ds(count_sums + here, 1)] = line
        out_ref[count_sums + n : count_sums + 2 * n] = en_ref[...]
        out_ref[at_sum : at_sum + rows] = ms_ref[...]
        wide = split_dot(mix_ref[...], tile_mask(channels // kernels, kernels))
        lane = lax.broadcasted_iota(jnp.int32, (n, channels), 1) // kernels
        row = lax.bitwise_xor(lax.broadcasted_iota(jnp.int32, (n, channels), 0), here)
        line = jnp.sum(jnp.where(lane == row, wide, 0.0), axis=0, keepdims=True)
        out_ref[count_sums + 4 * n : count_sums + 4 * n + 1] = line

    return pl.pallas_call(
        body,
        in_specs=[smem(), smem()] + vmem(6 + parts),
        out_shape=[
            jax.ShapeDtypeStruct(pack.shape, F),
            jax.ShapeDtypeStruct((low, channels), F),
        ],
        compiler_params=params(),
        name="late_sums",
    )(place, scale, pack, images, own_scale, energy, mixing_sum, mixing, *low_parts)


def style_final(scale, mixing_grad, scale_grad, rgb_grad, tokens, codes, labels, select, style, rgb, classes):
    samples, channels = scale_grad.shape
    depth, kernels = select.shape

    def body(s_ref, mg_ref, sg_ref, rg_ref, t_ref, c_ref, l_ref, sel_ref, sty_ref, rgb_ref, *outs):
        dsel_ref, dsty_ref, drgb_ref, dcodes_ref, table_ref = outs
        by = s_ref[0]
        codes = c_ref[...]
        logits = dot_nn(codes, sel_ref[...])
        e = jnp.exp(logits - jnp.max(logits, axis=1, keepdims=True))
        mixing = e / jnp.sum(e, axis=1, keepdims=True)
        mg = mg_ref[...] * by
        logit = (mixing * (mg - jnp.sum(mixing * mg, axis=1, keepdims=True))).astype(BF)
        sg = (sg_ref[...] * by).astype(BF)
        rg = (rg_ref[...] * by).astype(BF)
        dsel_ref[...] = dot_tn(codes, logit)
        dsty_ref[...] = dot_tn(codes, sg)
        drgb_ref[...] = dot_tn(codes, rg)
        dcodes_ref[...] = (
            dot_nt(logit, sel_ref[...]) + dot_nt(sg, sty_ref[...]) + dot_nt(rg, rgb_ref[...])
        )
        ids = lax.broadcasted_iota(jnp.int32, (samples, classes), 1)
        one_hot = jnp.where(ids == l_ref[...], 1.0, 0.0).astype(BF)
        t = t_ref[...] * by
        high = t.astype(BF)
        rest = (t - high.astype(F)).astype(BF)
        table_ref[...] = dot_tn(one_hot, high) + dot_tn(one_hot, rest)

    return pl.pallas_call(
        body,
        in_specs=[smem()] + vmem(9),
        out_shape=[
            jax.ShapeDtypeStruct((depth, kernels), F),
            jax.ShapeDtypeStruct((depth, channels), F),
            jax.ShapeDtypeStruct((depth, channels), F),
            jax.ShapeDtypeStruct((samples, depth), F),
            jax.ShapeDtypeStruct((classes, channels), F),
        ],
        compiler_params=params(),
        name="style_final",
    )(scale, mixing_grad, scale_grad, rgb_grad, tokens, codes, labels, select, style, rgb)


def local(
    images,
    styles,
    labels,
    noise_map,
    counts,
    cot_features,
    cot_image,
    kernel_bank,
    select_proj,
    style_proj,
    conv_bias,
    noise_gain,
    norm_attn,
    query_proj,
    key_proj,
    value_proj,
    out_proj,
    norm_cross,
    cross_query,
    cross_key,
    cross_value,
    cross_out,
    class_table,
    class_pos,
    norm_mlp,
    up_proj,
    down_proj,
    rgb_style,
    color_projection,
    color_bias,
):
    n, n_dp = lax.axis_size("rows"), lax.axis_size("dp")
    r, d = lax.axis_index("rows"), lax.axis_index("dp")
    side, channels = images.shape[1], images.shape[3]
    low = side * side
    points = 4 * low
    kernels, width = kernel_bank.shape[3], kernel_bank.shape[4]
    tokens = class_pos.shape[0]
    share = query_proj.shape[1]
    band = channels // n_dp
    samples = n * n_dp

    def by_phase(field):
        rest = field.shape[2:]
        split = field.reshape((side, 2, side, 2) + rest)
        order = (1, 3, 0, 2) + tuple(range(4, 4 + len(rest)))
        return split.transpose(order).reshape((points,) + rest)

    group_order = jnp.arange(n, dtype=jnp.int32) ^ r
    slots = jnp.arange(n_dp, dtype=jnp.int32)

    def tie_lists(*lists):
        flat = tie(*[v for part in lists for v in part])
        out = []
        for part in lists:
            out.append(list(flat[: len(part)]))
            flat = flat[len(part) :]
        return out

    def far_swaps(m):
        return [swap(m, "rows", j) for j in range(2, n, 2)]

    def near_swaps(blocks):
        return [swap(b, "rows", 1) for b in blocks]

    def whole(m, far_m, near_m):
        out = [None] * n
        out[::2] = [m] + far_m
        out[1::2] = near_m
        return out

    half = n // 2
    own_images = images[0].reshape(low, channels)
    codes = jnp.take(styles, jnp.arange(max(n, 8), dtype=jnp.int32) % n ^ r, axis=0)
    image_blocks = spread(own_images)
    qkv_proj = jnp.concatenate([query_proj, key_proj, value_proj], axis=1)
    image_blocks, (codes, qkv_proj) = tie_lists(image_blocks, [codes, qkv_proj])
    qkv_far = far_swaps(qkv_proj)
    near = [near_swaps([m])[0] for m in (qkv_proj, out_proj, cross_query, cross_out)]
    conv_part, conv_raw, demod, xs, mixing, scale_in = conv_forward(
        codes, select_proj, style_proj, image_blocks, kernel_bank, side
    )

    later = [styles, labels, counts, cot_features, cot_image, noise_map, conv_bias, noise_gain]
    later += [norm_attn, norm_cross, norm_mlp, class_table, class_pos, cross_key, cross_value]
    later += [rgb_style, color_projection, color_bias, out_proj, cross_query, cross_out, xs]
    (conv_part,), later, qkv_far, near = tie_lists([conv_part], later, qkv_far, near)
    styles, labels, counts, cot_features, cot_image, noise_map, conv_bias, noise_gain = later[:8]
    norm_attn, norm_cross, norm_mlp, class_table, class_pos, cross_key, cross_value = later[8:15]
    rgb_style, color_projection, color_bias, out_proj, cross_query, cross_out, xs = later[15:]

    parts = [conv_part[0]] + [swap(conv_part[j], "rows", j) for j in range(1, n)]
    qkv_near = near[:1] + near_swaps(qkv_far)
    wo_far = far_swaps(out_proj)
    own_live = lax.dynamic_index_in_dim(counts.astype(F), r, 0, keepdims=False)
    color_scale = jnp.dot(codes[:1], rgb_style, preferred_element_type=F) + 1.0
    grad_image = by_phase(cot_image[0].transpose(1, 2, 0)) * own_live
    colors = color_projection.astype(F)
    tinted = jnp.dot(grad_image, colors.T, precision=lax.Precision.HIGHEST)
    grad_four = by_phase(cot_features[0]).astype(F) * own_live + tinted * color_scale
    noise = by_phase(noise_map[0]).astype(F).reshape(points, 1)
    place = r.astype(jnp.int32).reshape(1)
    gains = jnp.stack([noise_gain, conv_bias, norm_attn, norm_cross, norm_mlp]).astype(F)
    parts, qkv_near, wo_far, rest = tie_lists(
        parts, qkv_near, wo_far, [grad_four, noise, gains, xs, styles, labels, class_table]
    )
    grad_four, noise, gains, xs, styles, labels, class_table = rest

    bands = xs.reshape(n * low, n_dp, band).transpose(1, 0, 2)
    label_rows = jnp.stack([labels // 256, labels % 256, counts]).astype(BF)
    codes_flat = jnp.concatenate([styles.reshape(-1), label_rows.reshape(-1)])
    codes_flat = jnp.pad(codes_flat, (0, -codes_flat.shape[0] % (16 * band))).reshape(-1, band)
    sent = jnp.concatenate(
        [bands, jnp.broadcast_to(codes_flat[None], (n_dp,) + codes_flat.shape)], axis=1
    )
    wo_near = near[1:2] + near_swaps(wo_far)
    wqkv = whole(qkv_proj, qkv_far, qkv_near)
    wo = whole(out_proj, wo_far, wo_near)
    conv, two, qkv, attn_own, attn_sent = attn_forward(place, parts, noise, gains, wqkv, wo)
    cq_far, co_far = far_swaps(cross_query), far_swaps(cross_out)
    (two, sent, labels, class_table), cq_far, co_far = tie_lists(
        [two, sent, labels, class_table], cq_far, co_far
    )

    class_rows = jnp.take(class_table, jnp.take(labels, group_order), axis=0)
    context = (class_rows.astype(F)[:, None, :] + class_pos.astype(F)[None]).astype(BF)
    flat_context = context.reshape(n * tokens, channels)
    ckv = jnp.dot(
        flat_context,
        jnp.concatenate([cross_key, cross_value], axis=1),
        preferred_element_type=F,
    ).astype(BF)
    ckv = ckv.reshape(n, tokens, 2 * share)
    ckv = [ckv[0]] + [swap(ckv[j], "rows", j) for j in range(1, n)]
    cq = whole(cross_query, cq_far, near[2:3] + near_swaps(cq_far))
    co = whole(cross_out, co_far, near[3:4] + near_swaps(co_far))
    received = lax.all_to_all(sent, "dp", 0, 0, tiled=True)
    grad_four_low = grad_four.astype(BF)
    three, normed_mlp, xq, cross_own, cross_sent = cross_forward(two, gains, cq, co, ckv)
    grad_far = far_swaps(grad_four_low)
    grad_near = near_swaps([grad_four_low])
    attn_near = near_swaps([attn_sent])
    (three, normed_mlp, received), grad_far, grad_near, attn_near = tie_lists(
        [three, normed_mlp, received], grad_far, grad_near, attn_near
    )

    normed_near = near_swaps([normed_mlp])
    grad_near += near_swaps(grad_far)
    (normed_mlp,), normed_near, grad_near = tie_lists([normed_mlp], normed_near, grad_near)
    grad_pairs = list(zip([grad_four_low] + grad_far, grad_near))
    normed_far = far_swaps(normed_mlp)
    mlp_in = [normed_mlp] + normed_near
    act, inner, *backward = mlp_core(mlp_in, grad_pairs[0], up_proj, down_proj)
    points_low = n * low
    depth = styles.shape[1]
    codes_back = received[:, points_low:].reshape(n_dp, -1)
    styles_all = codes_back[:, : n * depth].reshape(samples, depth)
    label_back = codes_back[:, n * depth : n * depth + 3 * n]
    label_back = label_back.reshape(n_dp, 3, n).astype(jnp.int32)
    inverse = (1.0 / jnp.sum(label_back[:, 2]).astype(F)).reshape(1)
    labels_all = (label_back[:, 0] * 256 + label_back[:, 1]).reshape(samples, 1)
    codes_all = jnp.take(styles_all.reshape(n_dp, n, depth), group_order, axis=1)
    band_proj = lax.dynamic_slice_in_dim(style_proj, d * band, band, axis=1)
    bands_ready = band_prepare(
        place, received, codes_all.reshape(samples, depth), select_proj, band_proj, points_low
    )
    cross_near = near_swaps([cross_sent])
    (act, inner), backward, normed_far, bands_ready, cross_near, ready = tie_lists(
        [act, inner],
        backward,
        normed_far,
        bands_ready,
        cross_near,
        [styles_all, labels_all, inverse],
    )
    at, mixing_all, scale_band = bands_ready
    styles_all, labels_all, inverse = ready
    acts, inners = [act], [inner]
    for i, block in enumerate(normed_far):
        pair = [block] + near_swaps([block])
        act, inner, *back = mlp_core(pair, grad_pairs[i + 1], up_proj, down_proj)
        acts.append(act)
        inners.append(inner)
        mlp_in += pair
        backward += back
    backward, acts, inners = tie_lists(near_sums(backward), acts, inners)
    grad_norm = far_sum(backward)
    grad_group = [g for p in grad_pairs for g in p]
    *forward, d_mlp = mlp_rest(mlp_in, grad_group, inners, acts, down_proj)
    (grad_norm, d_mlp), forward = tie_lists([grad_norm, d_mlp], forward)
    g_mlp = lax.psum_scatter(d_mlp, "dp", scatter_dimension=0, tiled=True)

    back = cross_backward(grad_norm, grad_four, three, two, gains, xq, cq, co, ckv)
    grad_two, d_gains, grads_own, grads_sent = back[:4]
    dkv = list(back[4:])
    forward_near = near_swaps(forward[1::2])
    (grad_two, grads_sent), forward_near = tie_lists([grad_two, grads_sent], forward_near)

    def pair_sums(blocks, near_blocks):
        return [
            (a.astype(F) + b.astype(F)).astype(BF) for a, b in zip(blocks[::2], near_blocks)
        ]

    def far_parts(sums):
        return sums[:1] + [swap(v, "rows", 2 * j) for j, v in enumerate(sums) if j]

    def add_all(blocks):
        total = blocks[0].astype(F)
        for v in blocks[1:]:
            total = total + v.astype(F)
        return total

    branch = far_parts(pair_sums(forward, forward_near))
    grads_near = near_swaps([grads_sent])
    back = attn_backward(place, grad_two, conv, noise, gains, qkv, dkv, wqkv, wo, width)
    late_sums, shares, (qkv_own, qkv_sent) = back[0], list(back[1 : 1 + n]), back[1 + n :]
    (late_sums, qkv_sent), shares, grads_near, branch = tie_lists(
        [late_sums, qkv_sent], shares, grads_near, branch
    )

    shares = [shares[0]] + [swap(shares[j], "rows", j) for j in range(1, n)]
    sent_near = near_swaps([qkv_sent])
    back = cross_weights(
        [attn_own] + attn_near, [cross_own] + cross_near, [grads_own] + grads_near, half, share
    )
    d_cross, d_out = list(back[:half]), list(back[half:])
    shares, d_cross, d_out, sent_near = tie_lists(shares, d_cross, d_out, sent_near)
    grad_taps, gs, grad_energy = tap_sums(shares, demod, conv_raw, side)

    rest, branch, d_cross, d_out, shares = tie_lists(
        [grad_taps, gs, grad_energy, late_sums, d_gains], branch, d_cross, d_out, shares
    )
    grad_taps, gs, grad_energy, late_sums, d_gains = rest
    lines = n_dp // 2
    ring = [grad_taps]
    flipped = []

    def ring_step(*work):
        flipped.append(lax.ppermute(ring[-1], "dp", ring_perm(n_dp, 0, 1)))
        if len(ring) < lines:
            ring.append(lax.ppermute(ring[-1], "dp", ring_perm(n_dp, 1, 0)))
        (ring[-1], flipped[-1]), *work = tie_lists([ring[-1], flipped[-1]], *work)
        return work

    ge_all = jnp.broadcast_to(grad_energy.reshape(1, n, width), (n_dp, n, width))
    ge_all = lax.all_to_all(ge_all, "dp", 0, 0, tiled=True).reshape(samples, 1, width)
    d_cross = far_parts(d_cross)
    back = attn_weights([attn_own] + attn_near, [qkv_own] + sent_near, half, share)
    d_query, d_key, d_value = (list(back[i * half : (i + 1) * half]) for i in range(3))
    (low_part, mixing_conv, ge_all), d_cross, d_query, d_key, d_value, d_out = ring_step(
        [*conv_back(gs, xs, mixing, kernel_bank, n), ge_all],
        d_cross,
        d_query,
        d_key,
        d_value,
        d_out,
    )

    d_out, d_query, d_key = far_parts(d_out), far_parts(d_query), far_parts(d_key)
    cross_side = scatter_side(add_all(d_cross).astype(BF))
    places = jnp.stack([r, d]).astype(jnp.int32)
    low_near = near_sums([low_part[j] for j in range(n)])
    done = bank_energy(places, mixing_all, scale_band, ge_all, kernel_bank, n)
    done, d_out, d_query, d_key, d_value, cross_side, low_near, (g_mlp,) = ring_step(
        list(done), d_out, d_query, d_key, d_value, cross_side, low_near, [g_mlp]
    )
    energy, scale_energy, mixing_energy = done

    count_sums = -(-(tokens + 9 + -(-samples * kernels // channels)) // 8) * 8
    count_all = -(-(count_sums + 4 * n + 1) // 8) * 8
    features, color_image, d_ck_cv, pack = side_outputs(
        place,
        three,
        branch,
        grad_image,
        color_scale,
        colors.T,
        color_bias.astype(F).reshape(3, 1),
        flat_context,
        shares,
        cross_key,
        cross_value,
        d_gains,
        late_sums,
        count_sums,
        count_all,
        side,
    )
    color_image = color_image.reshape(3, 2, 2, side, side).transpose(0, 3, 1, 4, 2)
    color_image = color_image.reshape(1, 3, 2 * side, 2 * side)
    low_parts = far_parts(low_near)

    def as_rows(v):
        v = v.reshape(1, -1)
        v = jnp.pad(v, ((0, 0), (0, -v.shape[1] % channels)))
        return v.reshape(-1, channels)

    pack, grad_images = late_sums_kernel(
        place,
        inverse,
        pack,
        low_parts,
        own_images,
        scale_in[:1],
        scale_energy.reshape(n, channels),
        as_rows(mixing_energy),
        mixing_conv,
        count_sums,
        tokens + 9,
    )
    (grad_images, pack), d_value, cross_side, d_out, d_query, d_key = ring_step(
        [grad_images, pack], d_value, cross_side, d_out, d_query, d_key
    )

    d_value = far_parts(d_value)
    pack = add_over(pack, "rows")
    while len(flipped) < lines:
        ((pack,),) = ring_step([pack])
    blocks = [None] * n_dp
    for t in range(lines):
        for e, v in enumerate((ring[t], flipped[t])):
            blocks[2 * t + e] = v

    sources = ring_source(n_dp, d, slots).astype(jnp.int32)
    cross_parts = scatter_lines(*cross_side)
    query_side = scatter_side(jnp.concatenate([add_all(d_out), add_all(d_query)], axis=1).astype(BF))
    sums, gathered = pack[:count_sums], pack[count_sums:]
    grad_bank = None
    delta = 1
    for tap_row in range(3):
        grad_bank = bank_main(tap_row, grad_bank, sources, inverse, at, blocks, energy, side)
        if delta < n_dp:
            sums, gathered = merge_step(sums, gathered, "dp", d, delta)
            delta *= 2
        if tap_row == 0:
            (grad_bank, sums, gathered), cross_parts, query_side = tie_lists(
                [grad_bank, sums, gathered], cross_parts, query_side
            )
            query_parts = scatter_lines(*query_side)
            keyval = [add_all(d_key), add_all(d_value), d_ck_cv.astype(F)]
            keyval_side = scatter_side(jnp.concatenate(keyval, axis=1).astype(BF))
        else:
            grad_bank, sums, gathered = tie(grad_bank, sums, gathered)
    while delta < n_dp:
        sums, gathered = merge_step(sums, gathered, "dp", d, delta)
        delta *= 2
    keyval_parts = scatter_lines(*keyval_side)
    gathered = gathered.reshape(n_dp, -1, channels)
    scale_grad, bands_grad, token_all, rgb_all = (
        gathered[:, i * n : (i + 1) * n].reshape(samples, channels) for i in range(4)
    )
    bands_grad = bands_grad.reshape(n_dp, samples, band).transpose(1, 0, 2)
    scale_grad = scale_grad + bands_grad.reshape(samples, channels)
    mixing_grad = gathered[:, 4 * n, : n * kernels].reshape(samples, kernels)
    mixing_sum = sums[tokens + 9 :].reshape(-1)[: samples * kernels]
    mixing_grad = mixing_grad + mixing_sum.reshape(samples, kernels)
    sums = sums[: tokens + 9] * inverse
    grad_images = grad_images.reshape(1, side, side, channels)

    d_select, d_style, d_rgb, d_codes, d_table = style_final(
        inverse,
        mixing_grad,
        scale_grad,
        rgb_all,
        token_all,
        styles_all,
        labels_all,
        select_proj,
        style_proj,
        rgb_style,
        class_table.shape[0],
    )
    styles_grad = lax.dynamic_slice_in_dim(d_codes, d * n, n, axis=0)

    cross_grads, query_grads, keyval_grads = tie(
        *(add_all(v) * inverse for v in (cross_parts, query_parts, keyval_parts))
    )
    g_mlp = g_mlp.astype(F) * inverse
    wide = up_proj.shape[1]

    def column(grads, i):
        return grads[:, i * share : (i + 1) * share]

    return (
        features,
        color_image,
        grad_images,
        styles_grad,
        grad_bank,
        d_select,
        d_style,
        sums[tokens + 7],
        sums[tokens + 8],
        sums[tokens + 6],
        column(query_grads, 1),
        column(keyval_grads, 0),
        column(keyval_grads, 1),
        column(query_grads, 0).T,
        sums[tokens + 1],
        column(cross_grads, 0),
        column(keyval_grads, 2),
        column(keyval_grads, 3),
        column(cross_grads, 1).T,
        d_table,
        sums[:tokens],
        sums[tokens],
        g_mlp[:, :wide],
        g_mlp[:, wide:].T,
        d_rgb,
        sums[tokens + 2 : tokens + 5].T,
        sums[tokens + 5, :3],
    )


def solution(mesh):
    whole = P()
    columns = P(None, "rows")
    lines = P("rows", None)
    both = P(("dp", "rows"), None, None, None)
    placed = (
        both,
        P("dp", None),
        P("dp"),
        P(("dp", "rows"), None, None),
        P("dp"),
        both,
        both,
        P(None, None, None, None, "rows"),
        whole,
        whole,
        whole,
        whole,
        whole,
        columns,
        columns,
        columns,
        lines,
        whole,
        columns,
        columns,
        columns,
        lines,
        whole,
        whole,
        whole,
        columns,
        lines,
        whole,
        whole,
        whole,
    )
    given = (
        both,
        both,
        both,
        P("dp", None),
        P(None, None, "dp", None, "rows"),
        whole,
        whole,
        whole,
        whole,
        whole,
        P("dp", "rows"),
        P("dp", "rows"),
        P("dp", "rows"),
        P("rows", "dp"),
        whole,
        P("dp", "rows"),
        P("dp", "rows"),
        P("dp", "rows"),
        P("rows", "dp"),
        whole,
        whole,
        whole,
        P("dp", "rows"),
        P("rows", "dp"),
        whole,
        whole,
        whole,
    )
    return jax.shard_map(local, mesh=mesh, in_specs=placed, out_specs=given, check_vma=False)
```

time: 709 us -> 462 us (0.65)
  waiting for transfers between devices: 192 us -> 75.5 us
  local copies, waits for them, and re-layouts: 138 us -> 50.9 us
  Pallas kernels: 135 us -> 211 us
  other arithmetic: 87.6 us -> 30.6 us
  matrix products: 51.4 us -> 2.95 us
    pallas_call x4 -> x17, Pallas kernels: 82 us -> 157 us  [the longest x3 28.2 us: bank_main(): pl.pallas_call(body, grid=(3,), in_specs=[smem(), smem(), pl.BlockSpec((b...]
    ppermute x73 -> x53, waiting for transfers between devices: 119 us -> 63.9 us  [swap(): return lax.ppermute(x, axis, [(i, i ^ delta) for i in range(n)])]
    unnamed x283 -> x150, local copies, waits for them, and re-layouts: 63.4 us -> 13.3 us
    dot_general x41 -> x0, matrix products: 49.1 us -> none  [the longest x12 15.6 us: dot_tn(): lax.dot_general(a, b, (((0,), (0,)), ((), ())), preferred_element_type=F)]
    ppermute x21 -> x19, waiting for transfers between devices: 50.8 us -> 11.6 us  [the longest x4 9.52 us: ring_step(): flipped.append(lax.ppermute(ring[-1], 'dp', ring_perm(n_dp, 0, 1)))]
    reduce_scatter x1, waiting for transfers between devices: 22.5 us -> 0.01 us  [local(): g_mlp = lax.psum_scatter(d_mlp, 'dp', scatter_dimension=0, tiled=True)]
    convert_element_type x20 -> x12, other arithmetic: 28.5 us -> 7.84 us  [the longest x3 2.15 us: near_sums(): out.append(near.astype(BF))]
    ppermute x73 -> x53, starting transfers between devices: 51.4 us -> 32.8 us  [swap(): return lax.ppermute(x, axis, [(i, i ^ delta) for i in range(n)])]
  transfers between devices with their start and end apart: 97 -> 75, of which waited for: 35 -> 18; matrix products, arithmetic and copies ran while one was open for 35% -> 15% of each run, Pallas kernels for 17% -> 46%
where the time goes in v2:
time: 462 us; the launch traced here: 457 us
  Pallas kernels  211 us (46%)
  waiting for transfers between devices  75.5 us (16%)
  starting transfers between devices  68.7 us (15%)
  local copies, waits for them, and re-layouts  50.9 us (11%)
  other arithmetic  30.6 us (7%)
  between operations  16.4 us (4%)
    ppermute x53, waiting for transfers between devices, swap(): return lax.ppermute(x, axis, [(i, i ^ delta) for i in range(n)])  63.9 us
    ppermute x53, starting transfers between devices, swap(): return lax.ppermute(x, axis, [(i, i ^ delta) for i in range(n)])  32.8 us
    pallas_call x3, Pallas kernels, bank_main(): pl.pallas_call(body, grid=(3,), in_specs=[smem(), smem(), pl.BlockSpec((b...  28.2 us
    pallas_call x1, Pallas kernels, conv_forward(): pl.pallas_call(body, grid=(steps,), in_specs=[pl.BlockSpec((pad, depth),...  24.1 us
    pallas_call x1, Pallas kernels, conv_back(): pl.pallas_call(body, grid=(steps,), in_specs=[pl.BlockSpec((9, rows, widt...  20.9 us
    pallas_call x1, Pallas kernels, bank_energy(): pl.pallas_call(body, grid_spec=pltpu.PrefetchScalarGridSpec(num_scalar_pr...  20.5 us
    pallas_call x1, Pallas kernels, attn_backward(): pl.pallas_call(body, out_shape=[jax.ShapeDtypeStruct((3, channels), F)] +...  18.3 us
    pallas_call x2, Pallas kernels, mlp_core(): pl.pallas_call(body, grid=(steps,), in_specs=[block] * (2 * count) + [pl....  16.6 us
  transfers between devices with their start and end apart: 75, of which 18 were waited for; matrix products, arithmetic and copies ran while one was open for 15% of the time, Pallas kernels for 46%

profile of v2, /device:TPU:0, one launch (start us, length us, event | category | flops | bytes accessed | tf_op | source)
XLA Modules:
  0.0 456.5 jit_solution(1866349980601442326)
XLA Ops:
  7.2 3.0 collective-permute-start.1
  18.2 24.1 %conv_forward.1 = (bf16[4,256,256]{2,1,0:T(8,128)(2,1)}, bf16[4,256,256]{2,1,0:T(8,128)(2,1)}, f32[4,1,256]{2,1,0:T(1,128)}, bf16[256,1024]{1,0:T(8,128)(2,1)}, f32[8,8]{1,0:T(8,128)}, /*index=5*/f32[8,1024]{1,0:T(8,128)}) custom-call(bf16[8,512]{1,0:T(8,128)(2,1)} %broadcast_select_fusion.1.c_ref, bf16[512,8]{1,0:T(8,128)(2,1)} %copy.109.sel_ref, ...), custom_call_target="tpu_custom_call" | custom-call | flops 14495514624 | bytes 37748736 | tf_op jit(solution)/shard_map/conv_forward/pallas_call | solution.py:287
  42.4 10.9 %collective-permute-done.3.rest_6_.rest_2_ = bf16[1024,768]{1,0:T(8,128)(2,1)} collective-permute-done((bf16[1024,768]{1,0:T(8,128)(2,1)S(1)}, bf16[1024,768]{1,0:T(8,128)(2,1)}, u32[]{:S(2)}, u32[]{:S(2)}) %collective-permute-start.3) | collective-permute-done | bytes 1572896 | tf_op jit(solution)/shard_map/ppermute | solution.py:37
  55.4 1.9 slice_bitcast_fusion.5
  68.8 2.0 collective-permute-done.10.rest_3_
  74.9 2.0 copy.114
  76.9 2.0 copy.115
  79.8 1.9 pad_maximum_fusion.2
  81.7 12.9 %attn_forward.1 = (bf16[256,1024]{1,0:T(8,128)(2,1)}, f32[256,1024]{1,0:T(8,128)}, bf16[4,256,768]{2,1,0:T(8,128)(2,1)}, bf16[256,1536]{1,0:T(8,128)(2,1)}, bf16[256,1536]{1,0:T(8,128)(2,1)}) custom-call(s32[1]{0:T(128)} %bitcast.place_ref, f32[256,1]{1,0:T(8,128)} %copy.113.noise_ref, f32[5,1024]{1,0:T(8,128)} %convert_element_type.259.gains_ref.in_ref, ...), custom_call_target="tpu_custom_call" | custom-call | flops 2684354560 | bytes 16777216 | tf_op jit(solution)/shard_map/attn_forward/pallas_call | solution.py:669
  94.5 2.4 collective-permute-done.15.rest_6_
  98.3 5.8 %all-to-all-start = ((bf16[8,288,128]{2,1,0:T(8,128)(2,1)}), bf16[8,288,128]{2,1,0:T(8,128)(2,1)}, u32[]{:S(2)}, u32[]{:S(2)}) async-start(bf16[8,288,128]{2,1,0:T(8,128)(2,1)} %pad_maximum_fusion.2), calls=%async_computation | async-start | bytes 1179648 | tf_op jit(solution)/shard_map/all_to_all | solution.py:1376
  109.5 1.9 collective-permute-done.19.rest_10_
  113.0 10.7 %cross_forward.1 = (f32[256,1024]{1,0:T(8,128)}, bf16[256,1024]{1,0:T(8,128)(2,1)}, bf16[4,256,256]{2,1,0:T(8,128)(2,1)}, bf16[256,1536]{1,0:T(8,128)(2,1)}, bf16[256,1536]{1,0:T(8,128)(2,1)}) custom-call(f32[256,1024]{1,0:T(8,128)} %get-tuple-element.340.two_ref, f32[5,1024]{1,0:T(8,128)} %convert_element_type.259.gains_ref.in_ref, ...), custom_call_target="tpu_custom_call" | custom-call | flops 1342177280 | bytes 8388608 | tf_op jit(solution)/shard_map/cross_forward/pallas_call | solution.py:713
  132.5 5.0 %band_prepare.1 = (bf16[1024,2048]{1,0:T(8,128)(2,1)}, f32[32,8]{1,0:T(8,128)}, f32[32,128]{1,0:T(8,128)}) custom-call(s32[1]{0:T(128)} %bitcast.place_ref, bf16[8,288,128]{2,1,0:T(8,128)(2,1)} %all-to-all-done.x_ref, bf16[32,512]{1,0:T(8,128)(2,1)} %broadcast_select_fusion.c_ref, bf16[512,8]{1,0:T(8,128)(2,1)} %copy.109.sel_ref, ...), custom_call_target="tpu_custom_call" | custom-call | tf_op jit(solution)/shard_map/band_prepare/pallas_call | solution.py:1070
  137.6 8.3 %mlp_core.2 = (bf16[512,1024]{1,0:T(8,128)(2,1)}, bf16[512,1024]{1,0:T(8,128)(2,1)}, bf16[256,1024]{1,0:T(8,128)(2,1)}, bf16[256,1024]{1,0:T(8,128)(2,1)}) custom-call(bf16[256,1024]{1,0:T(8,128)(2,1)} %get-tuple-element.362.refs_0_.rest_0_, bf16[256,1024]{1,0:T(8,128)(2,1)} %copy-done.60, bf16[256,1024]{1,0:T(8,128)(2,1)} %copy-done.25, ...), custom_call_target="tpu_custom_call" | custom-call | flops 3221225472 | bytes 4194304 | tf_op jit(solution)/shard_map/mlp_core/pallas_call | solution.py:766
  149.7 8.4 %mlp_core.3 = (bf16[512,1024]{1,0:T(8,128)(2,1)}, bf16[512,1024]{1,0:T(8,128)(2,1)}, bf16[256,1024]{1,0:T(8,128)(2,1)}, bf16[256,1024]{1,0:T(8,128)(2,1)}) custom-call(bf16[256,1024]{1,0:T(8,128)(2,1)} %collective-permute-done.26.refs_0_.rest_2_, bf16[256,1024]{1,0:T(8,128)(2,1)} %copy-done.64, bf16[256,1024]{1,0:T(8,128)(2,1)} %copy-done.58, ...), custom_call_target="tpu_custom_call" | custom-call | flops 3221225472 | bytes 4194304 | tf_op jit(solution)/shard_map/mlp_core/pallas_call | solution.py:766
  158.5 1.8 collective-permute-done.30
  162.7 12.7 %mlp_rest.1 = (bf16[256,1024]{1,0:T(8,128)(2,1)}, bf16[256,1024]{1,0:T(8,128)(2,1)}, bf16[256,1024]{1,0:T(8,128)(2,1)}, bf16[256,1024]{1,0:T(8,128)(2,1)}, bf16[1024,2048]{1,0:T(8,128)(2,1)}) custom-call(bf16[1024,1024]{1,0:T(8,128)(2,1)} %down_ref.1, bf16[256,1024]{1,0:T(8,128)(2,1)} %get-tuple-element.362.refs_0_.rest_0_, bf16[256,1024]{1,0:T(8,128)(2,1)} %copy-done.60, ...), custom_call_target="tpu_custom_call" | custom-call | flops 6442450944 | bytes 16777216 | tf_op jit(solution)/shard_map/mlp_rest/pallas_call | solution.py:821
  178.3 13.3 %cross_backward.1 = (f32[256,1024]{1,0:T(8,128)}, f32[2,1024]{1,0:T(2,128)}, bf16[256,2560]{1,0:T(8,128)(2,1)}, bf16[256,2560]{1,0:T(8,128)(2,1)}, bf16[16,512]{...) custom-call(f32[256,1024]{1,0:T(8,128)} %convert_add_fusion.1.gn_ref, ...), custom_call_target="tpu_custom_call" | custom-call | flops 2147483648 | bytes 12582912 | tf_op jit(solution)/shard_map/cross_backward/pallas_call | solution.py:879
  194.2 18.3 %attn_backward.1 = (f32[3,1024]{1,0:T(4,128)}, bf16[288,256]{1,0:T(8,128)(2,1)}, bf16[288,256]{1,0:T(8,128)(2,1)}, bf16[288,256]{1,0:T(8,128)(2,1)}, bf16[288,25...) custom-call(s32[1]{0:T(128)} %bitcast.place_ref, f32[256,1024]{1,0:T(8,128)} %get-tuple-element.401.g2_ref, ...), custom_call_target="tpu_custom_call" | custom-call | flops 6442450944 | bytes 25165824 | tf_op jit(solution)/shard_map/attn_backward/pallas_call | solution.py:946
  217.2 5.7 %cross_weights.1 = (bf16[1024,512]{1,0:T(8,128)(2,1)}, bf16[1024,512]{1,0:T(8,128)(2,1)}, bf16[1024,256]{1,0:T(8,128)(2,1)}, bf16[1024,256]{1,0:T(8,128)(2,1)}) custom-call(bf16[256,1536]{1,0:T(8,128)(2,1)} %get-tuple-element.423.refs_0_, bf16[256,1536]{1,0:T(8,128)(2,1)} %collective-permute-done.23.refs_1_, bf16[256,1536]{1,0:T(8,128)(2,1)} %get-tuple-element.425.refs_2_, ...), custom_call_target="tpu_custom_call" | custom-call | flops 1610612736 | bytes 5242880 | tf_op jit(solution)/shard_map/cross_weights/pallas_call | solution.py:1001
  224.9 2.7 tap_sums.1
  227.7 2.0 collective-permute-start.40
  233.4 3.7 all-to-all-start.1
  237.1 20.9 %conv_back.1 = (bf16[4,64,1024]{2,1,0:T(8,128)(2,1)}, f32[4,8]{1,0:T(4,128)}) custom-call(bf16[9,256,256]{2,1,0:T(8,128)(2,1)} %get-tuple-element.460.g_ref, bf16[256,1024]{1,0:T(8,128)(2,1)} %get-tuple-element.334.x_ref, f32[8,8]{1,0:T(8,128)} %get-tuple-element.461.m_ref, bf16[3,3,1024,8,256]{4,3,2,1,0:T(8,128)(2,1)} %b_ref.3), custom_call_target="tpu_custom_call" | custom-call | flops 9663676416 | bytes 37748736 | tf_op jit(solution)/shard_map/conv_back/pallas_call | solution.py:369
  258.0 4.9 %attn_weights.1 = (bf16[1024,256]{1,0:T(8,128)(2,1)}, bf16[1024,256]{1,0:T(8,128)(2,1)}, bf16[1024,256]{1,0:T(8,128)(2,1)}, bf16[1024,256]{1,0:T(8,128)(2,1)}, b...) custom-call(bf16[256,1536]{1,0:T(8,128)(2,1)} %get-tuple-element.423.refs_0_, ...), custom_call_target="tpu_custom_call" | custom-call | flops 1610612736 | bytes 4194304 | tf_op jit(solution)/shard_map/attn_weights/pallas_call | solution.py:1029
  263.7 1.9 add_convert_fusion
  266.5 2.0 collective-permute-start.48
  271.1 6.2 %side_outputs.1 = (f32[1,16,16,1024]{3,2,1,0:T(8,128)}, f32[3,256]{1,0:T(4,128)}, bf16[1024,512]{1,0:T(8,128)(2,1)}, f32[56,1024]{1,0:T(8,128)}) custom-call(s32[1]{0:T(128)} %bitcast.place_ref, f32[256,1024]{1,0:T(8,128)} %get-tuple-element.355.three_ref, f32[256,3]{1,0:T(8,128)} %bitcast.183, f32[1,1024]{1,0:T(1,128)} %bitcast.199, ...), custom_call_target="tpu_custom_call" | custom-call | tf_op jit(solution)/shard_map/side_outputs/pallas_call | solution.py:1141
  284.2 20.5 %bank_energy.1 = (bf16[3,3,128,8,256]{4,3,2,1,0:T(8,128)(2,1)}, f32[32,128]{1,0:T(8,128)}, f32[32,8]{1,0:T(8,128)}) custom-call(s32[2]{0:T(128)} %pad_add_fusion.place_ref, f32[32,8]{1,0:T(8,128)} %get-tuple-element.478.m_ref, f32[32,128]{1,0:T(8,128)} %get-tuple-element.479.s_ref, f32[32,1,256]{2,1,0:T(1,128)} %reshape.342.g_ref, ...), custom_call_target="tpu_custom_call" | custom-call | flops 14495514624 | bytes 9437184 | tf_op jit(solution)/shard_map/bank_energy/pallas_call | solution.py:452
  305.4 2.2 collective-permute-done.46
  307.6 9.7 %collective-permute-done.47 = bf16[1024,256]{1,0:T(8,128)(2,1)} collective-permute-done((bf16[1024,256]{1,0:T(8,128)(2,1)}, bf16[1024,256]{1,0:T(8,128)(2,1)}, u32[]{:S(2)}, u32[]{:S(2)}) %collective-permute-start.47) | collective-permute-done | bytes 524320 | tf_op jit(solution)/shard_map/ppermute | solution.py:37
  317.3 1.7 collective-permute-start.51
  324.4 2.0 copy.135
  327.7 2.1 late_sums.1
  329.7 2.0 collective-permute-done.51.rest_6_
  343.0 5.5 %collective-permute-done.56 = f32[56,1024]{1,0:T(8,128)S(1)} collective-permute-done((f32[56,1024]{1,0:T(8,128)S(1)}, f32[56,1024]{1,0:T(8,128)S(1)}, u32[]{:S(2)}, u32[]{:S(2)}) %collective-permute-start.56) | collective-permute-done | bytes 229408 | tf_op jit(solution)/shard_map/ppermute | solution.py:37
  349.6 9.5 %collective-permute-done.54.rest_7_ = bf16[4,256,256]{2,1,0:T(8,128)(2,1)S(1)} collective-permute-done((bf16[4,256,256]{2,1,0:T(8,128)(2,1)S(1)}, bf16[4,256,256]{2,1,0:T(8,128)(2,1)S(1)}, u32[]{:S(2)}, u32[]{:S(2)}) %collective-permute-start.54) | collective-permute-done | bytes 524320 | tf_op jit(solution)/shard_map/ppermute | solution.py:1478
  360.5 9.4 %bank_main.3.rest_9_ = f32[3,3,128,8,256]{4,3,2,1,0:T(8,128)} custom-call(s32[8]{0:T(128)} %fusion.25.src_ref, f32[1]{0:T(128)} %bitcast.31.scale_ref.s_ref, bf16[1024,2048]{1,0:T(8,128)(2,1)} %get-tuple-element.518.a_ref, bf16[4,256,256]{2,1,0:T(8,128)(2,1)} %get-tuple-element.459.rest_0_, bf16[4,256,256]{2,1,0:T(8,128)(2,1)} %copy-done.5, ...), custom_call_target="tpu_custom_call" | custom-call | flops 3221225472 | bytes 7864320 | tf_op jit(solution)/shard_map/bank_main/pallas_call | solution.py:536
  372.0 6.5 %collective-permute-done.57 = f32[56,1024]{1,0:T(8,128)S(1)} collective-permute-done((f32[56,1024]{1,0:T(8,128)S(1)}, f32[56,1024]{1,0:T(8,128)S(1)}, u32[]{:S(2)}, u32[]{:S(2)}) %collective-permute-start.57) | collective-permute-done | bytes 229408 | tf_op jit(solution)/shard_map/ppermute | solution.py:37
  381.5 2.6 collective-permute-start.66
  384.8 9.4 %bank_main.4.rest_9_ = f32[3,3,128,8,256]{4,3,2,1,0:T(8,128)} custom-call(s32[8]{0:T(128)} %fusion.25.src_ref, f32[1]{0:T(128)} %bitcast.31.scale_ref.s_ref, bf16[1024,2048]{1,0:T(8,128)(2,1)} %get-tuple-element.518.a_ref, bf16[4,256,256]{2,1,0:T(8,128)(2,1)} %get-tuple-element.459.rest_0_, ...), custom_call_target="tpu_custom_call", output_to_operand_aliasing={{}: (12, {})} | custom-call | flops 3221225472 | bytes 7864320 | tf_op jit(solution)/shard_map/bank_main/pallas_call | solution.py:536
  396.8 9.4 %bank_main.5 = f32[3,3,128,8,256]{4,3,2,1,0:T(8,128)} custom-call(s32[8]{0:T(128)} %fusion.25.src_ref, f32[1]{0:T(128)} %bitcast.31.scale_ref.s_ref, bf16[1024,2048]{1,0:T(8,128)(2,1)} %get-tuple-element.518.a_ref, bf16[4,256,256]{2,1,0:T(8,128)(2,1)} %get-tuple-element.459.rest_0_, bf16[4,256,256]{2,1,0:T(8,128)(2,1)} %copy-done.5, ...), custom_call_target="tpu_custom_call", output_to_operand_aliasing={{}: (12, {})} | custom-call | flops 3221225472 | bytes 7864320 | tf_op jit(solution)/shard_map/bank_main/pallas_call | solution.py:536
  407.5 2.0 collective-permute-start.69
  410.4 1.8 collective-permute-start.71
  412.1 15.9 %collective-permute-done.63 = f32[128,1024]{1,0:T(8,128)S(1)} collective-permute-done((f32[128,1024]{1,0:T(8,128)S(1)}, f32[128,1024]{1,0:T(8,128)S(1)}, u32[]{:S(2)}, u32[]{:S(2)}) %collective-permute-start.63) | collective-permute-done | bytes 524320 | tf_op jit(solution)/shard_map/ppermute | solution.py:37
  432.7 6.6 %style_final.1 = (f32[512,8]{1,0:T(8,128)}, f32[512,1024]{1,0:T(8,128)}, f32[512,1024]{1,0:T(8,128)}, f32[32,512]{1,0:T(8,128)}, f32[1000,1024]{1,0:T(8,128)}) custom-call(f32[1]{0:T(128)} %bitcast.31.scale_ref.s_ref, f32[32,8]{1,0:T(8,128)} %slice_add_fusion.3.mg_ref, f32[32,1024]{1,0:T(8,128)} %bitcast_add_fusion.sg_ref, f32[32,1024]{1,0:T(8,128)} %reshape.350.rg_ref, ...), custom_call_target="tpu_custom_call" | custom-call | tf_op jit(solution)/shard_map/style_final/pallas_call | solution.py:1224
  441.2 1.7 copy.132
  (415 shorter events, 120.6 us)
Async XLA Ops:
  10.3 32.1 %collective-permute-start.5 = (bf16[256,1024]{1,0:T(8,128)(2,1)}, bf16[256,1024]{1,0:T(8,128)(2,1)}, u32[]{:S(2)}, u32[]{:S(2)}) collective-permute-start(bf16[256,1024]{1,0:T(8,128)(2,1)} %rest_4_.4), channel_id=1, source_target_pairs={{0,1},{1,0},{2,3},{3,2},{4,5},{5,4},{6,7},{7,6},{8,9},{9,8},{10,11... | collective-permute-start | bytes 1572872 | tf_op jit(solution)/shard_map/ppermute | solution.py:37
  10.8 31.6 %collective-permute-start.6 = (bf16[1024,256]{1,0:T(8,128)(2,1)}, bf16[1024,256]{1,0:T(8,128)(2,1)S(1)}, u32[]{:S(2)}, u32[]{:S(2)}) collective-permute-start(bf16[1024,256]{1,0:T(8,128)(2,1)} %rest_0_.1), channel_id=1, source_target_pairs={{0,1},{1,0},{2,3},{3,2},{4,5},{5,4},{6,7},{7,6},{8,9},{9,8},{10,11... | collective-permute-start | bytes 1572872 | tf_op jit(solution)/shard_map/ppermute | solution.py:37
  10.8 31.6 %collective-permute-start.7 = (bf16[256,1024]{1,0:T(8,128)(2,1)}, bf16[256,1024]{1,0:T(8,128)(2,1)S(1)}, u32[]{:S(2)}, u32[]{:S(2)}) collective-permute-start(bf16[256,1024]{1,0:T(8,128)(2,1)} %rest_4_.3), channel_id=1, source_target_pairs={{0,1},{1,0},{2,3},{3,2},{4,5},{5,4},{6,7},{7,6},{8,9},{9,8},{10,11... | collective-permute-start | bytes 1572872 | tf_op jit(solution)/shard_map/ppermute | solution.py:37
  16.3 36.9 %collective-permute-start.3 = (bf16[1024,768]{1,0:T(8,128)(2,1)S(1)}, bf16[1024,768]{1,0:T(8,128)(2,1)}, u32[]{:S(2)}, u32[]{:S(2)}) collective-permute-start(bf16[1024,768]{1,0:T(8,128)(2,1)S(1)} %pad_maximum_fusion.1.rest_4_.rest_0_), channel_id=1, source_target_pairs={{0,2},{1,3},{2,0},{3,1},{4,6},{5,7},{6,4},{7,5},{8,10},{9,11},{10,... | collective-permute-start | bytes 4718600 | tf_op jit(solution)/shard_map/ppermute | solution.py:37
  17.3 35.9 %collective-permute-start.4 = (bf16[1024,768]{1,0:T(8,128)(2,1)S(1)}, bf16[1024,768]{1,0:T(8,128)(2,1)S(1)}, u32[]{:S(2)}, u32[]{:S(2)}) collective-permute-start(bf16[1024,768]{1,0:T(8,128)(2,1)S(1)} %pad_maximum_fusion.1.rest_4_.rest_0_), channel_id=1, source_target_pairs={{0,1},{1,0},{2,3},{3,2},{4,5},{5,4},{6,7},{7,6},{8,9},{9,8},{10,11... | collective-permute-start | bytes 4718600 | tf_op jit(solution)/shard_map/ppermute | solution.py:37
  53.3 20.8 %collective-permute-start.11 = (bf16[1024,768]{1,0:T(8,128)(2,1)}, bf16[1024,768]{1,0:T(8,128)(2,1)}, u32[]{:S(2)}, u32[]{:S(2)}) collective-permute-start(bf16[1024,768]{1,0:T(8,128)(2,1)} %collective-permute-done.3.rest_6_.rest_2_), channel_id=1, source_target_pairs={{0,1},{1,0},{2,3},{3,2},{4,5},{5,4},{6,7},{7,6},{8,9},{9,8},{10,11... | collective-permute-start | bytes 4718600 | tf_op jit(solution)/shard_map/ppermute | solution.py:37
  53.8 20.2 %collective-permute-start.12 = (bf16[256,1024]{1,0:T(8,128)(2,1)}, bf16[256,1024]{1,0:T(8,128)(2,1)}, u32[]{:S(2)}, u32[]{:S(2)}) collective-permute-start(bf16[256,1024]{1,0:T(8,128)(2,1)} %rest_4_.4), channel_id=1, source_target_pairs={{0,2},{1,3},{2,0},{3,1},{4,6},{5,7},{6,4},{7,5},{8,10},{9,11},{10,... | collective-permute-start | bytes 1572872 | tf_op jit(solution)/shard_map/ppermute | solution.py:37
  70.8 23.7 %collective-permute-start.14 = (bf16[1024,256]{1,0:T(8,128)(2,1)}, bf16[1024,256]{1,0:T(8,128)(2,1)}, u32[]{:S(2)}, u32[]{:S(2)}) collective-permute-start(bf16[1024,256]{1,0:T(8,128)(2,1)} %rest_0_.1), channel_id=1, source_target_pairs={{0,2},{1,3},{2,0},{3,1},{4,6},{5,7},{6,4},{7,5},{8,10},{9,11},{10,... | collective-permute-start | bytes 1572872 | tf_op jit(solution)/shard_map/ppermute | solution.py:37
  71.7 25.1 %collective-permute-start.15 = (bf16[256,1024]{1,0:T(8,128)(2,1)}, bf16[256,1024]{1,0:T(8,128)(2,1)}, u32[]{:S(2)}, u32[]{:S(2)}) collective-permute-start(bf16[256,1024]{1,0:T(8,128)(2,1)} %rest_4_.3), channel_id=1, source_target_pairs={{0,2},{1,3},{2,0},{3,1},{4,6},{5,7},{6,4},{7,5},{8,10},{9,11},{10,... | collective-permute-start | bytes 1572872 | tf_op jit(solution)/shard_map/ppermute | solution.py:37
  97.7 14.8 %collective-permute-start.16 = (bf16[1024,256]{1,0:T(8,128)(2,1)}, bf16[1024,256]{1,0:T(8,128)(2,1)}, u32[]{:S(2)}, u32[]{:S(2)}) collective-permute-start(bf16[1024,256]{1,0:T(8,128)(2,1)} %collective-permute-done.14.rest_2_), channel_id=1, source_target_pairs={{0,1},{1,0},{2,3},{3,2},{4,5},{5,4},{6,7},{7,6},{8,9},{9,8},{10,11... | collective-permute-start | bytes 1572872 | tf_op jit(solution)/shard_map/ppermute | solution.py:37
  97.8 14.7 %collective-permute-start.17 = (bf16[256,1024]{1,0:T(8,128)(2,1)}, bf16[256,1024]{1,0:T(8,128)(2,1)}, u32[]{:S(2)}, u32[]{:S(2)}) collective-permute-start(bf16[256,1024]{1,0:T(8,128)(2,1)} %collective-permute-done.15.rest_6_), channel_id=1, source_target_pairs={{0,1},{1,0},{2,3},{3,2},{4,5},{5,4},{6,7},{7,6},{8,9},{9,8},{10,11... | collective-permute-start | bytes 1572872 | tf_op jit(solution)/shard_map/ppermute | solution.py:37
  98.3 26.3 %all-to-all-start = ((bf16[8,288,128]{2,1,0:T(8,128)(2,1)}), bf16[8,288,128]{2,1,0:T(8,128)(2,1)}, u32[]{:S(2)}, u32[]{:S(2)}) async-start(bf16[8,288,128]{2,1,0:T(8,128)(2,1)} %pad_maximum_fusion.2), calls=%async_computation | async-start | bytes 1179648 | tf_op jit(solution)/shard_map/all_to_all | solution.py:1376
  104.1 213.3 %reduce-scatter.2.cloned.1.call-start = ((), (), s32[]{:S(2)}) async-start(), calls=%async_computation.3 | async-start | bytes 4718592 | tf_op jit(solution)/shard_map/reduce_scatter | solution.py:1430
  104.3 20.3 %collective-permute-start.23 = (bf16[256,1536]{1,0:T(8,128)(2,1)}, bf16[256,1536]{1,0:T(8,128)(2,1)}, u32[]{:S(2)}, u32[]{:S(2)}) collective-permute-start(bf16[256,1536]{1,0:T(8,128)(2,1)} %get-tuple-element.354), channel_id=1, source_target_pairs={{0,1},{1,0},{2,3},{3,2},{4,5},{5,4},{6,7},{7,6},{8,9},{9,8},{10,11... | collective-permute-start | bytes 2359304 | tf_op jit(solution)/shard_map/ppermute | solution.py:37
  111.5 13.1 %collective-permute-start.21 = (bf16[256,1024]{1,0:T(8,128)(2,1)S(1)}, bf16[256,1024]{1,0:T(8,128)(2,1)S(1)}, u32[]{:S(2)}, u32[]{:S(2)}) collective-permute-start(bf16[256,1024]{1,0:T(8,128)(2,1)S(1)} %convert_element_type.266.refs_2_.rest_4_), channel_id=1, source_target_pairs={{0,2},{1,3},{2,0},{3,1},{4,6},{5,7},{6,4},{7,5},{8,10},{9,11},{10,... | collective-permute-start | bytes 1572872 | tf_op jit(solution)/shard_map/ppermute | solution.py:37
  126.8 19.1 %collective-permute-start.27 = (bf16[256,1536]{1,0:T(8,128)(2,1)}, bf16[256,1536]{1,0:T(8,128)(2,1)S(1)}, u32[]{:S(2)}, u32[]{:S(2)}) collective-permute-start(bf16[256,1536]{1,0:T(8,128)(2,1)} %get-tuple-element.373), channel_id=1, source_target_pairs={{0,1},{1,0},{2,3},{3,2},{4,5},{5,4},{6,7},{7,6},{8,9},{9,8},{10,11... | collective-permute-start | bytes 2359304 | tf_op jit(solution)/shard_map/ppermute | solution.py:37
  130.8 15.1 %collective-permute-start.26 = (bf16[256,1024]{1,0:T(8,128)(2,1)}, bf16[256,1024]{1,0:T(8,128)(2,1)}, u32[]{:S(2)}, u32[]{:S(2)}) collective-permute-start(bf16[256,1024]{1,0:T(8,128)(2,1)} %get-tuple-element.362.refs_0_.rest_0_), channel_id=1, source_target_pairs={{0,2},{1,3},{2,0},{3,1},{4,6},{5,7},{6,4},{7,5},{8,10},{9,11},{10,... | collective-permute-start | bytes 1572872 | tf_op jit(solution)/shard_map/ppermute | solution.py:37
  161.5 14.1 %collective-permute-start.31 = (bf16[256,1024]{1,0:T(8,128)(2,1)S(1)}, bf16[256,1024]{1,0:T(8,128)(2,1)S(1)}, u32[]{:S(2)}, u32[]{:S(2)}) collective-permute-start(bf16[256,1024]{1,0:T(8,128)(2,1)S(1)} %add_convert_fusion.9), channel_id=1, source_target_pairs={{0,2},{1,3},{2,0},{3,1},{4,6},{5,7},{6,4},{7,5},{8,10},{9,11},{10,... | collective-permute-start | bytes 1572872 | tf_op jit(solution)/shard_map/ppermute | solution.py:37
  177.7 13.8 %collective-permute-start.32 = (bf16[256,1024]{1,0:T(8,128)(2,1)S(1)}, bf16[256,1024]{1,0:T(8,128)(2,1)S(1)}, u32[]{:S(2)}, u32[]{:S(2)}) collective-permute-start(bf16[256,1024]{1,0:T(8,128)(2,1)S(1)} %copy-done.63), channel_id=1, source_target_pairs={{0,1},{1,0},{2,3},{3,2},{4,5},{5,4},{6,7},{7,6},{8,9},{9,8},{10,11... | collective-permute-start | bytes 1572872 | tf_op jit(solution)/shard_map/ppermute | solution.py:37
  177.9 13.7 %collective-permute-start.33 = (bf16[256,1024]{1,0:T(8,128)(2,1)S(1)}, bf16[256,1024]{1,0:T(8,128)(2,1)S(1)}, u32[]{:S(2)}, u32[]{:S(2)}) collective-permute-start(bf16[256,1024]{1,0:T(8,128)(2,1)S(1)} %copy-done.62), channel_id=1, source_target_pairs={{0,1},{1,0},{2,3},{3,2},{4,5},{5,4},{6,7},{7,6},{8,9},{9,8},{10,11... | collective-permute-start | bytes 1572872 | tf_op jit(solution)/shard_map/ppermute | solution.py:37
  191.6 20.9 %collective-permute-start.34 = (bf16[256,2560]{1,0:T(8,128)(2,1)}, bf16[256,2560]{1,0:T(8,128)(2,1)S(1)}, u32[]{:S(2)}, u32[]{:S(2)}) collective-permute-start(bf16[256,2560]{1,0:T(8,128)(2,1)} %get-tuple-element.414), channel_id=1, source_target_pairs={{0,1},{1,0},{2,3},{3,2},{4,5},{5,4},{6,7},{7,6},{8,9},{9,8},{10,11... | collective-permute-start | bytes 3932168 | tf_op jit(solution)/shard_map/ppermute | solution.py:37
  192.0 20.5 %collective-permute-start.35 = (bf16[256,1024]{1,0:T(8,128)(2,1)S(1)}, bf16[256,1024]{1,0:T(8,128)(2,1)S(1)}, u32[]{:S(2)}, u32[]{:S(2)}) collective-permute-start(bf16[256,1024]{1,0:T(8,128)(2,1)S(1)} %add_convert_fusion.7), channel_id=1, source_target_pairs={{0,2},{1,3},{2,0},{3,1},{4,6},{5,7},{6,4},{7,5},{8,10},{9,11},{10,... | collective-permute-start | bytes 1572872 | tf_op jit(solution)/shard_map/ppermute | solution.py:37
  227.7 35.9 %collective-permute-start.40 = (bf16[4,256,256]{2,1,0:T(8,128)(2,1)}, bf16[4,256,256]{2,1,0:T(8,128)(2,1)S(1)}, u32[]{:S(2)}, u32[]{:S(2)}) collective-permute-start(bf16[4,256,256]{2,1,0:T(8,128)(2,1)} %get-tuple-element.459.rest_0_), channel_id=1, source_target_pairs={{0,8},{4,12},{8,16},{12,20},{16,24},{20,28},{24,0},{28,4},{1,9},{5... | collective-permute-start | bytes 1572872 | tf_op jit(solution)/shard_map/ppermute | solution.py:1480
  229.7 33.9 %collective-permute-start.41 = (bf16[4,256,256]{2,1,0:T(8,128)(2,1)}, bf16[4,256,256]{2,1,0:T(8,128)(2,1)S(1)}, u32[]{:S(2)}, u32[]{:S(2)}) collective-permute-start(bf16[4,256,256]{2,1,0:T(8,128)(2,1)} %get-tuple-element.459.rest_0_), channel_id=1, source_target_pairs={{0,4},{4,0},{8,12},{12,8},{16,20},{20,16},{24,28},{28,24},{1,5},{5... | collective-permute-start | bytes 1572872 | tf_op jit(solution)/shard_map/ppermute | solution.py:1478
  231.2 32.4 %collective-permute-start.42 = (bf16[1024,512]{1,0:T(8,128)(2,1)}, bf16[1024,512]{1,0:T(8,128)(2,1)}, u32[]{:S(2)}, u32[]{:S(2)}) collective-permute-start(bf16[1024,512]{1,0:T(8,128)(2,1)} %get-tuple-element.466), channel_id=1, source_target_pairs={{0,2},{1,3},{2,0},{3,1},{4,6},{5,7},{6,4},{7,5},{8,10},{9,11},{10,... | collective-permute-start | bytes 3145736 | tf_op jit(solution)/shard_map/ppermute | solution.py:37
  233.4 29.6 %all-to-all-start.1 = ((f32[8,4,256]{2,1,0:T(4,128)}), f32[8,4,256]{2,1,0:T(4,128)S(1)}, u32[]{:S(2)}, u32[]{:S(2)}) async-start(f32[8,4,256]{2,1,0:T(4,128)} %broadcast_in_dim.68), calls=%async_computation.1 | async-start | bytes 65536 | tf_op jit(solution)/shard_map/all_to_all | solution.py:1485
  266.5 16.8 %collective-permute-start.48 = (bf16[4,128,512]{2,1,0:T(8,128)(2,1)}, bf16[4,128,512]{2,1,0:T(8,128)(2,1)}, u32[]{:S(2)}, u32[]{:S(2)}) collective-permute-start(bf16[4,128,512]{2,1,0:T(8,128)(2,1)} %get-tuple-element.653), channel_id=1, source_target_pairs={{0,4},{4,0},{8,12},{12,8},{16,20},{20,16},{24,28},{28,24},{1,5},{5... | collective-permute-start | bytes 1572872 | tf_op jit(solution)/shard_map/ppermute | solution.py:147
  269.3 12.9 %collective-permute-start.50 = (bf16[64,1024]{1,0:T(8,128)(2,1)S(1)}, bf16[64,1024]{1,0:T(8,128)(2,1)S(1)}, u32[]{:S(2)}, u32[]{:S(2)}) collective-permute-start(bf16[64,1024]{1,0:T(8,128)(2,1)S(1)} %get-tuple-element.672), channel_id=1, source_target_pairs={{0,1},{1,0},{2,3},{3,2},{4,5},{5,4},{6,7},{7,6},{8,9},{9,8},{10,11... | collective-permute-start | bytes 393224 | tf_op jit(solution)/shard_map/ppermute | solution.py:37
  279.1 26.3 %collective-permute-start.43 = (bf16[4,256,256]{2,1,0:T(8,128)(2,1)S(1)}, bf16[4,256,256]{2,1,0:T(8,128)(2,1)S(1)}, u32[]{:S(2)}, u32[]{:S(2)}) collective-permute-start(bf16[4,256,256]{2,1,0:T(8,128)(2,1)S(1)} %collective-permute-done.40.rest_2_), channel_id=1, source_target_pairs={{0,8},{4,12},{8,16},{12,20},{16,24},{20,28},{24,0},{28,4},{1,9},{5... | collective-permute-start | bytes 1572872 | tf_op jit(solution)/shard_map/ppermute | solution.py:1480
  280.6 24.8 %collective-permute-start.44 = (bf16[4,256,256]{2,1,0:T(8,128)(2,1)S(1)}, bf16[4,256,256]{2,1,0:T(8,128)(2,1)S(1)}, u32[]{:S(2)}, u32[]{:S(2)}) collective-permute-start(bf16[4,256,256]{2,1,0:T(8,128)(2,1)S(1)} %collective-permute-done.40.rest_2_), channel_id=1, source_target_pairs={{0,4},{4,0},{8,12},{12,8},{16,20},{20,16},{24,28},{28,24},{1,5},{5... | collective-permute-start | bytes 1572872 | tf_op jit(solution)/shard_map/ppermute | solution.py:1478
  281.2 24.2 %collective-permute-start.45 = (bf16[1024,256]{1,0:T(8,128)(2,1)}, bf16[1024,256]{1,0:T(8,128)(2,1)}, u32[]{:S(2)}, u32[]{:S(2)}) collective-permute-start(bf16[1024,256]{1,0:T(8,128)(2,1)} %get-tuple-element.485), channel_id=1, source_target_pairs={{0,2},{1,3},{2,0},{3,1},{4,6},{5,7},{6,4},{7,5},{8,10},{9,11},{10,... | collective-permute-start | bytes 1572872 | tf_op jit(solution)/shard_map/ppermute | solution.py:37
  282.2 25.4 %collective-permute-start.46 = (bf16[1024,256]{1,0:T(8,128)(2,1)}, bf16[1024,256]{1,0:T(8,128)(2,1)}, u32[]{:S(2)}, u32[]{:S(2)}) collective-permute-start(bf16[1024,256]{1,0:T(8,128)(2,1)} %get-tuple-element.487), channel_id=1, source_target_pairs={{0,2},{1,3},{2,0},{3,1},{4,6},{5,7},{6,4},{7,5},{8,10},{9,11},{10,... | collective-permute-start | bytes 1572872 | tf_op jit(solution)/shard_map/ppermute | solution.py:37
  283.2 34.1 %collective-permute-start.47 = (bf16[1024,256]{1,0:T(8,128)(2,1)}, bf16[1024,256]{1,0:T(8,128)(2,1)}, u32[]{:S(2)}, u32[]{:S(2)}) collective-permute-start(bf16[1024,256]{1,0:T(8,128)(2,1)} %get-tuple-element.489), channel_id=1, source_target_pairs={{0,2},{1,3},{2,0},{3,1},{4,6},{5,7},{6,4},{7,5},{8,10},{9,11},{10,... | collective-permute-start | bytes 1572872 | tf_op jit(solution)/shard_map/ppermute | solution.py:37
  317.3 14.4 %collective-permute-start.51 = (bf16[4,256,256]{2,1,0:T(8,128)(2,1)S(1)}, bf16[4,256,256]{2,1,0:T(8,128)(2,1)S(1)}, u32[]{:S(2)}, u32[]{:S(2)}) collective-permute-start(bf16[4,256,256]{2,1,0:T(8,128)(2,1)S(1)} %collective-permute-done.43.rest_4_), channel_id=1, source_target_pairs={{0,8},{4,12},{8,16},{12,20},{16,24},{20,28},{24,0},{28,4},{1,9},{5... | collective-permute-start | bytes 1572872 | tf_op jit(solution)/shard_map/ppermute | solution.py:1480
  331.7 38.2 %collective-permute-start.67 = (bf16[1024,256]{1,0:T(8,128)(2,1)}, bf16[1024,256]{1,0:T(8,128)(2,1)S(1)}, u32[]{:S(2)}, u32[]{:S(2)}) collective-permute-start(bf16[1024,256]{1,0:T(8,128)(2,1)} %get-tuple-element.557), channel_id=1, source_target_pairs={{0,2},{1,3},{2,0},{3,1},{4,6},{5,7},{6,4},{7,5},{8,10},{9,11},{10,... | collective-permute-start | bytes 1572872 | tf_op jit(solution)/shard_map/ppermute | solution.py:37
  336.4 43.6 %collective-permute-start.61 = (bf16[4,128,512]{2,1,0:T(8,128)(2,1)}, bf16[4,128,512]{2,1,0:T(8,128)(2,1)S(1)}, u32[]{:S(2)}, u32[]{:S(2)}) collective-permute-start(bf16[4,128,512]{2,1,0:T(8,128)(2,1)} %get-tuple-element.651), channel_id=1, source_target_pairs={{0,4},{4,0},{8,12},{12,8},{16,20},{20,16},{24,28},{28,24},{1,5},{5... | collective-permute-start | bytes 1572872 | tf_op jit(solution)/shard_map/ppermute | solution.py:147
  337.9 21.2 %collective-permute-start.54 = (bf16[4,256,256]{2,1,0:T(8,128)(2,1)S(1)}, bf16[4,256,256]{2,1,0:T(8,128)(2,1)S(1)}, u32[]{:S(2)}, u32[]{:S(2)}) collective-permute-start(bf16[4,256,256]{2,1,0:T(8,128)(2,1)S(1)} %collective-permute-done.51.rest_6_), channel_id=1, source_target_pairs={{0,4},{4,0},{8,12},{12,8},{16,20},{20,16},{24,28},{28,24},{1,5},{5... | collective-permute-start | bytes 1572872 | tf_op jit(solution)/shard_map/ppermute | solution.py:1478
  339.8 40.2 %collective-permute-start.58 = (bf16[128,512]{1,0:T(8,128)(2,1)S(1)}, bf16[128,512]{1,0:T(8,128)(2,1)S(1)}, u32[]{:S(2)}, u32[]{:S(2)}) collective-permute-start(bf16[128,512]{1,0:T(8,128)(2,1)S(1)} %get-tuple-element.668), channel_id=1, source_target_pairs={{0,8},{4,12},{8,16},{12,20},{16,24},{20,28},{24,0},{28,4},{1,9},{5... | collective-permute-start | bytes 393224 | tf_op jit(solution)/shard_map/ppermute | solution.py:158
  348.4 31.6 %collective-permute-start.59 = (bf16[128,512]{1,0:T(8,128)(2,1)S(1)}, bf16[128,512]{1,0:T(8,128)(2,1)S(1)}, u32[]{:S(2)}, u32[]{:S(2)}) collective-permute-start(bf16[128,512]{1,0:T(8,128)(2,1)S(1)} %get-tuple-element.667), channel_id=1, source_target_pairs={{0,16},{4,20},{8,24},{12,28},{16,0},{20,4},{24,8},{28,12},{1,17},{... | collective-permute-start | bytes 393224 | tf_op jit(solution)/shard_map/ppermute | solution.py:158
  359.1 20.9 %collective-permute-start.60 = (bf16[128,512]{1,0:T(8,128)(2,1)S(1)}, bf16[128,512]{1,0:T(8,128)(2,1)S(1)}, u32[]{:S(2)}, u32[]{:S(2)}) collective-permute-start(bf16[128,512]{1,0:T(8,128)(2,1)S(1)} %get-tuple-element.666), channel_id=1, source_target_pairs={{0,24},{4,28},{8,0},{12,4},{16,8},{20,12},{24,16},{28,20},{1,25},{... | collective-permute-start | bytes 393224 | tf_op jit(solution)/shard_map/ppermute | solution.py:158
  378.5 27.7 %collective-permute-start.68 = (bf16[4,128,1024]{2,1,0:T(8,128)(2,1)S(1)}, bf16[4,128,1024]{2,1,0:T(8,128)(2,1)S(1)}, u32[]{:S(2)}, u32[]{:S(2)}) collective-permute-start(bf16[4,128,1024]{2,1,0:T(8,128)(2,1)S(1)} %dynamic-slice_bitcast_fusion), channel_id=1, source_target_pairs={{0,4},{4,0},{8,12},{12,8},{16,20},{20,16},{24,28},{28,24},{1,5},{5... | collective-permute-start | bytes 3145736 | tf_op jit(solution)/shard_map/ppermute | solution.py:147
  380.3 14.7 %collective-permute-start.64 = (bf16[128,512]{1,0:T(8,128)(2,1)S(1)}, bf16[128,512]{1,0:T(8,128)(2,1)S(1)}, u32[]{:S(2)}, u32[]{:S(2)}) collective-permute-start(bf16[128,512]{1,0:T(8,128)(2,1)S(1)} %get-tuple-element.663), channel_id=1, source_target_pairs={{0,8},{4,12},{8,16},{12,20},{16,24},{20,28},{24,0},{28,4},{1,9},{5... | collective-permute-start | bytes 393224 | tf_op jit(solution)/shard_map/ppermute | solution.py:158
  380.8 14.1 %collective-permute-start.65 = (bf16[128,512]{1,0:T(8,128)(2,1)S(1)}, bf16[128,512]{1,0:T(8,128)(2,1)S(1)}, u32[]{:S(2)}, u32[]{:S(2)}) collective-permute-start(bf16[128,512]{1,0:T(8,128)(2,1)S(1)} %get-tuple-element.665), channel_id=1, source_target_pairs={{0,16},{4,20},{8,24},{12,28},{16,0},{20,4},{24,8},{28,12},{1,17},{... | collective-permute-start | bytes 393224 | tf_op jit(solution)/shard_map/ppermute | solution.py:158
  381.5 13.4 %collective-permute-start.66 = (bf16[128,512]{1,0:T(8,128)(2,1)S(1)}, bf16[128,512]{1,0:T(8,128)(2,1)S(1)}, u32[]{:S(2)}, u32[]{:S(2)}) collective-permute-start(bf16[128,512]{1,0:T(8,128)(2,1)S(1)} %get-tuple-element.664), channel_id=1, source_target_pairs={{0,24},{4,28},{8,0},{12,4},{16,8},{20,12},{24,16},{28,20},{1,25},{... | collective-permute-start | bytes 393224 | tf_op jit(solution)/shard_map/ppermute | solution.py:158
  395.3 32.7 %collective-permute-start.63 = (f32[128,1024]{1,0:T(8,128)S(1)}, f32[128,1024]{1,0:T(8,128)S(1)}, u32[]{:S(2)}, u32[]{:S(2)}) collective-permute-start(f32[128,1024]{1,0:T(8,128)S(1)} %pad_maximum_fusion.3), channel_id=1, source_target_pairs={{0,16},{4,20},{8,24},{12,28},{16,0},{20,4},{24,8},{28,12},{1,17},{... | collective-permute-start | bytes 1572872 | tf_op jit(solution)/shard_map/ppermute | solution.py:37
  407.5 36.0 %collective-permute-start.69 = (bf16[128,1024]{1,0:T(8,128)(2,1)}, bf16[128,1024]{1,0:T(8,128)(2,1)}, u32[]{:S(2)}, u32[]{:S(2)}) collective-permute-start(bf16[128,1024]{1,0:T(8,128)(2,1)} %get-tuple-element.648), channel_id=1, source_target_pairs={{0,8},{4,12},{8,16},{12,20},{16,24},{20,28},{24,0},{28,4},{1,9},{5... | collective-permute-start | bytes 786440 | tf_op jit(solution)/shard_map/ppermute | solution.py:158
  409.5 34.0 %collective-permute-start.70 = (bf16[128,1024]{1,0:T(8,128)(2,1)}, bf16[128,1024]{1,0:T(8,128)(2,1)}, u32[]{:S(2)}, u32[]{:S(2)}) collective-permute-start(bf16[128,1024]{1,0:T(8,128)(2,1)} %get-tuple-element.650), channel_id=1, source_target_pairs={{0,16},{4,20},{8,24},{12,28},{16,0},{20,4},{24,8},{28,12},{1,17},{... | collective-permute-start | bytes 786440 | tf_op jit(solution)/shard_map/ppermute | solution.py:158
  410.4 33.1 %collective-permute-start.71 = (bf16[128,1024]{1,0:T(8,128)(2,1)}, bf16[128,1024]{1,0:T(8,128)(2,1)}, u32[]{:S(2)}, u32[]{:S(2)}) collective-permute-start(bf16[128,1024]{1,0:T(8,128)(2,1)} %get-tuple-element.649), channel_id=1, source_target_pairs={{0,24},{4,28},{8,0},{12,4},{16,8},{20,12},{24,16},{28,20},{1,25},{... | collective-permute-start | bytes 786440 | tf_op jit(solution)/shard_map/ppermute | solution.py:158
  (97 other events, 974.6 us)
Sparse Core Ops, SparseCore 0:
  176.9 92.8 reduce-scatter.1

commit v3 on v2

--- a/solution.py
+++ b/solution.py
@@ -138,6 +138,10 @@
     return ((place // 2 + slot // 2) % lines) * 2 + ((place % 2) ^ (slot % 2))
 
 
+def scatter(grads):
+    return lax.psum_scatter(grads, "dp", scatter_dimension=0, tiled=True)
+
+
 def scatter_side(grads):
     n = lax.axis_size("dp")
     side = lax.axis_index("dp") % 2
@@ -202,7 +206,7 @@
     return jnp.where(lane % kernels == row, 1.0, 0.0).astype(BF)
 
 
-def conv_forward(codes, select, style, images, bank, side):
+def conv_forward(codes, select, style, payload, images, bank, side):
     groups = len(images)
     low, channels = images[0].shape
     rows = groups * low
@@ -213,17 +217,20 @@
     parts = block // SUB
     span = SUB * kernels
 
-    def body(c_ref, sel_ref, sty_ref, *rest):
+    extra = payload.shape[0]
+
+    def body(c_ref, sel_ref, sty_ref, pay_ref, *rest):
         x_refs = rest[:groups]
-        b_ref, out_ref, raw_ref, dem_ref, xs_ref, mix_ref, sc_ref = rest[groups : groups + 7]
-        acc, en, scale, mix_row, widen = rest[groups + 7 :]
+        b_ref, out_r = rest[groups], rest[groups + 1 : 2 * groups + 1]
+        raw_ref, dem_ref, xs_ref, mix_ref, sc_ref = rest[2 * groups + 1 : 2 * groups + 6]
+        acc, en, scale, mix_row, widen = rest[2 * groups + 6 :]
         step = pl.program_id(0)
 
         @pl.when(step == 0)
         def _():
             acc[...] = jnp.zeros_like(acc)
             en[...] = jnp.zeros_like(en)
-            logits = dot_nn(c_ref[...], sel_ref[...])
+            logits = dot_nt(c_ref[...], sel_ref[...])
             e = jnp.exp(logits - jnp.max(logits, axis=1, keepdims=True))
             mixing = e / jnp.sum(e, axis=1, keepdims=True)
             mix_ref[...] = mixing
@@ -238,7 +245,8 @@
         xs = []
         for s in range(groups):
             xs.append((x_refs[s][...].astype(F) * here[s : s + 1]).astype(BF))
-            xs_ref[s * low : (s + 1) * low] = xs[s]
+            xs_ref[0, s * low : (s + 1) * low] = xs[s]
+        xs_ref[0, rows:] = pay_ref[...]
         a = []
         for s in range(groups):
             a.append((dot_nn(xs[s], widen[...]) * mix_row[s : s + 1]).astype(BF))
@@ -282,31 +290,32 @@
                         o = o.reshape(low, width)
                         q = (py * 2 + px) * low
                         raw_ref[s, q : q + low] = o.astype(raw_ref.dtype)
-                        out_ref[s, q : q + low] = (o * demod[s]).astype(BF)
+                        out_r[s][q : q + low] = (o * demod[s]).astype(BF)
 
     return pl.pallas_call(
         body,
         grid=(steps,),
         in_specs=[
             pl.BlockSpec((pad, depth), lambda i: (0, 0)),
-            pl.BlockSpec((depth, kernels), lambda i: (0, 0)),
+            pl.BlockSpec((kernels, depth), lambda i: (0, 0)),
             pl.BlockSpec((depth, channels), lambda i: (0, 0)),
+            pl.BlockSpec((extra, block), lambda i: (0, 0)),
         ]
         + [pl.BlockSpec((low, block), lambda i: (0, i))] * groups
         + [pl.BlockSpec((3, 3, block, kernels, width), lambda i: (0, 0, i, 0, 0))],
-        out_specs=[
-            pl.BlockSpec((groups, 4 * low, width), lambda i: (0, 0, 0)),
+        out_specs=[pl.BlockSpec((4 * low, width), lambda i: (0, 0))] * groups
+        + [
             pl.BlockSpec((groups, 4 * low, width), lambda i: (0, 0, 0)),
             pl.BlockSpec((groups, 1, width), lambda i: (0, 0, 0)),
-            pl.BlockSpec((rows, block), lambda i: (0, i)),
+            pl.BlockSpec((1, rows + extra, block), lambda i: (i, 0, 0)),
             pl.BlockSpec((pad, kernels), lambda i: (0, 0)),
             pl.BlockSpec((pad, channels), lambda i: (0, 0)),
         ],
-        out_shape=[
-            jax.ShapeDtypeStruct((groups, 4 * low, width), BF),
+        out_shape=[jax.ShapeDtypeStruct((4 * low, width), BF)] * groups
+        + [
             jax.ShapeDtypeStruct((groups, 4 * low, width), BF),
             jax.ShapeDtypeStruct((groups, 1, width), F),
-            jax.ShapeDtypeStruct((rows, channels), BF),
+            jax.ShapeDtypeStruct((steps, rows + extra, block), BF),
             jax.ShapeDtypeStruct((pad, kernels), F),
             jax.ShapeDtypeStruct((pad, channels), F),
         ],
@@ -324,15 +333,16 @@
             transcendentals=0,
         ),
         name="conv_forward",
-    )(codes, select, style, *images, bank)
-
-
-def conv_back(gs, xs, mixing, bank, groups):
+    )(codes, select, style, payload, *images, bank)
+
+
+def conv_back(gs, xs, mixing, bank, groups, part, parts):
     _, rows, width = gs.shape
-    channels, kernels = xs.shape[1], bank.shape[3]
+    blocks, held, block = xs.shape
+    steps = blocks // parts
+    first = part * steps
+    channels, kernels = steps * block, bank.shape[3]
     pad = mixing.shape[0]
-    block = min(channels, 128)
-    steps = channels // block
     low = rows // groups
 
     def body(g_ref, x_ref, m_ref, b_ref, low_ref, mix_ref, acc, mix_row, widen):
@@ -348,7 +358,7 @@
         for t in range(9):
             p = dot_nt(g_ref[t], b_ref[t // 3, t % 3].reshape(block * kernels, width))
             total = p if total is None else total + p
-        wide = dot_nn(x_ref[...], widen[...])
+        wide = dot_nn(x_ref[0, :rows], widen[...])
         acc[...] += jnp.sum((wide * total).reshape(groups, low // 8, 8, block * kernels), axis=1)
         for s in range(groups):
             cut = slice(s * low, (s + 1) * low)
@@ -371,9 +381,9 @@
         grid=(steps,),
         in_specs=[
             pl.BlockSpec((9, rows, width), lambda i: (0, 0, 0)),
-            pl.BlockSpec((rows, block), lambda i: (0, i)),
+            pl.BlockSpec((1, held, block), lambda i: (first + i, 0, 0)),
             pl.BlockSpec((pad, kernels), lambda i: (0, 0)),
-            pl.BlockSpec((3, 3, block, kernels, width), lambda i: (0, 0, i, 0, 0)),
+            pl.BlockSpec((3, 3, block, kernels, width), lambda i: (0, 0, first + i, 0, 0)),
         ],
         out_specs=[
             pl.BlockSpec((groups, low, block), lambda i: (0, 0, i)),
@@ -398,94 +408,154 @@
     )(gs, xs, mixing, bank)
 
 
-def bank_energy(place, mixing, scale, ge, bank, group):
+def roll_kernels(v, shift):
+    n = v.shape[-2]
+    return pltpu.roll(v, shift % n, v.ndim - 2) if shift % n else v
+
+
+def bank_pairs(place, bank, band):
+    kernels, width = bank.shape[3], bank.shape[4]
+    count = kernels // 2 + 1
+    block = min(band, SUB)
+
+    def body(place_ref, b_ref, q_ref):
+        for c in range(block // 8):
+            cut = slice(c * 8, (c + 1) * 8)
+            total = [None] * count
+            for t in range(9):
+                b = b_ref[t // 3, t % 3, cut].astype(F)
+                for r in range(count):
+                    p = b * roll_kernels(b, -r)
+                    total[r] = p if t == 0 else total[r] + p
+            for r in range(count):
+                q_ref[r, c * 8 * kernels : (c + 1) * 8 * kernels] = (
+                    total[r].reshape(8 * kernels, width).astype(BF)
+                )
+
+    return pl.pallas_call(
+        body,
+        grid_spec=pltpu.PrefetchScalarGridSpec(
+            num_scalar_prefetch=1,
+            grid=(band // block,),
+            in_specs=[
+                pl.BlockSpec(
+                    (3, 3, block, kernels, width),
+                    lambda i, s: (0, 0, s[1] * (band // block) + i, 0, 0),
+                )
+            ],
+            out_specs=pl.BlockSpec((count, block * kernels, width), lambda i, s: (0, i, 0)),
+        ),
+        out_shape=jax.ShapeDtypeStruct((count, band * kernels, width), BF),
+        compiler_params=params(),
+        cost_estimate=pl.CostEstimate(
+            flops=20 * count * band * kernels * width,
+            bytes_accessed=18 * band * kernels * width,
+            transcendentals=0,
+        ),
+        name="bank_pairs",
+    )(place, bank)
+
+
+def energy_sums(place, mixing, scale, ge, pairs, group):
     samples, kernels = mixing.shape
     band = scale.shape[1]
-    width = bank.shape[4]
-    span = SUB * kernels
-    bands = band // SUB
-    chunk = min(samples, 32)
-    chunks = samples // chunk
-    kind = BF if chunks == 1 else F
-
-    def body(place_ref, m_ref, s_ref, g_ref, b_ref, e_ref, se_ref, me_ref, rows, wides, diag):
-        u, part = pl.program_id(0), pl.program_id(1)
-        cut = pl.ds(pl.multiple_of(part * chunk, chunk), chunk)
-
-        @pl.when((u == 0) & (part == 0))
-        def _():
-            rows[...] = split_dot(m_ref[...], tile_mask(band, kernels))
-            wides[...] = split_dot(s_ref[...], widen_mask(band, kernels))
-
-        lanes = pl.ds(pl.multiple_of(u * span, span), span)
-        scaled = rows[cut, lanes] * wides[cut, lanes]
-        mask = band_mask(kernels)[None]
-        d = jnp.where(mask, scaled[:, None, :], 0.0).astype(BF).reshape(chunk * SUB, span)
-        d_turned = d.T
-        ge = 2.0 * g_ref[...]
-        acc = None
-        for t in range(9):
-            b = b_ref[t // 3, t % 3].reshape(span, width)
-            m = dot_nn(d, b)
-            w = (m.reshape(chunk, SUB, width) * ge).reshape(chunk * SUB, width).astype(BF)
-            e = dot_nn(d_turned, w).reshape(SUB, kernels, width)
-            if chunks == 1:
-                e_ref[t // 3, t % 3] = e.astype(kind)
-            else:
-                e_ref[t // 3, t % 3] = e + jnp.where(part == 0, 0.0, e_ref[t // 3, t % 3])
-            p = dot_nt(w, b)
-            acc = p if acc is None else acc + p
-        kept = jnp.where(mask, acc.reshape(chunk, SUB, span), 0.0)
-        diag[cut, lanes] = jnp.sum(kept, axis=1)
-
-        @pl.when((u == bands - 1) & (part == chunks - 1))
-        def _():
-            exact = dict(precision=lax.Precision.HIGHEST, preferred_element_type=F)
-            over = (((1,), (1,)), ((), ()))
-            se = lax.dot_general(diag[...] * rows[...], widen_mask(band, kernels).astype(F), over, **exact)
-            me = lax.dot_general(diag[...] * wides[...], tile_mask(band, kernels).astype(F), over, **exact)
-            for s in range(samples):
-                to = pl.ds(s // group * group + lax.bitwise_xor(place_ref[0], s % group), 1)
-                se_ref[to] = se[s : s + 1]
-                me_ref[to] = me[s : s + 1]
-
-    return pl.pallas_call(
-        body,
-        grid_spec=pltpu.PrefetchScalarGridSpec(
-            num_scalar_prefetch=1,
-            grid=(bands, chunks),
-            in_specs=[
-                pl.BlockSpec((samples, kernels), lambda i, c, s: (0, 0)),
-                pl.BlockSpec((samples, band), lambda i, c, s: (0, 0)),
-                pl.BlockSpec((chunk, 1, width), lambda i, c, s: (c, 0, 0)),
-                pl.BlockSpec(
-                    (3, 3, SUB, kernels, width), lambda i, c, s: (0, 0, s[1] * bands + i, 0, 0)
-                ),
-            ],
-            out_specs=[
-                pl.BlockSpec((3, 3, SUB, kernels, width), lambda i, c, s: (0, 0, i, 0, 0)),
-                pl.BlockSpec((samples, band), lambda i, c, s: (0, 0)),
-                pl.BlockSpec((samples, kernels), lambda i, c, s: (0, 0)),
-            ],
-            scratch_shapes=[
-                pltpu.VMEM((samples, band * kernels), F),
-                pltpu.VMEM((samples, band * kernels), F),
-                pltpu.VMEM((samples, band * kernels), F),
-            ],
-        ),
+    count = pairs.shape[0]
+    exact = dict(precision=lax.Precision.HIGHEST, preferred_element_type=F)
+    along = (((1,), (0,)), ((), ()))
+
+    def fold(a, mask):
+        high = a.astype(BF)
+        rest = (a - high.astype(F)).astype(BF)
+        return dot_nt(high, mask) + dot_nt(rest, mask)
+
+    def body(place_ref, m_ref, s_ref, g_ref, q_ref, se_ref, me_ref):
+        m = m_ref[...]
+        wides = split_dot(s_ref[...], widen_mask(band, kernels))
+        ge = (2.0 * g_ref[...]).astype(BF)
+        row = lax.broadcasted_iota(jnp.int32, (kernels, kernels), 0)
+        lane = lax.broadcasted_iota(jnp.int32, (kernels, kernels), 1)
+        tile = tile_mask(band, kernels)
+        square = wides * wides
+        se, me = None, None
+        for r in range(count):
+            g = dot_nt(ge, q_ref[r])
+            ahead = jnp.where(row == (lane + r) % kernels, 1.0, 0.0)
+            behind = jnp.where(row == (lane + kernels - r) % kernels, 1.0, 0.0)
+            next_m = lax.dot_general(m, ahead, along, **exact)
+            both = split_dot(m * next_m, tile)
+            weight = 1.0 if r == 0 or 2 * r == kernels else 2.0
+            part = (weight * both) * g
+            se = part if se is None else se + part
+            h = fold(g * square, tile)
+            part = next_m * h
+            if weight == 2.0:
+                part = part + lax.dot_general(m * h, behind, along, **exact)
+            me = part if me is None else me + part
+        se = fold(se * wides, widen_mask(band, kernels))
+        for s in range(samples):
+            to = pl.ds(s // group * group + lax.bitwise_xor(place_ref[0], s % group), 1)
+            se_ref[to] = se[s : s + 1]
+            me_ref[to] = me[s : s + 1]
+
+    return pl.pallas_call(
+        body,
+        in_specs=[smem()] + vmem(4),
         out_shape=[
-            jax.ShapeDtypeStruct((3, 3, band, kernels, width), kind),
             jax.ShapeDtypeStruct((samples, band), F),
             jax.ShapeDtypeStruct((samples, kernels), F),
         ],
         compiler_params=params(),
+        name="energy_sums",
+    )(place, mixing, scale, ge, pairs)
+
+
+def bank_energy(place, lefts, ge, bank):
+    kernels, width = bank.shape[3], bank.shape[4]
+    count, rows_all, samples = lefts.shape
+    band = rows_all // kernels
+    step = min(band, 16)
+
+    def body(place_ref, l_ref, ge_ref, b_ref, o_ref, rights):
+        @pl.when(pl.program_id(0) == 0)
+        def _():
+            ge = ge_ref[...].astype(BF)
+            for r in range(count):
+                rights[r] = dot_nn(l_ref[r], ge)
+
+        for tx in range(3):
+            for i in range(band // step):
+                cut = slice(i * step * kernels, (i + 1) * step * kernels)
+                b = b_ref[0, tx, i * step : (i + 1) * step].astype(F)
+                e = rights[0, cut].reshape(step, kernels, width) * b
+                for r in range(1, count):
+                    right = rights[r, cut].reshape(step, kernels, width)
+                    e = e + right * roll_kernels(b, -r)
+                    if 2 * r != kernels:
+                        e = e + roll_kernels(right * b, r)
+                o_ref[0, tx, i * step : (i + 1) * step] = e.astype(BF)
+
+    return pl.pallas_call(
+        body,
+        grid_spec=pltpu.PrefetchScalarGridSpec(
+            num_scalar_prefetch=1,
+            grid=(3,),
+            in_specs=[
+                pl.BlockSpec((count, band * kernels, samples), lambda t, s: (0, 0, 0)),
+                pl.BlockSpec((samples, width), lambda t, s: (0, 0)),
+                pl.BlockSpec((1, 3, band, kernels, width), lambda t, s: (t, 0, s[1], 0, 0)),
+            ],
+            out_specs=pl.BlockSpec((1, 3, band, kernels, width), lambda t, s: (t, 0, 0, 0, 0)),
+            scratch_shapes=[pltpu.VMEM((count, band * kernels, width), F)],
+        ),
+        out_shape=jax.ShapeDtypeStruct((3, 3, band, kernels, width), BF),
+        compiler_params=params(),
         cost_estimate=pl.CostEstimate(
-            flops=54 * bands * samples * SUB * span * width,
-            bytes_accessed=36 * bands * span * width,
+            flops=400 * band * kernels * width,
+            bytes_accessed=36 * band * kernels * width,
             transcendentals=0,
         ),
         name="bank_energy",
-    )(place, mixing, scale, ge, bank)
+    )(place, lefts, ge, bank)
 
 
 def line_sums(g, tap, axis):
@@ -496,77 +566,84 @@
     return g[0] + move_up(g[1], axis)
 
 
-def bank_main(tap_row, before, sources, scale, at, taps, energy, side):
+def bank_main(sources, scale, at, taps, energy, side):
     blocks = len(taps)
     groups, points, width = taps[0].shape
     low = side * side
     held = blocks * groups * low
     band, kernels = energy.shape[2], energy.shape[3]
 
-    def body(src_ref, scale_ref, a_ref, *rest):
+    def body(place_ref, scale_ref, a_ref, *rest):
+        here = place_ref[1]
         g_refs = rest[:blocks]
-        e_ref = rest[blocks]
-        o_ref, lines, sums = rest[-3:]
-        tx = pl.program_id(0)
-
-        @pl.when(tx == 0)
-        def _():
-            for b in range(blocks):
-                for s in range(groups):
-                    g = g_refs[b][s].astype(F).reshape(2, 2, side, side, width)
-                    at_row = pl.multiple_of((src_ref[b] * groups + s) * low, low)
-                    for px in range(2):
-                        v = line_sums((g[0, px], g[1, px]), tap_row, 0)
-                        lines[px, pl.ds(at_row, low)] = v.reshape(low, width)
-
+        e_ref, o_ref, lines, sums = rest[blocks:]
+        ty = pl.program_id(0)
         for tap in range(3):
 
-            @pl.when(tx == tap)
+            @pl.when(ty == tap)
             def _():
-                for b in range(blocks * groups):
-                    cut = slice(b * low, (b + 1) * low)
-                    pair = [lines[px, cut].reshape(side, side, width) for px in range(2)]
-                    sums[cut] = line_sums(pair, tap, 1).reshape(low, width).astype(BF)
-
-        p = dot_nn(a_ref[...], sums[...]).reshape(band, kernels, width)
-        o_ref[0, 0] = (p + e_ref[0, 0].astype(F)) * scale_ref[0]
-
-    whole = [] if before is None else [before]
-    tap_block = pl.BlockSpec((1, 1, band, kernels, width), lambda t: (tap_row, t, 0, 0, 0))
+                for b in range(blocks):
+                    for s in range(groups):
+                        g = g_refs[b][s].astype(F).reshape(2, 2, side, side, width)
+                        for px in range(2):
+                            v = line_sums((g[0, px], g[1, px]), tap, 0)
+                            line = lax.rem(here // 2 + blocks // 2 - b // 2, blocks // 2)
+                            source = 2 * line + lax.bitwise_xor(lax.rem(here, 2), b % 2)
+                            at_row = (source * groups + s) * low
+                            at_row = pl.multiple_of(at_row, low)
+                            lines[px, pl.ds(at_row, low)] = v.reshape(low, width)
+
+        for tx in range(3):
+            for b in range(blocks * groups):
+                cut = slice(b * low, (b + 1) * low)
+                pair = [lines[px, cut].reshape(side, side, width) for px in range(2)]
+                sums[cut] = line_sums(pair, tx, 1).reshape(low, width).astype(BF)
+            p = dot_nn(a_ref[...], sums[...]).reshape(band, kernels, width)
+            o_ref[0, tx] = (p + e_ref[0, tx].astype(F)) * scale_ref[0]
+
     return pl.pallas_call(
         body,
         grid=(3,),
         in_specs=[smem(), smem(), pl.BlockSpec((band * kernels, held), lambda t: (0, 0))]
         + [pl.BlockSpec((groups, points, width), lambda t: (0, 0, 0))] * blocks
-        + [tap_block]
-        + [pl.BlockSpec(memory_space=pl.ANY)] * len(whole),
-        out_specs=tap_block,
+        + [pl.BlockSpec((1, 3, band, kernels, width), lambda t: (t, 0, 0, 0, 0))],
+        out_specs=pl.BlockSpec((1, 3, band, kernels, width), lambda t: (t, 0, 0, 0, 0)),
         out_shape=jax.ShapeDtypeStruct((3, 3, band, kernels, width), F),
-        input_output_aliases={4 + blocks: 0} if whole else {},
         scratch_shapes=[pltpu.VMEM((2, held, width), F), pltpu.VMEM((held, width), BF)],
         compiler_params=params(),
         cost_estimate=pl.CostEstimate(
-            flops=6 * band * kernels * held * width,
-            bytes_accessed=6 * held * width + 18 * band * kernels * width,
+            flops=18 * band * kernels * held * width,
+            bytes_accessed=18 * held * width + 54 * band * kernels * width,
             transcendentals=0,
         ),
         name="bank_main",
-    )(sources, scale, at, *taps, energy, *whole)
-
-
-def tap_sums(grads, demod, raw, side):
+    )(sources, scale, at, *taps, energy)
+
+
+def tap_sums(grads, demod, raw, context, side, copies):
     groups = len(grads)
     _, points, width = raw.shape
     low = side * side
 
-    def body(d_ref, r_ref, *rest):
+    channels = context.shape[1]
+    tokens = context.shape[0] // groups
+
+    def body(d_ref, r_ref, c_ref, *rest):
         g_refs = rest[:groups]
-        taps_ref, sums_ref, en_ref = rest[groups:]
+        taps_ref, sums_ref, en_ref, token_ref, keys, values = rest[groups:]
+        for s in range(groups):
+            cut = slice(s * tokens, (s + 1) * tokens)
+            keys[cut] = g_refs[s][points : points + tokens]
+            values[cut] = g_refs[s][points + tokens : points + 2 * tokens]
+        token_ref[:, :width] = dot_tn(c_ref[...], keys[...]).astype(BF)
+        token_ref[:, width:] = dot_tn(c_ref[...], values[...]).astype(BF)
         for s in range(groups):
             part = g_refs[s][:points].astype(F)
             demod = d_ref[s]
             grad_demod = jnp.sum(part * r_ref[s].astype(F), axis=0, keepdims=True)
-            en_ref[s] = -0.5 * grad_demod * demod * demod * demod
+            en = -0.5 * grad_demod * demod * demod * demod
+            for i in range(copies):
+                en_ref[i, s : s + 1] = en
             taps_ref[s] = (part * demod).astype(BF)
             g = taps_ref[s].astype(F).reshape(2, 2, side, side, width)
             for ty in range(3):
@@ -580,11 +657,13 @@
         out_shape=[
             jax.ShapeDtypeStruct((groups, points, width), BF),
             jax.ShapeDtypeStruct((9, groups * low, width), BF),
-            jax.ShapeDtypeStruct((groups, 1, width), F),
+            jax.ShapeDtypeStruct((copies, groups, width), F),
+            jax.ShapeDtypeStruct((channels, 2 * width), BF),
         ],
+        scratch_shapes=[pltpu.VMEM((groups * tokens, width), BF)] * 2,
         compiler_params=params(),
         name="tap_sums",
-    )(demod, raw, *grads)
+    )(demod, raw, context, *grads)
 
 
 def rms(field, gain):
@@ -661,9 +740,9 @@
                 q, k, v = (
                     qkv_ref[j, :, i * share + h * HD : i * share + (h + 1) * HD] for i in range(3)
                 )
-                heads.append(dot_tn(self_prob(q, k).astype(BF), v).astype(BF))
+                heads.append(dot_tn(v, self_prob(q, k).astype(BF)))
             side_ref, cut = side_slot(own_ref, send_ref, j, channels, share)
-            side_ref[:, cut] = jnp.concatenate(heads, axis=1)
+            side_ref[:, cut] = jnp.concatenate(heads).T.astype(BF)
             two_ref[...] += dot_nn(side_ref[:, cut], wo_r[j][...])
 
     return pl.pallas_call(
@@ -704,9 +783,9 @@
                 q = xq_ref[j, :, h * HD : (h + 1) * HD]
                 k = ckv_r[j][:, h * HD : (h + 1) * HD]
                 v = ckv_r[j][:, share + h * HD : share + (h + 1) * HD]
-                heads.append(dot_tn(cross_prob(q, k).astype(BF), v).astype(BF))
+                heads.append(dot_tn(v, cross_prob(q, k).astype(BF)))
             side_ref, cut = side_slot(own_ref, send_ref, j, channels, share)
-            side_ref[:, cut] = jnp.concatenate(heads, axis=1)
+            side_ref[:, cut] = jnp.concatenate(heads).T.astype(BF)
             three_ref[...] += dot_nn(side_ref[:, cut], co_r[j][...])
         mlp_ref[...] = rms(three_ref[...], gains_ref[4:5])[0].astype(BF)
 
@@ -862,11 +941,11 @@
                 gp = dot_nt(v, g)
                 gs = p * (gp - jnp.sum(p * gp, axis=0, keepdims=True))
                 raw = (gs * (1.0 / math.sqrt(HD))).astype(BF)
-                gq.append(dot_tn(raw, k).astype(BF))
+                gq.append(dot_tn(k, raw))
                 gk.append(dot_nn(raw, q).astype(BF))
                 gv.append(dot_nn(p.astype(BF), g).astype(BF))
             side_ref, cut = side_slot(own_ref, send_ref, j, 2 * channels, share)
-            side_ref[:, cut] = jnp.concatenate(gq, axis=1)
+            side_ref[:, cut] = jnp.concatenate(gq).T.astype(BF)
             dkv_r[j][...] = jnp.concatenate(gk + gv, axis=1)
             grad_norm2 = grad_norm2 + dot_nt(side_ref[:, cut], cq_r[j][...])
         back, gain = rms_back(two_ref[...], in_ref[3:4], grad_norm2)
@@ -924,11 +1003,12 @@
                 gs = p * (gp - jnp.sum(p * gp, axis=0, keepdims=True))
                 square = jnp.sum(gs, axis=1, keepdims=True) * (-1.0 / math.sqrt(HD))
                 raw = (gs * (2.0 / math.sqrt(HD))).astype(BF)
-                gq.append(dot_tn(raw, k).astype(BF))
+                gq.append(dot_tn(k, raw))
                 gk.append((dot_nn(raw, q) + 2.0 * k.astype(F) * square).astype(BF))
                 gv.append(dot_nn(p.astype(BF), g).astype(BF))
             side_ref, cut = side_slot(own_ref, send_ref, j, 0, 3 * share)
-            side_ref[:, cut] = jnp.concatenate(gq + gk + gv, axis=1)
+            gq = jnp.concatenate(gq).T.astype(BF)
+            side_ref[:, cut] = jnp.concatenate([gq] + gk + gv, axis=1)
             grad_norm = grad_norm + dot_nt(side_ref[:, cut], wqkv_r[j][...])
         back, gain = rms_back(one, gains_ref[2:3], grad_norm)
         grad_conv = (grad_two + back) * silu_slope(out)
@@ -983,20 +1063,20 @@
 
     def body(*refs):
         attn, cross, grad = refs[:2], refs[2:4], refs[4:6]
-        both, out = refs[6 : 6 + count], refs[6 + count : 6 + 2 * count]
+        out, last = refs[6 : 6 + count], refs[6 + count : 6 + 2 * count]
         turned = refs[-1]
         turn(turned, cross, 0, channels)
         for i in range(count):
             cut = slice(2 * channels + i * share, 2 * channels + (i + 1) * share)
-            both[i][:, :share] = pair_product(turned, grad, cut)
+            out[i][:, :share] = pair_product(turned, grad, cut)
         turn(turned, grad, 0, channels)
         for i in range(count):
             cut = slice(channels + i * share, channels + (i + 1) * share)
-            both[i][:, share:] = pair_product(turned, cross, cut)
+            out[i][:, share:] = pair_product(turned, cross, cut)
         turn(turned, grad, channels, channels)
         for i in range(count):
             cut = slice(channels + i * share, channels + (i + 1) * share)
-            out[i][...] = pair_product(turned, attn, cut)
+            last[i][...] = pair_product(turned, attn, cut)
 
     return pl.pallas_call(
         body,
@@ -1019,16 +1099,17 @@
 
     def body(*refs):
         attn, grad = refs[:2], refs[2:4]
-        out, turned = refs[4 : 4 + 3 * count], refs[-1]
+        out, last, turned = refs[4 : 4 + count], refs[4 + count : 4 + 2 * count], refs[-1]
         turn(turned, attn, 0, channels)
         for i in range(count):
-            for k in range(3):
-                cut = slice((3 * i + k) * share, (3 * i + k + 1) * share)
-                out[k * count + i][...] = pair_product(turned, grad, cut)
-
-    return pl.pallas_call(
-        body,
-        out_shape=[jax.ShapeDtypeStruct((channels, share), BF)] * (3 * count),
+            at = 3 * i * share
+            out[i][...] = pair_product(turned, grad, slice(at, at + 2 * share))
+            last[i][...] = pair_product(turned, grad, slice(at + 2 * share, at + 3 * share))
+
+    return pl.pallas_call(
+        body,
+        out_shape=[jax.ShapeDtypeStruct((channels, 2 * share), BF)] * count
+        + [jax.ShapeDtypeStruct((channels, share), BF)] * count,
         scratch_shapes=[pltpu.VMEM((channels, 2 * points), BF)],
         compiler_params=params(),
         cost_estimate=pl.CostEstimate(
@@ -1040,20 +1121,118 @@
     )(*attn_pair, *grad_pair)
 
 
+def phase_order(points, side):
+    row = lax.broadcasted_iota(jnp.int32, (points, points), 0)
+    lane = lax.broadcasted_iota(jnp.int32, (points, points), 1)
+    line, place = phase_place(row, side)
+    return lane == 2 * side * line + place
+
+
+def phase_place(row, side):
+    phase, spot = row // (side * side), row % (side * side)
+    return 2 * (spot // side) + phase // 2, 2 * (spot % side) + phase % 2
+
+
+def phase_masks(side):
+    shape = (4 * side * side, 2 * side)
+    row = lax.broadcasted_iota(jnp.int32, shape, 0)
+    lane = lax.broadcasted_iota(jnp.int32, shape, 1)
+    line, place = phase_place(row, side)
+    return jnp.where(lane == line, 1.0, 0.0), jnp.where(lane == place, 1.0, 0.0)
+
+
+def cotangents(place, counts, features, image, noise, vectors, colors, code, rgb, side):
+    points, channels = features.shape
+    count = len(vectors)
+    exact = dict(precision=lax.Precision.HIGHEST, preferred_element_type=F)
+    along = (((1,), (0,)), ((), ()))
+
+    def body(place_ref, live_ref, f_ref, im_ref, n_ref, col_ref, c_ref, rgb_ref, *rest):
+        vec_r = rest[:count]
+        four_ref, low_ref, gi_ref, no_ref, cs_ref, gains_ref = rest[count:]
+        for i in range(count):
+            gains_ref[i : i + 1] = vec_r[i][...].astype(F).reshape(1, channels)
+        order = jnp.where(phase_order(points, side), 1.0, 0.0).astype(BF)
+        by = live_ref[place_ref[0]].astype(F)
+        lines, places = phase_masks(side)
+
+        def column(v):
+            rows = lax.dot_general(lines, v, along, **exact)
+            return jnp.sum(rows * places, axis=1, keepdims=True)
+
+        no_ref[...] = column(n_ref[0].astype(F))
+        scale = dot_nn(c_ref[...], rgb_ref[...])[:1] + 1.0
+        cs_ref[...] = scale
+        four = dot_nn(order, f_ref[...]) * by
+        col = col_ref[...].astype(F)
+        for c in range(3):
+            gi = column(im_ref[0, c]) * by
+            gi_ref[:, c : c + 1] = gi
+            four = four + gi * (col[c : c + 1] * scale)
+        four_ref[...] = four
+        low_ref[...] = four.astype(BF)
+
+    return pl.pallas_call(
+        body,
+        in_specs=[smem(), smem()] + vmem(6 + count),
+        out_shape=[
+            jax.ShapeDtypeStruct((points, channels), F),
+            jax.ShapeDtypeStruct((points, channels), BF),
+            jax.ShapeDtypeStruct((points, 3), F),
+            jax.ShapeDtypeStruct((points, 1), F),
+            jax.ShapeDtypeStruct((1, channels), F),
+            jax.ShapeDtypeStruct((count, channels), F),
+        ],
+        compiler_params=params(),
+        name="cotangents",
+    )(place, counts, features, image, noise, colors, code, rgb, *vectors)
+
+
+def class_tokens(rows, pos, ck, cv):
+    n = rows.shape[0]
+    tokens, channels = pos.shape
+    share = ck.shape[1]
+
+    def body(r_ref, p_ref, ck_ref, cv_ref, ctx_ref, *out_r):
+        pos = p_ref[...].astype(F)
+        rows = r_ref[...].astype(F)
+        for j in range(n):
+            ctx_ref[j * tokens : (j + 1) * tokens] = (rows[j : j + 1] + pos).astype(BF)
+        for w, at in ((ck_ref, 0), (cv_ref, share)):
+            product = dot_nn(ctx_ref[...], w[...])
+            for j in range(n):
+                out_r[j][:, at : at + share] = product[j * tokens : (j + 1) * tokens].astype(BF)
+
+    return pl.pallas_call(
+        body,
+        out_shape=[jax.ShapeDtypeStruct((n * tokens, channels), BF)]
+        + [jax.ShapeDtypeStruct((tokens, 2 * share), BF)] * n,
+        compiler_params=params(),
+        name="class_tokens",
+    )(rows, pos, ck, cv)
+
+
 def band_prepare(place, received, codes, select, style, points_low):
     n_dp, _, band = received.shape
     samples, depth = codes.shape
-    kernels = select.shape[1]
+    kernels = select.shape[0]
     low = n_dp * points_low // samples
     columns = samples * low
     step = 8
 
-    def body(place_ref, x_ref, c_ref, sel_ref, sty_ref, at_ref, mix_ref, scale_ref, turned):
-        logits = dot_nn(c_ref[...], sel_ref[...])
+    def body(place_ref, x_ref, c_ref, sel_ref, sty_ref, at_ref, mix_ref, scale_ref, left_ref, turned):
+        logits = dot_nt(c_ref[...], sel_ref[...])
         e = jnp.exp(logits - jnp.max(logits, axis=1, keepdims=True))
         mixing = e / jnp.sum(e, axis=1, keepdims=True)
         mix_ref[...] = mixing
         scale_ref[...] = dot_nn(c_ref[...], sty_ref[...]) + 1.0
+        scale_turned = scale_ref[...].T
+        mix_turned = mixing.T
+        for r in range(kernels // 2 + 1):
+            ahead = jnp.concatenate([mix_turned[r:], mix_turned[:r]]) if r else mix_turned
+            both = 2.0 * mix_turned * ahead
+            left = (scale_turned * scale_turned)[:, None, :] * both[None]
+            left_ref[r] = left.reshape(band * kernels, samples).astype(BF)
         for b in range(n_dp):
             turned[:, b * points_low : (b + 1) * points_low] = x_ref[b, :points_low].astype(F).T
         row = lax.broadcasted_iota(jnp.int32, (samples, columns), 0)
@@ -1074,6 +1253,7 @@
             jax.ShapeDtypeStruct((band * kernels, columns), BF),
             jax.ShapeDtypeStruct((samples, kernels), F),
             jax.ShapeDtypeStruct((samples, band), F),
+            jax.ShapeDtypeStruct((kernels // 2 + 1, band * kernels, samples), BF),
         ],
         scratch_shapes=[pltpu.VMEM((band, columns), F)],
         compiler_params=params(),
@@ -1081,44 +1261,39 @@
     )(place, received, codes, select, style)
 
 
-def side_outputs(place, three, branch, image_grad, color_scale, colors, bias, context, shares, ck, cv, gains, late, count_sums, count_all, side):
+def side_outputs(place, three, branch, image_grad, color_scale, colors, bias, tokens, shares, ck, cv, gains, late, count_sums, count_all, side):
     points, channels = three.shape
     n, parts = len(shares), len(branch)
     share = ck.shape[1]
-    tokens = context.shape[0] // n
     low = side * side
     exact = dict(precision=lax.Precision.HIGHEST, preferred_element_type=F)
 
-    def body(place_ref, three_ref, gi_ref, cs_ref, col_ref, bias_ref, ctx_ref, ck_ref, cv_ref, gains_ref, late_ref, *rest):
+    def body(place_ref, bias_ref, three_ref, gi_ref, cs_ref, col_ref, ck_ref, cv_ref, gains_ref, late_ref, *rest):
         branch_r, share_r = rest[:parts], rest[parts : parts + n]
-        feat_ref, color_ref, dkv_ref, pack_ref, four_ref, keys, values = rest[parts + n :]
+        feat_ref, color_ref, pack_ref, four_ref, keys, values = rest[parts + n :]
         here = place_ref[0]
         four = three_ref[...]
         for b in branch_r:
             four = four + b[...].astype(F)
         four_ref[...] = four
-        row = lax.broadcasted_iota(jnp.int32, (points, points), 0)
-        lane = lax.broadcasted_iota(jnp.int32, (points, points), 1)
-        phase, spot = lane // low, lane % low
-        line = 2 * (spot // side) + phase // 2
-        target = 2 * side * line + 2 * (spot % side) + phase % 2
-        order = jnp.where(row == target, 1.0, 0.0)
-        moved = lax.dot_general(order, four, (((1,), (0,)), ((), ())), **exact)
+        order = jnp.where(phase_order(points, side), 1.0, 0.0)
+        moved = lax.dot_general(order, four, (((0,), (0,)), ((), ())), **exact)
         feat_ref[...] = moved.reshape(1, 2 * side, 2 * side, channels)
-        scale, col = cs_ref[...], col_ref[...]
+        scale, col = cs_ref[...], col_ref[...].astype(F)
         tint = col * scale
-        color_ref[...] = bias_ref[...] + lax.dot_general(
-            tint, four_ref[...], (((1,), (1,)), ((), ())), **exact
-        )
+        color = lax.dot_general(four_ref[...], tint, (((1,), (1,)), ((), ())), **exact)
+        lines, places = phase_masks(side)
+        for c in range(3):
+            spread_out = color[:, c : c + 1] * places
+            color_ref[0, c] = bias_ref[c] + lax.dot_general(
+                lines, spread_out, (((0,), (0,)), ((), ())), **exact
+            )
         gi = gi_ref[...]
         image = lax.dot_general(gi, four_ref[...], (((0,), (0,)), ((), ())), **exact)
         for j in range(n):
             cut = slice(j * tokens, (j + 1) * tokens)
             keys[cut] = share_r[j][points : points + tokens]
             values[cut] = share_r[j][points + tokens : points + 2 * tokens]
-        turned = ctx_ref[...]
-        dkv_ref[:, :share] = dot_tn(turned, keys[...]).astype(BF)
-        dkv_ref[:, share:] = dot_tn(turned, values[...]).astype(BF)
         grad = dot_nt(keys[...], ck_ref[...]) + dot_nt(values[...], cv_ref[...])
         pack_ref[...] = jnp.zeros_like(pack_ref)
         total = None
@@ -1140,11 +1315,10 @@
 
     return pl.pallas_call(
         body,
-        in_specs=[smem()] + vmem(10 + parts + n),
+        in_specs=[smem(), smem()] + vmem(8 + parts + n),
         out_shape=[
             jax.ShapeDtypeStruct((1, 2 * side, 2 * side, channels), F),
-            jax.ShapeDtypeStruct((3, points), F),
-            jax.ShapeDtypeStruct((channels, 2 * share), BF),
+            jax.ShapeDtypeStruct((1, 3, 2 * side, 2 * side), F),
             jax.ShapeDtypeStruct((count_all, channels), F),
         ],
         scratch_shapes=[
@@ -1154,7 +1328,7 @@
         ],
         compiler_params=params(),
         name="side_outputs",
-    )(place, three, image_grad, color_scale, colors, bias, context, ck, cv, gains, late, *branch, *shares)
+    )(place, bias, three, image_grad, color_scale, colors, ck, cv, gains, late, *branch, *shares)
 
 
 def late_sums_kernel(place, scale, pack, low_parts, images, own_scale, energy, mixing_sum, mixing, count_sums, at_sum):
@@ -1169,7 +1343,7 @@
         total = low_r[0][...].astype(F)
         for v in low_r[1:]:
             total = total + v[...].astype(F)
-        grad_ref[...] = total * (own_ref[...] * scale_ref[0])
+        grad_ref[...] = total * (own_ref[0:1] * scale_ref[0])
         out_ref[...] = pack_ref[...]
         line = jnp.sum(total * im_ref[...].astype(F), axis=0, keepdims=True)
         out_ref[pl.ds(count_sums + here, 1)] = line
@@ -1193,27 +1367,29 @@
     )(place, scale, pack, images, own_scale, energy, mixing_sum, mixing, *low_parts)
 
 
-def style_final(scale, mixing_grad, scale_grad, rgb_grad, tokens, codes, labels, select, style, rgb, classes):
+def style_final(places, scale, mixing_grad, scale_grad, rgb_grad, tokens, codes, labels, select, style, rgb, classes, group):
     samples, channels = scale_grad.shape
-    depth, kernels = select.shape
-
-    def body(s_ref, mg_ref, sg_ref, rg_ref, t_ref, c_ref, l_ref, sel_ref, sty_ref, rgb_ref, *outs):
-        dsel_ref, dsty_ref, drgb_ref, dcodes_ref, table_ref = outs
+    kernels, depth = select.shape
+
+    def body(place_ref, s_ref, mg_ref, sg_ref, rg_ref, t_ref, c_ref, l_ref, sel_ref, sty_ref, rgb_ref, *outs):
+        dsel_ref, dsty_ref, drgb_ref, dcodes_ref, table_ref, held = outs
         by = s_ref[0]
         codes = c_ref[...]
-        logits = dot_nn(codes, sel_ref[...])
+        logits = dot_nt(codes, sel_ref[...])
         e = jnp.exp(logits - jnp.max(logits, axis=1, keepdims=True))
         mixing = e / jnp.sum(e, axis=1, keepdims=True)
         mg = mg_ref[...] * by
         logit = (mixing * (mg - jnp.sum(mixing * mg, axis=1, keepdims=True))).astype(BF)
         sg = (sg_ref[...] * by).astype(BF)
         rg = (rg_ref[...] * by).astype(BF)
-        dsel_ref[...] = dot_tn(codes, logit)
+        dsel_ref[...] = dot_tn(logit, codes)
         dsty_ref[...] = dot_tn(codes, sg)
         drgb_ref[...] = dot_tn(codes, rg)
-        dcodes_ref[...] = (
-            dot_nt(logit, sel_ref[...]) + dot_nt(sg, sty_ref[...]) + dot_nt(rg, rgb_ref[...])
+        held[...] = (
+            dot_nn(logit, sel_ref[...]) + dot_nt(sg, sty_ref[...]) + dot_nt(rg, rgb_ref[...])
         )
+        for j in range(group):
+            dcodes_ref[j : j + 1] = held[pl.ds(place_ref[1] * group + j, 1)]
         ids = lax.broadcasted_iota(jnp.int32, (samples, classes), 1)
         one_hot = jnp.where(ids == l_ref[...], 1.0, 0.0).astype(BF)
         t = t_ref[...] * by
@@ -1223,17 +1399,18 @@
 
     return pl.pallas_call(
         body,
-        in_specs=[smem()] + vmem(9),
+        in_specs=[smem(), smem()] + vmem(9),
         out_shape=[
-            jax.ShapeDtypeStruct((depth, kernels), F),
+            jax.ShapeDtypeStruct((kernels, depth), F),
             jax.ShapeDtypeStruct((depth, channels), F),
             jax.ShapeDtypeStruct((depth, channels), F),
-            jax.ShapeDtypeStruct((samples, depth), F),
+            jax.ShapeDtypeStruct((group, depth), F),
             jax.ShapeDtypeStruct((classes, channels), F),
         ],
+        scratch_shapes=[pltpu.VMEM((samples, depth), F)],
         compiler_params=params(),
         name="style_final",
-    )(scale, mixing_grad, scale_grad, rgb_grad, tokens, codes, labels, select, style, rgb)
+    )(places, scale, mixing_grad, scale_grad, rgb_grad, tokens, codes, labels, select, style, rgb)
 
 
 def local(
@@ -1312,86 +1489,83 @@
     own_images = images[0].reshape(low, channels)
     codes = jnp.take(styles, jnp.arange(max(n, 8), dtype=jnp.int32) % n ^ r, axis=0)
     image_blocks = spread(own_images)
+    depth, points_low = styles.shape[1], n * low
+    label_rows = jnp.stack([labels // 256, labels % 256, counts]).astype(BF)
+    payload = jnp.concatenate([styles.reshape(-1), label_rows.reshape(-1)])
+    block = min(channels, 128)
+    payload = jnp.pad(payload, (0, -payload.shape[0] % (16 * block))).reshape(-1, block)
     qkv_proj = jnp.concatenate([query_proj, key_proj, value_proj], axis=1)
     image_blocks, (codes, qkv_proj) = tie_lists(image_blocks, [codes, qkv_proj])
     qkv_far = far_swaps(qkv_proj)
     near = [near_swaps([m])[0] for m in (qkv_proj, out_proj, cross_query, cross_out)]
-    conv_part, conv_raw, demod, xs, mixing, scale_in = conv_forward(
-        codes, select_proj, style_proj, image_blocks, kernel_bank, side
-    )
+    select_turned = select_proj.T
+    *conv_part, conv_raw, demod, xs, mixing, scale_in = conv_forward(
+        codes, select_turned, style_proj, payload, image_blocks, kernel_bank, side
+    )
+
+    places = jnp.stack([r, d]).astype(jnp.int32)
+    conv_part[0], places = tie(conv_part[0], places)
+    pairs = bank_pairs(places, kernel_bank, band)
 
     later = [styles, labels, counts, cot_features, cot_image, noise_map, conv_bias, noise_gain]
     later += [norm_attn, norm_cross, norm_mlp, class_table, class_pos, cross_key, cross_value]
     later += [rgb_style, color_projection, color_bias, out_proj, cross_query, cross_out, xs]
-    (conv_part,), later, qkv_far, near = tie_lists([conv_part], later, qkv_far, near)
+    conv_part, (pairs,), later, qkv_far, near = tie_lists(
+        conv_part, [pairs], later, qkv_far, near
+    )
     styles, labels, counts, cot_features, cot_image, noise_map, conv_bias, noise_gain = later[:8]
     norm_attn, norm_cross, norm_mlp, class_table, class_pos, cross_key, cross_value = later[8:15]
     rgb_style, color_projection, color_bias, out_proj, cross_query, cross_out, xs = later[15:]
 
     parts = [conv_part[0]] + [swap(conv_part[j], "rows", j) for j in range(1, n)]
     qkv_near = near[:1] + near_swaps(qkv_far)
+    place = r.astype(jnp.int32).reshape(1)
+    colors = color_projection.T
+    grad_four, grad_four_low, grad_image, noise, color_scale, gains = cotangents(
+        place,
+        counts,
+        cot_features.reshape(points, channels),
+        cot_image,
+        noise_map,
+        (noise_gain, conv_bias, norm_attn, norm_cross, norm_mlp),
+        colors,
+        codes,
+        rgb_style,
+        side,
+    )
+    parts, qkv_near, rest = tie_lists(
+        parts,
+        qkv_near,
+        [grad_four, grad_four_low, grad_image, color_scale, noise, gains]
+        + [xs, labels, class_table, out_proj],
+    )
+    grad_four, grad_four_low, grad_image, color_scale, noise, gains = rest[:6]
+    xs, labels, class_table, out_proj = rest[6:]
     wo_far = far_swaps(out_proj)
-    own_live = lax.dynamic_index_in_dim(counts.astype(F), r, 0, keepdims=False)
-    color_scale = jnp.dot(codes[:1], rgb_style, preferred_element_type=F) + 1.0
-    grad_image = by_phase(cot_image[0].transpose(1, 2, 0)) * own_live
-    colors = color_projection.astype(F)
-    tinted = jnp.dot(grad_image, colors.T, precision=lax.Precision.HIGHEST)
-    grad_four = by_phase(cot_features[0]).astype(F) * own_live + tinted * color_scale
-    noise = by_phase(noise_map[0]).astype(F).reshape(points, 1)
-    place = r.astype(jnp.int32).reshape(1)
-    gains = jnp.stack([noise_gain, conv_bias, norm_attn, norm_cross, norm_mlp]).astype(F)
-    parts, qkv_near, wo_far, rest = tie_lists(
-        parts, qkv_near, wo_far, [grad_four, noise, gains, xs, styles, labels, class_table]
-    )
-    grad_four, noise, gains, xs, styles, labels, class_table = rest
-
-    bands = xs.reshape(n * low, n_dp, band).transpose(1, 0, 2)
-    label_rows = jnp.stack([labels // 256, labels % 256, counts]).astype(BF)
-    codes_flat = jnp.concatenate([styles.reshape(-1), label_rows.reshape(-1)])
-    codes_flat = jnp.pad(codes_flat, (0, -codes_flat.shape[0] % (16 * band))).reshape(-1, band)
-    sent = jnp.concatenate(
-        [bands, jnp.broadcast_to(codes_flat[None], (n_dp,) + codes_flat.shape)], axis=1
-    )
+
+    if band == block:
+        bands = xs
+    else:
+        split = xs[:, :points_low].reshape(xs.shape[0], points_low, block // band, band)
+        split = split.transpose(0, 2, 1, 3).reshape(n_dp, points_low, band)
+        rest = jnp.broadcast_to(payload.reshape(1, -1, band), (n_dp, payload.size // band, band))
+        bands = jnp.concatenate([split, rest], axis=1)
+    received = lax.all_to_all(bands, "dp", 0, 0, tiled=True)
     wo_near = near[1:2] + near_swaps(wo_far)
     wqkv = whole(qkv_proj, qkv_far, qkv_near)
     wo = whole(out_proj, wo_far, wo_near)
     conv, two, qkv, attn_own, attn_sent = attn_forward(place, parts, noise, gains, wqkv, wo)
-    cq_far, co_far = far_swaps(cross_query), far_swaps(cross_out)
-    (two, sent, labels, class_table), cq_far, co_far = tie_lists(
-        [two, sent, labels, class_table], cq_far, co_far
-    )
-
-    class_rows = jnp.take(class_table, jnp.take(labels, group_order), axis=0)
-    context = (class_rows.astype(F)[:, None, :] + class_pos.astype(F)[None]).astype(BF)
-    flat_context = context.reshape(n * tokens, channels)
-    ckv = jnp.dot(
-        flat_context,
-        jnp.concatenate([cross_key, cross_value], axis=1),
-        preferred_element_type=F,
-    ).astype(BF)
-    ckv = ckv.reshape(n, tokens, 2 * share)
+    cq_far = far_swaps(cross_query)
+    (two, received, labels, class_table), cq_far = tie_lists(
+        [two, received, labels, class_table], cq_far
+    )
+
+    co_far = far_swaps(cross_out)
+    flat_context, *ckv = class_tokens(
+        jnp.take(class_table, jnp.take(labels, group_order), axis=0), class_pos, cross_key, cross_value
+    )
     ckv = [ckv[0]] + [swap(ckv[j], "rows", j) for j in range(1, n)]
     cq = whole(cross_query, cq_far, near[2:3] + near_swaps(cq_far))
-    co = whole(cross_out, co_far, near[3:4] + near_swaps(co_far))
-    received = lax.all_to_all(sent, "dp", 0, 0, tiled=True)
-    grad_four_low = grad_four.astype(BF)
-    three, normed_mlp, xq, cross_own, cross_sent = cross_forward(two, gains, cq, co, ckv)
-    grad_far = far_swaps(grad_four_low)
-    grad_near = near_swaps([grad_four_low])
-    attn_near = near_swaps([attn_sent])
-    (three, normed_mlp, received), grad_far, grad_near, attn_near = tie_lists(
-        [three, normed_mlp, received], grad_far, grad_near, attn_near
-    )
-
-    normed_near = near_swaps([normed_mlp])
-    grad_near += near_swaps(grad_far)
-    (normed_mlp,), normed_near, grad_near = tie_lists([normed_mlp], normed_near, grad_near)
-    grad_pairs = list(zip([grad_four_low] + grad_far, grad_near))
-    normed_far = far_swaps(normed_mlp)
-    mlp_in = [normed_mlp] + normed_near
-    act, inner, *backward = mlp_core(mlp_in, grad_pairs[0], up_proj, down_proj)
-    points_low = n * low
-    depth = styles.shape[1]
     codes_back = received[:, points_low:].reshape(n_dp, -1)
     styles_all = codes_back[:, : n * depth].reshape(samples, depth)
     label_back = codes_back[:, n * depth : n * depth + 3 * n]
@@ -1401,19 +1575,33 @@
     codes_all = jnp.take(styles_all.reshape(n_dp, n, depth), group_order, axis=1)
     band_proj = lax.dynamic_slice_in_dim(style_proj, d * band, band, axis=1)
     bands_ready = band_prepare(
-        place, received, codes_all.reshape(samples, depth), select_proj, band_proj, points_low
-    )
+        place, received, codes_all.reshape(samples, depth), select_turned, band_proj, points_low
+    )
+    (two,), co_far, cq, ckv, bands_ready, ready = tie_lists(
+        [two], co_far, cq, ckv, bands_ready, [styles_all, labels_all, inverse]
+    )
+    at, mixing_all, scale_band, lefts = bands_ready
+    styles_all, labels_all, inverse = ready
+    co = whole(cross_out, co_far, near[3:4] + near_swaps(co_far))
+    three, normed_mlp, xq, cross_own, cross_sent = cross_forward(two, gains, cq, co, ckv)
+    grad_far = far_swaps(grad_four_low)
+    grad_near = near_swaps([grad_four_low])
+    attn_near = near_swaps([attn_sent])
+    (three, normed_mlp), grad_far, grad_near, attn_near = tie_lists(
+        [three, normed_mlp], grad_far, grad_near, attn_near
+    )
+
+    normed_near = near_swaps([normed_mlp])
+    grad_near += near_swaps(grad_far)
+    (normed_mlp,), normed_near, grad_near = tie_lists([normed_mlp], normed_near, grad_near)
+    grad_pairs = list(zip([grad_four_low] + grad_far, grad_near))
+    normed_far = far_swaps(normed_mlp)
+    mlp_in = [normed_mlp] + normed_near
+    act, inner, *backward = mlp_core(mlp_in, grad_pairs[0], up_proj, down_proj)
     cross_near = near_swaps([cross_sent])
-    (act, inner), backward, normed_far, bands_ready, cross_near, ready = tie_lists(
-        [act, inner],
-        backward,
-        normed_far,
-        bands_ready,
-        cross_near,
-        [styles_all, labels_all, inverse],
-    )
-    at, mixing_all, scale_band = bands_ready
-    styles_all, labels_all, inverse = ready
+    (act, inner), backward, normed_far, cross_near = tie_lists(
+        [act, inner], backward, normed_far, cross_near
+    )
     acts, inners = [act], [inner]
     for i, block in enumerate(normed_far):
         pair = [block] + near_swaps([block])
@@ -1464,12 +1652,18 @@
     )
     d_cross, d_out = list(back[:half]), list(back[half:])
     shares, d_cross, d_out, sent_near = tie_lists(shares, d_cross, d_out, sent_near)
-    grad_taps, gs, grad_energy = tap_sums(shares, demod, conv_raw, side)
+    grad_taps, gs, grad_energy, d_tokens = tap_sums(
+        shares, demod, conv_raw, flat_context, side, n_dp
+    )
 
     rest, branch, d_cross, d_out, shares = tie_lists(
-        [grad_taps, gs, grad_energy, late_sums, d_gains], branch, d_cross, d_out, shares
-    )
-    grad_taps, gs, grad_energy, late_sums, d_gains = rest
+        [grad_taps, gs, grad_energy, d_tokens, late_sums, d_gains],
+        branch,
+        d_cross,
+        d_out,
+        shares,
+    )
+    grad_taps, gs, grad_energy, d_tokens, late_sums, d_gains = rest
     lines = n_dp // 2
     ring = [grad_taps]
     flipped = []
@@ -1481,41 +1675,45 @@
         (ring[-1], flipped[-1]), *work = tie_lists([ring[-1], flipped[-1]], *work)
         return work
 
-    ge_all = jnp.broadcast_to(grad_energy.reshape(1, n, width), (n_dp, n, width))
-    ge_all = lax.all_to_all(ge_all, "dp", 0, 0, tiled=True).reshape(samples, 1, width)
+    ge_all = lax.all_to_all(grad_energy, "dp", 0, 0, tiled=True).reshape(samples, width)
     d_cross = far_parts(d_cross)
     back = attn_weights([attn_own] + attn_near, [qkv_own] + sent_near, half, share)
-    d_query, d_key, d_value = (list(back[i * half : (i + 1) * half]) for i in range(3))
-    (low_part, mixing_conv, ge_all), d_cross, d_query, d_key, d_value, d_out = ring_step(
-        [*conv_back(gs, xs, mixing, kernel_bank, n), ge_all],
+    d_attn, d_value = list(back[:half]), list(back[half:])
+    low_first, mix_first = conv_back(gs, xs, mixing, kernel_bank, n, 0, 2)
+    (low_first, mix_first, ge_all, gs, d_tokens), d_cross, d_attn, d_value, d_out = ring_step(
+        [low_first, mix_first, ge_all, gs, d_tokens], d_cross, d_attn, d_value, d_out
+    )
+    d_out = far_parts(d_out)
+    token_side = scatter_side(d_tokens)
+    low_last, mix_last = conv_back(gs, xs, mixing, kernel_bank, n, 1, 2)
+    ready, d_out, d_cross, d_attn, shares, token_side = ring_step(
+        [low_last, mix_last],
+        d_out,
         d_cross,
-        d_query,
-        d_key,
-        d_value,
-        d_out,
-    )
-
-    d_out, d_query, d_key = far_parts(d_out), far_parts(d_query), far_parts(d_key)
-    cross_side = scatter_side(add_all(d_cross).astype(BF))
-    places = jnp.stack([r, d]).astype(jnp.int32)
+        d_attn,
+        shares,
+        token_side,
+    )
+    low_last, mix_last = ready
+    low_part = jnp.concatenate([low_first, low_last], axis=2)
+    mixing_conv = mix_first + mix_last
+
+    cross_grads = jnp.concatenate([add_all(d_cross), add_all(d_out)], axis=1).astype(BF)
+    token_parts = scatter_lines(*token_side)
+    d_attn = far_parts(d_attn)
     low_near = near_sums([low_part[j] for j in range(n)])
-    done = bank_energy(places, mixing_all, scale_band, ge_all, kernel_bank, n)
-    done, d_out, d_query, d_key, d_value, cross_side, low_near, (g_mlp,) = ring_step(
-        list(done), d_out, d_query, d_key, d_value, cross_side, low_near, [g_mlp]
-    )
-    energy, scale_energy, mixing_energy = done
-
+    done = energy_sums(place, mixing_all, scale_band, ge_all, pairs, n)
     count_sums = -(-(tokens + 9 + -(-samples * kernels // channels)) // 8) * 8
     count_all = -(-(count_sums + 4 * n + 1) // 8) * 8
-    features, color_image, d_ck_cv, pack = side_outputs(
+    features, color_image, pack = side_outputs(
         place,
         three,
         branch,
         grad_image,
         color_scale,
-        colors.T,
-        color_bias.astype(F).reshape(3, 1),
-        flat_context,
+        colors,
+        color_bias.astype(F),
+        tokens,
         shares,
         cross_key,
         cross_value,
@@ -1525,66 +1723,53 @@
         count_all,
         side,
     )
-    color_image = color_image.reshape(3, 2, 2, side, side).transpose(0, 3, 1, 4, 2)
-    color_image = color_image.reshape(1, 3, 2 * side, 2 * side)
-    low_parts = far_parts(low_near)
+    done, d_attn, low_near, (g_mlp, pack, lefts, cross_grads), d_value, token_parts = ring_step(
+        list(done), d_attn, low_near, [g_mlp, pack, lefts, cross_grads], d_value, token_parts
+    )
+    cross_grads = scatter(cross_grads)
+    scale_energy, mixing_energy = done
 
     def as_rows(v):
         v = v.reshape(1, -1)
         v = jnp.pad(v, ((0, 0), (0, -v.shape[1] % channels)))
         return v.reshape(-1, channels)
 
+    low_parts = far_parts(low_near)
     pack, grad_images = late_sums_kernel(
         place,
         inverse,
         pack,
         low_parts,
         own_images,
-        scale_in[:1],
+        scale_in,
         scale_energy.reshape(n, channels),
         as_rows(mixing_energy),
         mixing_conv,
         count_sums,
         tokens + 9,
     )
-    (grad_images, pack), d_value, cross_side, d_out, d_query, d_key = ring_step(
-        [grad_images, pack], d_value, cross_side, d_out, d_query, d_key
-    )
-
+    pack = add_over(pack, "rows")
     d_value = far_parts(d_value)
-    pack = add_over(pack, "rows")
+    energy = bank_energy(places, lefts, ge_all, kernel_bank)
+    (grad_images, pack, energy), d_value, d_attn = ring_step(
+        [grad_images, pack, energy], d_value, d_attn
+    )
     while len(flipped) < lines:
         ((pack,),) = ring_step([pack])
+
+    everyone_rows = jnp.broadcast_to(pack.astype(BF)[None], (n_dp,) + pack.shape)
+    everyone_rows = lax.all_to_all(everyone_rows, "dp", 0, 0, tiled=True)
+    attn_side = jnp.concatenate([add_all(d_attn), add_all(d_value)], axis=1).astype(BF)
+    attn_side = scatter_side(attn_side)
     blocks = [None] * n_dp
     for t in range(lines):
         for e, v in enumerate((ring[t], flipped[t])):
             blocks[2 * t + e] = v
-
-    sources = ring_source(n_dp, d, slots).astype(jnp.int32)
-    cross_parts = scatter_lines(*cross_side)
-    query_side = scatter_side(jnp.concatenate([add_all(d_out), add_all(d_query)], axis=1).astype(BF))
-    sums, gathered = pack[:count_sums], pack[count_sums:]
-    grad_bank = None
-    delta = 1
-    for tap_row in range(3):
-        grad_bank = bank_main(tap_row, grad_bank, sources, inverse, at, blocks, energy, side)
-        if delta < n_dp:
-            sums, gathered = merge_step(sums, gathered, "dp", d, delta)
-            delta *= 2
-        if tap_row == 0:
-            (grad_bank, sums, gathered), cross_parts, query_side = tie_lists(
-                [grad_bank, sums, gathered], cross_parts, query_side
-            )
-            query_parts = scatter_lines(*query_side)
-            keyval = [add_all(d_key), add_all(d_value), d_ck_cv.astype(F)]
-            keyval_side = scatter_side(jnp.concatenate(keyval, axis=1).astype(BF))
-        else:
-            grad_bank, sums, gathered = tie(grad_bank, sums, gathered)
-    while delta < n_dp:
-        sums, gathered = merge_step(sums, gathered, "dp", d, delta)
-        delta *= 2
-    keyval_parts = scatter_lines(*keyval_side)
-    gathered = gathered.reshape(n_dp, -1, channels)
+    grad_bank = bank_main(places, inverse, at, blocks, energy, side)
+    (grad_bank, everyone_rows), attn_side = tie_lists([grad_bank, everyone_rows], attn_side)
+    attn_parts = scatter_lines(*attn_side)
+    sums = jnp.sum(everyone_rows[:, :count_sums].astype(F), axis=0)
+    gathered = everyone_rows[:, count_sums:].astype(F)
     scale_grad, bands_grad, token_all, rgb_all = (
         gathered[:, i * n : (i + 1) * n].reshape(samples, channels) for i in range(4)
     )
@@ -1596,7 +1781,8 @@
     sums = sums[: tokens + 9] * inverse
     grad_images = grad_images.reshape(1, side, side, channels)
 
-    d_select, d_style, d_rgb, d_codes, d_table = style_final(
+    d_select, d_style, d_rgb, styles_grad, d_table = style_final(
+        places,
         inverse,
         mixing_grad,
         scale_grad,
@@ -1604,15 +1790,15 @@
         token_all,
         styles_all,
         labels_all,
-        select_proj,
+        select_turned,
         style_proj,
         rgb_style,
         class_table.shape[0],
-    )
-    styles_grad = lax.dynamic_slice_in_dim(d_codes, d * n, n, axis=0)
-
-    cross_grads, query_grads, keyval_grads = tie(
-        *(add_all(v) * inverse for v in (cross_parts, query_parts, keyval_parts))
+        n,
+    )
+
+    cross_grads, attn_grads, token_grads = tie(
+        *(add_all(v) * inverse for v in ([cross_grads], attn_parts, token_parts))
     )
     g_mlp = g_mlp.astype(F) * inverse
     wide = up_proj.shape[1]
@@ -1626,19 +1812,19 @@
         grad_images,
         styles_grad,
         grad_bank,
-        d_select,
+        d_select.T,
         d_style,
         sums[tokens + 7],
         sums[tokens + 8],
         sums[tokens + 6],
-        column(query_grads, 1),
-        column(keyval_grads, 0),
-        column(keyval_grads, 1),
-        column(query_grads, 0).T,
+        column(attn_grads, 0),
+        column(attn_grads, 1),
+        column(attn_grads, 2),
+        column(cross_grads, 2).T,
         sums[tokens + 1],
         column(cross_grads, 0),
-        column(keyval_grads, 2),
-        column(keyval_grads, 3),
+        column(token_grads, 0),
+        column(token_grads, 1),
         column(cross_grads, 1).T,
         d_table,
         sums[:tokens],

time: 462 us -> 421 us (0.911)
  local copies, waits for them, and re-layouts: 50.9 us -> 31.2 us
  other arithmetic: 30.6 us -> 20.4 us
  waiting for transfers between devices: 75.5 us -> 69.1 us
  starting transfers between devices: 68.7 us -> 63.6 us
    ppermute x53 -> x49, waiting for transfers between devices: 63.9 us -> 38.4 us  [swap(): return lax.ppermute(x, axis, [(i, i ^ delta) for i in range(n)])]
    ppermute x3 -> x2, waiting for transfers between devices: 0.01 us -> 21.3 us  [scatter_side(): return (mine, lax.ppermute(theirs, 'dp', ring_perm(n, 0, 1)))]
    pallas_call x3 -> x7, Pallas kernels: 17.7 us -> 38 us  [the longest x1 7.67 us: bank_pairs(): pl.pallas_call(body, grid_spec=pltpu.PrefetchScalarGridSpec(num_scalar_pr...]
    pallas_call x3 -> x1, Pallas kernels: 28.2 us -> 17.2 us  [bank_main(): pl.pallas_call(body, grid=(3,), in_specs=[smem(), smem(), pl.BlockSpec((b...]
    ppermute x4, waiting for transfers between devices: 9.52 us -> 0.01 us  [ring_step(): flipped.append(lax.ppermute(ring[-1], 'dp', ring_perm(n_dp, 0, 1)))]
    ppermute x9 -> x6, waiting for transfers between devices: 0.02 us -> 9.26 us  [scatter_lines(): pieces.append(lax.ppermute(piece, 'dp', ring_perm(n, step, 0)))]
    pallas_call x1, Pallas kernels: 20.5 us -> 11.8 us  [bank_energy(): pl.pallas_call(body, grid_spec=pltpu.PrefetchScalarGridSpec(num_scalar_pr...]
    ppermute x53 -> x49, starting transfers between devices: 32.8 us -> 25.7 us  [swap(): return lax.ppermute(x, axis, [(i, i ^ delta) for i in range(n)])]
  transfers between devices with their start and end apart: 75 -> 69, of which waited for: 18 -> 20; matrix products, arithmetic and copies ran while one was open for 15% -> 9% of each run, Pallas kernels for 46% -> 52%
where the time goes in v3:
time: 421 us; the launch traced here: 414 us
  Pallas kernels  213 us (51%)
  waiting for transfers between devices  69.1 us (16%)
  starting transfers between devices  63.6 us (15%)
  local copies, waits for them, and re-layouts  31.2 us (7%)
  other arithmetic  20.4 us (5%)
  between operations  16.3 us (4%)
    ppermute x49, waiting for transfers between devices, swap(): return lax.ppermute(x, axis, [(i, i ^ delta) for i in range(n)])  38.4 us
    ppermute x49, starting transfers between devices, swap(): return lax.ppermute(x, axis, [(i, i ^ delta) for i in range(n)])  25.7 us
    pallas_call x2, Pallas kernels, conv_back(): pl.pallas_call(body, grid=(steps,), in_specs=[pl.BlockSpec((9, rows, widt...  24.1 us
    pallas_call x1, Pallas kernels, conv_forward(): pl.pallas_call(body, grid=(steps,), in_specs=[pl.BlockSpec((pad, depth),...  23.5 us
    ppermute x2, waiting for transfers between devices, scatter_side(): return (mine, lax.ppermute(theirs, 'dp', ring_perm(n, 0, 1)))  21.3 us
    pallas_call x1, Pallas kernels, bank_main(): pl.pallas_call(body, grid=(3,), in_specs=[smem(), smem(), pl.BlockSpec((b...  17.2 us
    pallas_call x1, Pallas kernels, attn_backward(): pl.pallas_call(body, out_shape=[jax.ShapeDtypeStruct((3, channels), F)] +...  16.9 us
    pallas_call x2, Pallas kernels, mlp_core(): pl.pallas_call(body, grid=(steps,), in_specs=[block] * (2 * count) + [pl....  16.5 us
  transfers between devices with their start and end apart: 69, of which 20 were waited for; matrix products, arithmetic and copies ran while one was open for 9% of the time, Pallas kernels for 52%

profile of v3, /device:TPU:0, one launch (start us, length us, event | category | flops | bytes accessed | tf_op | source)
XLA Modules:
  0.0 414.1 jit_solution(17914567338986886689)
XLA Ops:
  7.2 3.0 collective-permute-start.1
  18.8 23.5 %conv_forward.1 = (bf16[256,256]{1,0:T(8,128)(2,1)}, bf16[256,256]{1,0:T(8,128)(2,1)}, bf16[256,256]{1,0:T(8,128)(2,1)}, bf16[256,256]{1,0:T(8,128)(2,1)}, bf16[...) custom-call(bf16[8,512]{1,0:T(8,128)(2,1)} %broadcast_select_fusion., ...), custom_call_target="tpu_custom_call" | custom-call | flops 14495514624 | bytes 37748736 | tf_op jit(solution)/shard_map/conv_forward/pallas_call | solution.py:295
  42.3 7.7 %bank_pairs.1.q_ref = bf16[5,1024,256]{2,1,0:T(8,128)(2,1)} custom-call(s32[2]{0:T(128)} %pad_add_fusion.place_ref, bf16[3,3,1024,8,256]{4,3,2,1,0:T(8,128)(2,1)} %b_ref.7), custom_call_target="tpu_custom_call" | custom-call | flops 26214400 | bytes 4718592 | tf_op jit(solution)/shard_map/bank_pairs/pallas_call | solution.py:435
  50.0 3.7 collective-permute-done.3.rest_6_.rest_2_
  55.4 1.6 collective-permute-start.9
  57.1 3.8 cotangents.1
  60.9 3.0 collective-permute-done.9.rest_2_
  65.4 5.9 %all-to-all-start = ((bf16[8,288,128]{2,1,0:T(8,128)(2,1)}), bf16[8,288,128]{2,1,0:T(8,128)(2,1)S(1)}, u32[]{:S(2)}, u32[]{:S(2)}) async-start(bf16[8,288,128]{2,1,0:T(8,128)(2,1)} %get-tuple-element.376.x_ref), calls=%async_computation | async-start | bytes 1179648 | tf_op jit(solution)/shard_map/all_to_all | solution.py:1553
  71.6 7.0 %collective-permute-done.12.rest_10_.rest_6_ = bf16[256,1024]{1,0:T(8,128)(2,1)} collective-permute-done((bf16[256,1024]{1,0:T(8,128)(2,1)}, bf16[256,1024]{1,0:T(8,128)(2,1)}, u32[]{:S(2)}, u32[]{:S(2)}) %collective-permute-start.12) | collective-permute-done | bytes 524320 | tf_op jit(solution)/shard_map/ppermute | solution.py:37
  79.1 1.6 constant_dynamic-slice_fusion.sty_ref
  80.7 1.5 collective-permute-start.15
  82.3 13.5 %attn_forward.1 = (bf16[256,1024]{1,0:T(8,128)(2,1)}, f32[256,1024]{1,0:T(8,128)}, bf16[4,256,768]{2,1,0:T(8,128)(2,1)}, bf16[256,1536]{1,0:T(8,128)(2,1)}, bf16[256,1536]{1,0:T(8,128)(2,1)}) custom-call(s32[1]{0:T(128)} %bitcast.place_ref, f32[256,1]{1,0:T(8,128)} %get-tuple-element.365.noise_ref, f32[5,1024]{1,0:T(8,128)} %get-tuple-element.366.gains_ref.in_ref, ...), custom_call_target="tpu_custom_call" | custom-call | flops 2684354560 | bytes 16777216 | tf_op jit(solution)/shard_map/attn_forward/pallas_call | solution.py:748
  98.6 2.2 class_tokens.1
  106.6 5.4 %band_prepare.1 = (bf16[1024,2048]{1,0:T(8,128)(2,1)}, f32[32,8]{1,0:T(8,128)}, f32[32,128]{1,0:T(8,128)}, bf16[5,1024,32]{2,1,0:T(8,128)(2,1)}) custom-call(s32[1]{0:T(128)} %bitcast.place_ref, bf16[8,288,128]{2,1,0:T(8,128)(2,1)} %copy-done.3, bf16[32,512]{1,0:T(8,128)(2,1)} %broadcast_select_fusion.c_ref, bf16[8,512]{1,0:T(8,128)(2,1)} %bitcast.119, ...), custom_call_target="tpu_custom_call" | custom-call | tf_op jit(solution)/shard_map/band_prepare/pallas_call | solution.py:1249
  115.3 10.3 %cross_forward.1 = (f32[256,1024]{1,0:T(8,128)}, bf16[256,1024]{1,0:T(8,128)(2,1)}, bf16[4,256,256]{2,1,0:T(8,128)(2,1)}, bf16[256,1536]{1,0:T(8,128)(2,1)}, bf16[256,1536]{1,0:T(8,128)(2,1)}) custom-call(f32[256,1024]{1,0:T(8,128)} %get-tuple-element.398.two_ref, f32[5,1024]{1,0:T(8,128)} %get-tuple-element.366.gains_ref.in_ref, bf16[1024,256]{1,0:T(8,128)(2,1)} %rest_0_.2, ...), custom_call_target="tpu_custom_call" | custom-call | flops 1342177280 | bytes 8388608 | tf_op jit(solution)/shard_map/cross_forward/pallas_call | solution.py:792
  130.8 8.3 %mlp_core.2 = (bf16[512,1024]{1,0:T(8,128)(2,1)}, bf16[512,1024]{1,0:T(8,128)(2,1)}, bf16[256,1024]{1,0:T(8,128)(2,1)}, bf16[256,1024]{1,0:T(8,128)(2,1)}) custom-call(bf16[256,1024]{1,0:T(8,128)(2,1)} %get-tuple-element.422.refs_0_.rest_0_, bf16[256,1024]{1,0:T(8,128)(2,1)} %copy-done.52, bf16[256,1024]{1,0:T(8,128)(2,1)} %get-tuple-element.411.refs_2_.rest_4_, ...), custom_call_target="tpu_custom_call" | custom-call | flops 3221225472 | bytes 4194304 | tf_op jit(solution)/shard_map/mlp_core/pallas_call | solution.py:845
  139.1 5.4 %collective-permute-done.26.refs_0_.rest_2_ = bf16[256,1024]{1,0:T(8,128)(2,1)S(1)} collective-permute-done((bf16[256,1024]{1,0:T(8,128)(2,1)}, bf16[256,1024]{1,0:T(8,128)(2,1)S(1)}, u32[]{:S(2)}, u32[]{:S(2)}) %collective-permute-start.26) | collective-permute-done | bytes 524320 | tf_op jit(solution)/shard_map/ppermute | solution.py:37
  147.3 8.2 %mlp_core.3 = (bf16[512,1024]{1,0:T(8,128)(2,1)}, bf16[512,1024]{1,0:T(8,128)(2,1)}, bf16[256,1024]{1,0:T(8,128)(2,1)}, bf16[256,1024]{1,0:T(8,128)(2,1)}) custom-call(bf16[256,1024]{1,0:T(8,128)(2,1)} %copy-done.55, bf16[256,1024]{1,0:T(8,128)(2,1)} %copy-done.57, bf16[256,1024]{1,0:T(8,128)(2,1)} %copy-done.50, bf16[256,1024]{1,0:T(8,128)(2,1)} %copy-done.53, ...), custom_call_target="tpu_custom_call" | custom-call | flops 3221225472 | bytes 4194304 | tf_op jit(solution)/shard_map/mlp_core/pallas_call | solution.py:845
  156.0 1.8 collective-permute-done.30
  158.5 12.7 %mlp_rest.1 = (bf16[256,1024]{1,0:T(8,128)(2,1)}, bf16[256,1024]{1,0:T(8,128)(2,1)}, bf16[256,1024]{1,0:T(8,128)(2,1)}, bf16[256,1024]{1,0:T(8,128)(2,1)}, bf16[1024,2048]{1,0:T(8,128)(2,1)}) custom-call(bf16[1024,1024]{1,0:T(8,128)(2,1)} %down_ref.1, bf16[256,1024]{1,0:T(8,128)(2,1)} %get-tuple-element.422.refs_0_.rest_0_, bf16[256,1024]{1,0:T(8,128)(2,1)} %copy-done.52, ...), custom_call_target="tpu_custom_call" | custom-call | flops 6442450944 | bytes 16777216 | tf_op jit(solution)/shard_map/mlp_rest/pallas_call | solution.py:900
  174.7 12.2 %cross_backward.1 = (f32[256,1024]{1,0:T(8,128)}, f32[2,1024]{1,0:T(2,128)}, bf16[256,2560]{1,0:T(8,128)(2,1)}, bf16[256,2560]{1,0:T(8,128)(2,1)}, bf16[16,512]{...) custom-call(f32[256,1024]{1,0:T(8,128)} %convert_add_fusion.gn_ref, ...), custom_call_target="tpu_custom_call" | custom-call | flops 2147483648 | bytes 12582912 | tf_op jit(solution)/shard_map/cross_backward/pallas_call | solution.py:958
  189.2 16.9 %attn_backward.1 = (f32[3,1024]{1,0:T(4,128)}, bf16[288,256]{1,0:T(8,128)(2,1)}, bf16[288,256]{1,0:T(8,128)(2,1)}, bf16[288,256]{1,0:T(8,128)(2,1)}, bf16[288,25...) custom-call(s32[1]{0:T(128)} %bitcast.place_ref, f32[256,1024]{1,0:T(8,128)} %get-tuple-element.458.g2_ref, ...), custom_call_target="tpu_custom_call" | custom-call | flops 6442450944 | bytes 25165824 | tf_op jit(solution)/shard_map/attn_backward/pallas_call | solution.py:1026
  208.2 5.7 %cross_weights.1 = (bf16[1024,512]{1,0:T(8,128)(2,1)}, bf16[1024,512]{1,0:T(8,128)(2,1)}, bf16[1024,256]{1,0:T(8,128)(2,1)}, bf16[1024,256]{1,0:T(8,128)(2,1)}) custom-call(bf16[256,1536]{1,0:T(8,128)(2,1)} %get-tuple-element.480.refs_0_, bf16[256,1536]{1,0:T(8,128)(2,1)} %copy-done.45, bf16[256,1536]{1,0:T(8,128)(2,1)} %get-tuple-element.482.refs_2_, ...), custom_call_target="tpu_custom_call" | custom-call | flops 1610612736 | bytes 5242880 | tf_op jit(solution)/shard_map/cross_weights/pallas_call | solution.py:1081
  215.7 3.5 tap_sums.1
  224.8 3.9 all-to-all-start.1
  228.8 12.1 %conv_back.2 = (bf16[4,64,512]{2,1,0:T(8,128)(2,1)}, f32[4,8]{1,0:T(4,128)}) custom-call(bf16[9,256,256]{2,1,0:T(8,128)(2,1)} %get-tuple-element.529.g_ref, bf16[8,288,128]{2,1,0:T(8,128)(2,1)} %get-tuple-element.376.x_ref, f32[8,8]{1,0:T(8,128)} %get-tuple-element.513.m_ref, bf16[3,3,1024,8,256]{4,3,2,1,0:T(8,128)(2,1)} %b_ref.7), custom_call_target="tpu_custom_call" | custom-call | flops 4831838208 | bytes 18874368 | tf_op jit(solution)/shard_map/conv_back/pallas_call | solution.py:379
  240.9 5.1 %attn_weights.1 = (bf16[1024,512]{1,0:T(8,128)(2,1)}, bf16[1024,512]{1,0:T(8,128)(2,1)}, bf16[1024,256]{1,0:T(8,128)(2,1)}, bf16[1024,256]{1,0:T(8,128)(2,1)}) custom-call(bf16[256,1536]{1,0:T(8,128)(2,1)} %get-tuple-element.480.refs_0_, bf16[256,1536]{1,0:T(8,128)(2,1)} %copy-done.45, bf16[256,1536]{1,0:T(8,128)(2,1)} %get-tuple-element.520.refs_2_, ...), custom_call_target="tpu_custom_call" | custom-call | flops 1610612736 | bytes 4194304 | tf_op jit(solution)/shard_map/attn_weights/pallas_call | solution.py:1109
  246.6 2.0 collective-permute-start.43
  251.6 5.2 %energy_sums.1 = (f32[32,128]{1,0:T(8,128)}, f32[32,8]{1,0:T(8,128)}) custom-call(s32[1]{0:T(128)} %bitcast.place_ref, f32[32,8]{1,0:T(8,128)} %get-tuple-element.550.m_ref, f32[32,128]{1,0:T(8,128)} %get-tuple-element.551.s_ref, f32[32,256]{1,0:T(8,128)} %reshape.251.g_ref.ge_ref, bf16[5,1024,256]{2,1,0:T(8,128)(2,1)} %bank_pairs.1.q_ref), custom_call_target="tpu_custom_call" | custom-call | tf_op jit(solution)/shard_map/energy_sums/pallas_call | solution.py:500
  256.9 12.0 %conv_back.3 = (bf16[4,64,512]{2,1,0:T(8,128)(2,1)}, f32[4,8]{1,0:T(4,128)}) custom-call(bf16[9,256,256]{2,1,0:T(8,128)(2,1)} %get-tuple-element.529.g_ref, bf16[8,288,128]{2,1,0:T(8,128)(2,1)} %get-tuple-element.376.x_ref, f32[8,8]{1,0:T(8,128)} %get-tuple-element.513.m_ref, bf16[3,3,1024,8,256]{4,3,2,1,0:T(8,128)(2,1)} %b_ref.7), custom_call_target="tpu_custom_call" | custom-call | flops 4831838208 | bytes 18874368 | tf_op jit(solution)/shard_map/conv_back/pallas_call | solution.py:379
  268.9 9.0 %collective-permute-done.46 = bf16[4,128,512]{2,1,0:T(8,128)(2,1)S(1)} collective-permute-done((bf16[4,128,512]{2,1,0:T(8,128)(2,1)S(1)}, bf16[4,128,512]{2,1,0:T(8,128)(2,1)S(1)}, u32[]{:S(2)}, u32[]{:S(2)}) %collective-permute-start.46) | collective-permute-done | bytes 524320 | tf_op jit(solution)/shard_map/ppermute | solution.py:151
  277.9 1.5 collective-permute-start.47
  280.2 1.6 collective-permute-start.52
  285.6 7.6 %side_outputs.1 = (f32[1,16,16,1024]{3,2,1,0:T(8,128)}, f32[1,3,16,16]{3,2,1,0:T(8,128)}, f32[56,1024]{1,0:T(8,128)}) custom-call(s32[1]{0:T(128)} %bitcast.place_ref, f32[3]{0:T(128)} %convert_element_type.175.bias_ref, f32[256,1024]{1,0:T(8,128)} %get-tuple-element.413.three_ref, f32[256,3]{1,0:T(8,128)} %get-tuple-element.414.gi_ref, ...), custom_call_target="tpu_custom_call" | custom-call | tf_op jit(solution)/shard_map/side_outputs/pallas_call | solution.py:1316
  293.3 3.0 collective-permute-done.52
  298.1 1.7 collective-permute-start.54
  300.5 5.8 %collective-permute-done.53 = bf16[128,512]{1,0:T(8,128)(2,1)S(1)} collective-permute-done((bf16[128,512]{1,0:T(8,128)(2,1)S(1)}, bf16[128,512]{1,0:T(8,128)(2,1)S(1)}, u32[]{:S(2)}, u32[]{:S(2)}) %collective-permute-start.53) | collective-permute-done | bytes 131104 | tf_op jit(solution)/shard_map/ppermute | solution.py:162
  313.4 2.1 late_sums.1
  317.4 11.8 %bank_energy.1.rest_8_ = bf16[3,3,128,8,256]{4,3,2,1,0:T(8,128)(2,1)} custom-call(s32[2]{0:T(128)} %pad_add_fusion.place_ref, bf16[5,1024,32]{2,1,0:T(8,128)(2,1)} %get-tuple-element.583.l_ref, f32[32,256]{1,0:T(8,128)} %reshape.251.g_ref.ge_ref, bf16[3,3,1024,8,256]{4,3,2,1,0:T(8,128)(2,1)} %b_ref.7), custom_call_target="tpu_custom_call" | custom-call | flops 104857600 | bytes 9437184 | tf_op jit(solution)/shard_map/bank_energy/pallas_call | solution.py:537
  329.3 2.0 collective-permute-start.58
  331.4 6.2 %collective-permute-done.58 = f32[56,1024]{1,0:T(8,128)S(1)} collective-permute-done((f32[56,1024]{1,0:T(8,128)S(1)}, f32[56,1024]{1,0:T(8,128)S(1)}, u32[]{:S(2)}, u32[]{:S(2)}) %collective-permute-start.58) | collective-permute-done | bytes 229408 | tf_op jit(solution)/shard_map/ppermute | solution.py:37
  338.7 6.5 %all-to-all-start.2 = ((bf16[8,56,1024]{2,1,0:T(8,128)(2,1)}), bf16[8,56,1024]{2,1,0:T(8,128)(2,1)S(1)}, u32[]{:S(2)}, u32[]{:S(2)}) async-start(bf16[8,56,1024]{2,1,0:T(8,128)(2,1)} %broadcast_in_dim.55), calls=%async_computation.3 | async-start | bytes 1835008 | tf_op jit(solution)/shard_map/all_to_all | solution.py:1761
  347.0 2.1 collective-permute-start.60
  349.0 17.2 %bank_main.1 = f32[3,3,128,8,256]{4,3,2,1,0:T(8,128)} custom-call(s32[2]{0:T(128)} %pad_add_fusion.place_ref, f32[1]{0:T(128)} %bitcast.16.scale_ref.s_ref, bf16[1024,2048]{1,0:T(8,128)(2,1)} %get-tuple-element.589.a_ref, bf16[4,256,256]{2,1,0:T(8,128)(2,1)} %get-tuple-element.511.rest_0_, bf16[4,256,256]{2,1,0:T(8,128)(2,1)} %copy-done.48, ...), custom_call_target="tpu_custom_call" | custom-call | flops 9663676416 | bytes 23592960 | tf_op jit(solution)/shard_map/bank_main/pallas_call | solution.py:604
  366.2 12.3 %collective-permute-done.60 = bf16[4,128,768]{2,1,0:T(8,128)(2,1)} collective-permute-done((bf16[4,128,768]{2,1,0:T(8,128)(2,1)S(1)}, bf16[4,128,768]{2,1,0:T(8,128)(2,1)}, u32[]{:S(2)}, u32[]{:S(2)}) %collective-permute-start.60) | collective-permute-done | bytes 786464 | tf_op jit(solution)/shard_map/ppermute | solution.py:151
  382.0 2.1 collective-permute-start.62
  384.0 1.8 collective-permute-start.63
  390.1 6.5 %style_final.1 = (f32[8,512]{1,0:T(8,128)}, f32[512,1024]{1,0:T(8,128)}, f32[512,1024]{1,0:T(8,128)}, f32[4,512]{1,0:T(4,128)}, f32[1000,1024]{1,0:T(8,128)}) custom-call(s32[2]{0:T(128)} %pad_add_fusion.place_ref, f32[1]{0:T(128)} %bitcast.16.scale_ref.s_ref, f32[32,8]{1,0:T(8,128)} %slice_add_fusion.mg_ref, f32[32,1024]{1,0:T(8,128)} %bitcast_add_fusion.sg_ref, ...), custom_call_target="tpu_custom_call" | custom-call | tf_op jit(solution)/shard_map/style_final/pallas_call | solution.py:1400
  (342 shorter events, 88.1 us)
Async XLA Ops:
  10.3 39.8 %collective-permute-start.5 = (bf16[256,1024]{1,0:T(8,128)(2,1)}, bf16[256,1024]{1,0:T(8,128)(2,1)}, u32[]{:S(2)}, u32[]{:S(2)}) collective-permute-start(bf16[256,1024]{1,0:T(8,128)(2,1)} %rest_4_.5), channel_id=1, source_target_pairs={{0,1},{1,0},{2,3},{3,2},{4,5},{5,4},{6,7},{7,6},{8,9},{9,8},{10,11... | collective-permute-start | bytes 1572872 | tf_op jit(solution)/shard_map/ppermute | solution.py:37
  10.8 39.3 %collective-permute-start.6 = (bf16[1024,256]{1,0:T(8,128)(2,1)}, bf16[1024,256]{1,0:T(8,128)(2,1)S(1)}, u32[]{:S(2)}, u32[]{:S(2)}) collective-permute-start(bf16[1024,256]{1,0:T(8,128)(2,1)} %rest_0_.2), channel_id=1, source_target_pairs={{0,1},{1,0},{2,3},{3,2},{4,5},{5,4},{6,7},{7,6},{8,9},{9,8},{10,11... | collective-permute-start | bytes 1572872 | tf_op jit(solution)/shard_map/ppermute | solution.py:37
  10.8 39.3 %collective-permute-start.7 = (bf16[256,1024]{1,0:T(8,128)(2,1)}, bf16[256,1024]{1,0:T(8,128)(2,1)}, u32[]{:S(2)}, u32[]{:S(2)}) collective-permute-start(bf16[256,1024]{1,0:T(8,128)(2,1)} %rest_4_.4), channel_id=1, source_target_pairs={{0,1},{1,0},{2,3},{3,2},{4,5},{5,4},{6,7},{7,6},{8,9},{9,8},{10,11... | collective-permute-start | bytes 1572872 | tf_op jit(solution)/shard_map/ppermute | solution.py:37
  17.0 36.8 %collective-permute-start.3 = (bf16[1024,768]{1,0:T(8,128)(2,1)S(1)}, bf16[1024,768]{1,0:T(8,128)(2,1)S(1)}, u32[]{:S(2)}, u32[]{:S(2)}) collective-permute-start(bf16[1024,768]{1,0:T(8,128)(2,1)S(1)} %pad_maximum_fusion.rest_4_.rest_0_), channel_id=1, source_target_pairs={{0,2},{1,3},{2,0},{3,1},{4,6},{5,7},{6,4},{7,5},{8,10},{9,11},{10,... | collective-permute-start | bytes 4718600 | tf_op jit(solution)/shard_map/ppermute | solution.py:37
  17.3 36.4 %collective-permute-start.4 = (bf16[1024,768]{1,0:T(8,128)(2,1)S(1)}, bf16[1024,768]{1,0:T(8,128)(2,1)S(1)}, u32[]{:S(2)}, u32[]{:S(2)}) collective-permute-start(bf16[1024,768]{1,0:T(8,128)(2,1)S(1)} %pad_maximum_fusion.rest_4_.rest_0_), channel_id=1, source_target_pairs={{0,1},{1,0},{2,3},{3,2},{4,5},{5,4},{6,7},{7,6},{8,9},{9,8},{10,11... | collective-permute-start | bytes 4718600 | tf_op jit(solution)/shard_map/ppermute | solution.py:37
  54.9 8.9 %collective-permute-start.11 = (bf16[1024,768]{1,0:T(8,128)(2,1)S(1)}, bf16[1024,768]{1,0:T(8,128)(2,1)S(1)}, u32[]{:S(2)}, u32[]{:S(2)}) collective-permute-start(bf16[1024,768]{1,0:T(8,128)(2,1)S(1)} %collective-permute-done.3.rest_6_.rest_2_), channel_id=1, source_target_pairs={{0,1},{1,0},{2,3},{3,2},{4,5},{5,4},{6,7},{7,6},{8,9},{9,8},{10,11... | collective-permute-start | bytes 4718600 | tf_op jit(solution)/shard_map/ppermute | solution.py:37
  65.0 13.6 %collective-permute-start.12 = (bf16[256,1024]{1,0:T(8,128)(2,1)}, bf16[256,1024]{1,0:T(8,128)(2,1)}, u32[]{:S(2)}, u32[]{:S(2)}) collective-permute-start(bf16[256,1024]{1,0:T(8,128)(2,1)} %rest_4_.5), channel_id=1, source_target_pairs={{0,2},{1,3},{2,0},{3,1},{4,6},{5,7},{6,4},{7,5},{8,10},{9,11},{10,... | collective-permute-start | bytes 1572872 | tf_op jit(solution)/shard_map/ppermute | solution.py:37
  65.4 30.3 %all-to-all-start = ((bf16[8,288,128]{2,1,0:T(8,128)(2,1)}), bf16[8,288,128]{2,1,0:T(8,128)(2,1)S(1)}, u32[]{:S(2)}, u32[]{:S(2)}) async-start(bf16[8,288,128]{2,1,0:T(8,128)(2,1)} %get-tuple-element.376.x_ref), calls=%async_computation | async-start | bytes 1179648 | tf_op jit(solution)/shard_map/all_to_all | solution.py:1553
  71.3 235.5 %reduce-scatter.3.cloned.1.call-start = ((), (), s32[]{:S(2)}) async-start(), calls=%async_computation.5 | async-start | bytes 4718592 | tf_op jit(solution)/shard_map/reduce_scatter | solution.py:1618
  78.6 17.1 %collective-permute-start.14 = (bf16[1024,256]{1,0:T(8,128)(2,1)S(1)}, bf16[1024,256]{1,0:T(8,128)(2,1)}, u32[]{:S(2)}, u32[]{:S(2)}) collective-permute-start(bf16[1024,256]{1,0:T(8,128)(2,1)S(1)} %copy-done.4), channel_id=1, source_target_pairs={{0,2},{1,3},{2,0},{3,1},{4,6},{5,7},{6,4},{7,5},{8,10},{9,11},{10,... | collective-permute-start | bytes 1572872 | tf_op jit(solution)/shard_map/ppermute | solution.py:37
  80.7 23.7 %collective-permute-start.15 = (bf16[256,1024]{1,0:T(8,128)(2,1)}, bf16[256,1024]{1,0:T(8,128)(2,1)}, u32[]{:S(2)}, u32[]{:S(2)}) collective-permute-start(bf16[256,1024]{1,0:T(8,128)(2,1)} %rest_4_.4), channel_id=1, source_target_pairs={{0,2},{1,3},{2,0},{3,1},{4,6},{5,7},{6,4},{7,5},{8,10},{9,11},{10,... | collective-permute-start | bytes 1572872 | tf_op jit(solution)/shard_map/ppermute | solution.py:37
  96.4 15.7 %collective-permute-start.16 = (bf16[1024,256]{1,0:T(8,128)(2,1)}, bf16[1024,256]{1,0:T(8,128)(2,1)S(1)}, u32[]{:S(2)}, u32[]{:S(2)}) collective-permute-start(bf16[1024,256]{1,0:T(8,128)(2,1)} %collective-permute-done.14.rest_2_), channel_id=1, source_target_pairs={{0,1},{1,0},{2,3},{3,2},{4,5},{5,4},{6,7},{7,6},{8,9},{9,8},{10,11... | collective-permute-start | bytes 1572872 | tf_op jit(solution)/shard_map/ppermute | solution.py:37
  100.7 11.3 %collective-permute-start.17 = (bf16[16,512]{1,0:T(8,128)(2,1)}, bf16[16,512]{1,0:T(8,128)(2,1)S(1)}, u32[]{:S(2)}, u32[]{:S(2)}) collective-permute-start(bf16[16,512]{1,0:T(8,128)(2,1)} %get-tuple-element.390), channel_id=1, source_target_pairs={{0,1},{1,0},{2,3},{3,2},{4,5},{5,4},{6,7},{7,6},{8,9},{9,8},{10,11... | collective-permute-start | bytes 49160 | tf_op jit(solution)/shard_map/ppermute | solution.py:37
  101.2 10.9 %collective-permute-start.18 = (bf16[16,512]{1,0:T(8,128)(2,1)}, bf16[16,512]{1,0:T(8,128)(2,1)S(1)}, u32[]{:S(2)}, u32[]{:S(2)}) collective-permute-start(bf16[16,512]{1,0:T(8,128)(2,1)} %get-tuple-element.391), channel_id=1, source_target_pairs={{0,2},{1,3},{2,0},{3,1},{4,6},{5,7},{6,4},{7,5},{8,10},{9,11},{10,... | collective-permute-start | bytes 49160 | tf_op jit(solution)/shard_map/ppermute | solution.py:37
  101.7 10.4 %collective-permute-start.19 = (bf16[16,512]{1,0:T(8,128)(2,1)}, bf16[16,512]{1,0:T(8,128)(2,1)S(1)}, u32[]{:S(2)}, u32[]{:S(2)}) collective-permute-start(bf16[16,512]{1,0:T(8,128)(2,1)} %get-tuple-element.392), channel_id=1, source_target_pairs={{0,3},{1,2},{2,1},{3,0},{4,7},{5,6},{6,5},{7,4},{8,11},{9,10},{10,... | collective-permute-start | bytes 49160 | tf_op jit(solution)/shard_map/ppermute | solution.py:37
  104.4 22.4 %collective-permute-start.23 = (bf16[256,1536]{1,0:T(8,128)(2,1)}, bf16[256,1536]{1,0:T(8,128)(2,1)S(1)}, u32[]{:S(2)}, u32[]{:S(2)}) collective-permute-start(bf16[256,1536]{1,0:T(8,128)(2,1)} %get-tuple-element.412), channel_id=1, source_target_pairs={{0,1},{1,0},{2,3},{3,2},{4,5},{5,4},{6,7},{7,6},{8,9},{9,8},{10,11... | collective-permute-start | bytes 2359304 | tf_op jit(solution)/shard_map/ppermute | solution.py:37
  112.7 14.1 %collective-permute-start.21 = (bf16[256,1024]{1,0:T(8,128)(2,1)}, bf16[256,1024]{1,0:T(8,128)(2,1)S(1)}, u32[]{:S(2)}, u32[]{:S(2)}) collective-permute-start(bf16[256,1024]{1,0:T(8,128)(2,1)} %get-tuple-element.411.refs_2_.rest_4_), channel_id=1, source_target_pairs={{0,2},{1,3},{2,0},{3,1},{4,6},{5,7},{6,4},{7,5},{8,10},{9,11},{10,... | collective-permute-start | bytes 1572872 | tf_op jit(solution)/shard_map/ppermute | solution.py:37
  113.2 13.6 %collective-permute-start.22 = (bf16[256,1024]{1,0:T(8,128)(2,1)}, bf16[256,1024]{1,0:T(8,128)(2,1)S(1)}, u32[]{:S(2)}, u32[]{:S(2)}) collective-permute-start(bf16[256,1024]{1,0:T(8,128)(2,1)} %get-tuple-element.411.refs_2_.rest_4_), channel_id=1, source_target_pairs={{0,1},{1,0},{2,3},{3,2},{4,5},{5,4},{6,7},{7,6},{8,9},{9,8},{10,11... | collective-permute-start | bytes 1572872 | tf_op jit(solution)/shard_map/ppermute | solution.py:37
  127.4 11.7 %collective-permute-start.27 = (bf16[256,1536]{1,0:T(8,128)(2,1)}, bf16[256,1536]{1,0:T(8,128)(2,1)S(1)}, u32[]{:S(2)}, u32[]{:S(2)}) collective-permute-start(bf16[256,1536]{1,0:T(8,128)(2,1)} %get-tuple-element.429), channel_id=1, source_target_pairs={{0,1},{1,0},{2,3},{3,2},{4,5},{5,4},{6,7},{7,6},{8,9},{9,8},{10,11... | collective-permute-start | bytes 2359304 | tf_op jit(solution)/shard_map/ppermute | solution.py:37
  130.3 14.2 %collective-permute-start.26 = (bf16[256,1024]{1,0:T(8,128)(2,1)}, bf16[256,1024]{1,0:T(8,128)(2,1)S(1)}, u32[]{:S(2)}, u32[]{:S(2)}) collective-permute-start(bf16[256,1024]{1,0:T(8,128)(2,1)} %get-tuple-element.422.refs_0_.rest_0_), channel_id=1, source_target_pairs={{0,2},{1,3},{2,0},{3,1},{4,6},{5,7},{6,4},{7,5},{8,10},{9,11},{10,... | collective-permute-start | bytes 1572872 | tf_op jit(solution)/shard_map/ppermute | solution.py:37
  144.5 11.3 %collective-permute-start.28 = (bf16[256,1024]{1,0:T(8,128)(2,1)}, bf16[256,1024]{1,0:T(8,128)(2,1)S(1)}, u32[]{:S(2)}, u32[]{:S(2)}) collective-permute-start(bf16[256,1024]{1,0:T(8,128)(2,1)} %get-tuple-element.431), channel_id=1, source_target_pairs={{0,1},{1,0},{2,3},{3,2},{4,5},{5,4},{6,7},{7,6},{8,9},{9,8},{10,11... | collective-permute-start | bytes 1572872 | tf_op jit(solution)/shard_map/ppermute | solution.py:37
  158.0 14.0 %collective-permute-start.31 = (bf16[256,1024]{1,0:T(8,128)(2,1)S(1)}, bf16[256,1024]{1,0:T(8,128)(2,1)S(1)}, u32[]{:S(2)}, u32[]{:S(2)}) collective-permute-start(bf16[256,1024]{1,0:T(8,128)(2,1)S(1)} %add_convert_fusion.8), channel_id=1, source_target_pairs={{0,2},{1,3},{2,0},{3,1},{4,6},{5,7},{6,4},{7,5},{8,10},{9,11},{10,... | collective-permute-start | bytes 1572872 | tf_op jit(solution)/shard_map/ppermute | solution.py:37
  174.2 12.8 %collective-permute-start.32 = (bf16[256,1024]{1,0:T(8,128)(2,1)S(1)}, bf16[256,1024]{1,0:T(8,128)(2,1)S(1)}, u32[]{:S(2)}, u32[]{:S(2)}) collective-permute-start(bf16[256,1024]{1,0:T(8,128)(2,1)S(1)} %copy-done.56), channel_id=1, source_target_pairs={{0,1},{1,0},{2,3},{3,2},{4,5},{5,4},{6,7},{7,6},{8,9},{9,8},{10,11... | collective-permute-start | bytes 1572872 | tf_op jit(solution)/shard_map/ppermute | solution.py:37
  174.4 12.6 %collective-permute-start.33 = (bf16[256,1024]{1,0:T(8,128)(2,1)S(1)}, bf16[256,1024]{1,0:T(8,128)(2,1)S(1)}, u32[]{:S(2)}, u32[]{:S(2)}) collective-permute-start(bf16[256,1024]{1,0:T(8,128)(2,1)S(1)} %copy-done.54), channel_id=1, source_target_pairs={{0,1},{1,0},{2,3},{3,2},{4,5},{5,4},{6,7},{7,6},{8,9},{9,8},{10,11... | collective-permute-start | bytes 1572872 | tf_op jit(solution)/shard_map/ppermute | solution.py:37
  187.0 19.1 %collective-permute-start.34 = (bf16[256,2560]{1,0:T(8,128)(2,1)}, bf16[256,2560]{1,0:T(8,128)(2,1)S(1)}, u32[]{:S(2)}, u32[]{:S(2)}) collective-permute-start(bf16[256,2560]{1,0:T(8,128)(2,1)} %get-tuple-element.471), channel_id=1, source_target_pairs={{0,1},{1,0},{2,3},{3,2},{4,5},{5,4},{6,7},{7,6},{8,9},{9,8},{10,11... | collective-permute-start | bytes 3932168 | tf_op jit(solution)/shard_map/ppermute | solution.py:37
  187.4 18.7 %collective-permute-start.35 = (bf16[256,1024]{1,0:T(8,128)(2,1)S(1)}, bf16[256,1024]{1,0:T(8,128)(2,1)S(1)}, u32[]{:S(2)}, u32[]{:S(2)}) collective-permute-start(bf16[256,1024]{1,0:T(8,128)(2,1)S(1)} %add_convert_fusion.6), channel_id=1, source_target_pairs={{0,2},{1,3},{2,0},{3,1},{4,6},{5,7},{6,4},{7,5},{8,10},{9,11},{10,... | collective-permute-start | bytes 1572872 | tf_op jit(solution)/shard_map/ppermute | solution.py:37
  219.3 27.3 %collective-permute-start.42 = (bf16[1024,512]{1,0:T(8,128)(2,1)}, bf16[1024,512]{1,0:T(8,128)(2,1)S(1)}, u32[]{:S(2)}, u32[]{:S(2)}) collective-permute-start(bf16[1024,512]{1,0:T(8,128)(2,1)} %get-tuple-element.519), channel_id=1, source_target_pairs={{0,2},{1,3},{2,0},{3,1},{4,6},{5,7},{6,4},{7,5},{8,10},{9,11},{10,... | collective-permute-start | bytes 3145736 | tf_op jit(solution)/shard_map/ppermute | solution.py:37
  221.8 24.8 %collective-permute-start.40 = (bf16[4,256,256]{2,1,0:T(8,128)(2,1)}, bf16[4,256,256]{2,1,0:T(8,128)(2,1)}, u32[]{:S(2)}, u32[]{:S(2)}) collective-permute-start(bf16[4,256,256]{2,1,0:T(8,128)(2,1)} %get-tuple-element.511.rest_0_), channel_id=1, source_target_pairs={{0,8},{4,12},{8,16},{12,20},{16,24},{20,28},{24,0},{28,4},{1,9},{5... | collective-permute-start | bytes 1572872 | tf_op jit(solution)/shard_map/ppermute | solution.py:1674
  223.3 23.3 %collective-permute-start.41 = (bf16[4,256,256]{2,1,0:T(8,128)(2,1)}, bf16[4,256,256]{2,1,0:T(8,128)(2,1)S(1)}, u32[]{:S(2)}, u32[]{:S(2)}) collective-permute-start(bf16[4,256,256]{2,1,0:T(8,128)(2,1)} %get-tuple-element.511.rest_0_), channel_id=1, source_target_pairs={{0,4},{4,0},{8,12},{12,8},{16,20},{20,16},{24,28},{28,24},{1,5},{5... | collective-permute-start | bytes 1572872 | tf_op jit(solution)/shard_map/ppermute | solution.py:1672
  224.8 21.2 %all-to-all-start.1 = ((f32[8,4,256]{2,1,0:T(4,128)}), f32[8,4,256]{2,1,0:T(4,128)S(1)}, u32[]{:S(2)}, u32[]{:S(2)}) async-start(f32[8,4,256]{2,1,0:T(4,128)} %get-tuple-element.516), calls=%async_computation.1 | async-start | bytes 65536 | tf_op jit(solution)/shard_map/all_to_all | solution.py:1678
  228.7 173.4 %reduce-scatter.5.cloned.1.call-start = ((), (), s32[]{:S(2)}) async-start(), calls=%async_computation.6 | async-start | bytes 1769472 | tf_op jit(solution)/shard_map/reduce_scatter | solution.py:142
  246.6 31.2 %collective-permute-start.43 = (bf16[4,256,256]{2,1,0:T(8,128)(2,1)}, bf16[4,256,256]{2,1,0:T(8,128)(2,1)}, u32[]{:S(2)}, u32[]{:S(2)}) collective-permute-start(bf16[4,256,256]{2,1,0:T(8,128)(2,1)} %collective-permute-done.40.rest_2_), channel_id=1, source_target_pairs={{0,8},{4,12},{8,16},{12,20},{16,24},{20,28},{24,0},{28,4},{1,9},{5... | collective-permute-start | bytes 1572872 | tf_op jit(solution)/shard_map/ppermute | solution.py:1674
  248.7 29.2 %collective-permute-start.44 = (bf16[4,256,256]{2,1,0:T(8,128)(2,1)}, bf16[4,256,256]{2,1,0:T(8,128)(2,1)S(1)}, u32[]{:S(2)}, u32[]{:S(2)}) collective-permute-start(bf16[4,256,256]{2,1,0:T(8,128)(2,1)} %collective-permute-done.40.rest_2_), channel_id=1, source_target_pairs={{0,4},{4,0},{8,12},{12,8},{16,20},{20,16},{24,28},{28,24},{1,5},{5... | collective-permute-start | bytes 1572872 | tf_op jit(solution)/shard_map/ppermute | solution.py:1672
  250.3 27.6 %collective-permute-start.46 = (bf16[4,128,512]{2,1,0:T(8,128)(2,1)S(1)}, bf16[4,128,512]{2,1,0:T(8,128)(2,1)S(1)}, u32[]{:S(2)}, u32[]{:S(2)}) collective-permute-start(bf16[4,128,512]{2,1,0:T(8,128)(2,1)S(1)} %get-tuple-element.706), channel_id=1, source_target_pairs={{0,4},{4,0},{8,12},{12,8},{16,20},{20,16},{24,28},{28,24},{1,5},{5... | collective-permute-start | bytes 1572872 | tf_op jit(solution)/shard_map/ppermute | solution.py:151
  250.9 27.0 %collective-permute-start.45 = (bf16[1024,256]{1,0:T(8,128)(2,1)}, bf16[1024,256]{1,0:T(8,128)(2,1)S(1)}, u32[]{:S(2)}, u32[]{:S(2)}) collective-permute-start(bf16[1024,256]{1,0:T(8,128)(2,1)} %get-tuple-element.533), channel_id=1, source_target_pairs={{0,2},{1,3},{2,0},{3,1},{4,6},{5,7},{6,4},{7,5},{8,10},{9,11},{10,... | collective-permute-start | bytes 1572872 | tf_op jit(solution)/shard_map/ppermute | solution.py:37
  277.9 28.9 %collective-permute-start.47 = (bf16[4,256,256]{2,1,0:T(8,128)(2,1)}, bf16[4,256,256]{2,1,0:T(8,128)(2,1)}, u32[]{:S(2)}, u32[]{:S(2)}) collective-permute-start(bf16[4,256,256]{2,1,0:T(8,128)(2,1)} %collective-permute-done.43.rest_4_), channel_id=1, source_target_pairs={{0,8},{4,12},{8,16},{12,20},{16,24},{20,28},{24,0},{28,4},{1,9},{5... | collective-permute-start | bytes 1572872 | tf_op jit(solution)/shard_map/ppermute | solution.py:1674
  279.4 27.4 %collective-permute-start.48 = (bf16[4,256,256]{2,1,0:T(8,128)(2,1)}, bf16[4,256,256]{2,1,0:T(8,128)(2,1)}, u32[]{:S(2)}, u32[]{:S(2)}) collective-permute-start(bf16[4,256,256]{2,1,0:T(8,128)(2,1)} %collective-permute-done.43.rest_4_), channel_id=1, source_target_pairs={{0,4},{4,0},{8,12},{12,8},{16,20},{20,16},{24,28},{28,24},{1,5},{5... | collective-permute-start | bytes 1572872 | tf_op jit(solution)/shard_map/ppermute | solution.py:1672
  280.2 16.1 %collective-permute-start.52 = (bf16[128,512]{1,0:T(8,128)(2,1)S(1)}, bf16[128,512]{1,0:T(8,128)(2,1)S(1)}, u32[]{:S(2)}, u32[]{:S(2)}) collective-permute-start(bf16[128,512]{1,0:T(8,128)(2,1)S(1)} %get-tuple-element.717), channel_id=1, source_target_pairs={{0,8},{4,12},{8,16},{12,20},{16,24},{20,28},{24,0},{28,4},{1,9},{5... | collective-permute-start | bytes 393224 | tf_op jit(solution)/shard_map/ppermute | solution.py:162
  281.8 25.1 %collective-permute-start.49 = (bf16[1024,512]{1,0:T(8,128)(2,1)}, bf16[1024,512]{1,0:T(8,128)(2,1)}, u32[]{:S(2)}, u32[]{:S(2)}) collective-permute-start(bf16[1024,512]{1,0:T(8,128)(2,1)} %get-tuple-element.557), channel_id=1, source_target_pairs={{0,2},{1,3},{2,0},{3,1},{4,6},{5,7},{6,4},{7,5},{8,10},{9,11},{10,... | collective-permute-start | bytes 3145736 | tf_op jit(solution)/shard_map/ppermute | solution.py:37
  283.3 14.2 %collective-permute-start.50 = (bf16[64,1024]{1,0:T(8,128)(2,1)S(1)}, bf16[64,1024]{1,0:T(8,128)(2,1)S(1)}, u32[]{:S(2)}, u32[]{:S(2)}) collective-permute-start(bf16[64,1024]{1,0:T(8,128)(2,1)S(1)} %get-tuple-element.722), channel_id=1, source_target_pairs={{0,1},{1,0},{2,3},{3,2},{4,5},{5,4},{6,7},{7,6},{8,9},{9,8},{10,11... | collective-permute-start | bytes 393224 | tf_op jit(solution)/shard_map/ppermute | solution.py:37
  308.4 29.3 %collective-permute-start.55 = (bf16[4,256,256]{2,1,0:T(8,128)(2,1)}, bf16[4,256,256]{2,1,0:T(8,128)(2,1)}, u32[]{:S(2)}, u32[]{:S(2)}) collective-permute-start(bf16[4,256,256]{2,1,0:T(8,128)(2,1)} %collective-permute-done.47.rest_6_), channel_id=1, source_target_pairs={{0,4},{4,0},{8,12},{12,8},{16,20},{20,16},{24,28},{28,24},{1,5},{5... | collective-permute-start | bytes 1572872 | tf_op jit(solution)/shard_map/ppermute | solution.py:1672
  309.4 28.2 %collective-permute-start.59 = (bf16[1024,256]{1,0:T(8,128)(2,1)}, bf16[1024,256]{1,0:T(8,128)(2,1)S(1)}, u32[]{:S(2)}, u32[]{:S(2)}) collective-permute-start(bf16[1024,256]{1,0:T(8,128)(2,1)} %get-tuple-element.585), channel_id=1, source_target_pairs={{0,2},{1,3},{2,0},{3,1},{4,6},{5,7},{6,4},{7,5},{8,10},{9,11},{10,... | collective-permute-start | bytes 1572872 | tf_op jit(solution)/shard_map/ppermute | solution.py:37
  315.5 13.7 %collective-permute-start.57 = (f32[56,1024]{1,0:T(8,128)}, f32[56,1024]{1,0:T(8,128)S(1)}, u32[]{:S(2)}, u32[]{:S(2)}) collective-permute-start(f32[56,1024]{1,0:T(8,128)} %get-tuple-element.582), channel_id=1, source_target_pairs={{0,1},{1,0},{2,3},{3,2},{4,5},{5,4},{6,7},{7,6},{8,9},{9,8},{10,11... | collective-permute-start | bytes 688136 | tf_op jit(solution)/shard_map/ppermute | solution.py:37
  338.7 39.9 %all-to-all-start.2 = ((bf16[8,56,1024]{2,1,0:T(8,128)(2,1)}), bf16[8,56,1024]{2,1,0:T(8,128)(2,1)S(1)}, u32[]{:S(2)}, u32[]{:S(2)}) async-start(bf16[8,56,1024]{2,1,0:T(8,128)(2,1)} %broadcast_in_dim.55), calls=%async_computation.3 | async-start | bytes 1835008 | tf_op jit(solution)/shard_map/all_to_all | solution.py:1761
  347.0 31.6 %collective-permute-start.60 = (bf16[4,128,768]{2,1,0:T(8,128)(2,1)S(1)}, bf16[4,128,768]{2,1,0:T(8,128)(2,1)}, u32[]{:S(2)}, u32[]{:S(2)}) collective-permute-start(bf16[4,128,768]{2,1,0:T(8,128)(2,1)S(1)} %get-tuple-element.702), channel_id=1, source_target_pairs={{0,4},{4,0},{8,12},{12,8},{16,20},{20,16},{24,28},{28,24},{1,5},{5... | collective-permute-start | bytes 2359304 | tf_op jit(solution)/shard_map/ppermute | solution.py:151
  380.7 20.0 %collective-permute-start.61 = (bf16[128,768]{1,0:T(8,128)(2,1)}, bf16[128,768]{1,0:T(8,128)(2,1)}, u32[]{:S(2)}, u32[]{:S(2)}) collective-permute-start(bf16[128,768]{1,0:T(8,128)(2,1)} %get-tuple-element.708), channel_id=1, source_target_pairs={{0,8},{4,12},{8,16},{12,20},{16,24},{20,28},{24,0},{28,4},{1,9},{5... | collective-permute-start | bytes 589832 | tf_op jit(solution)/shard_map/ppermute | solution.py:162
  382.0 18.7 %collective-permute-start.62 = (bf16[128,768]{1,0:T(8,128)(2,1)}, bf16[128,768]{1,0:T(8,128)(2,1)}, u32[]{:S(2)}, u32[]{:S(2)}) collective-permute-start(bf16[128,768]{1,0:T(8,128)(2,1)} %get-tuple-element.710), channel_id=1, source_target_pairs={{0,16},{4,20},{8,24},{12,28},{16,0},{20,4},{24,8},{28,12},{1,17},{... | collective-permute-start | bytes 589832 | tf_op jit(solution)/shard_map/ppermute | solution.py:162
  384.0 16.7 %collective-permute-start.63 = (bf16[128,768]{1,0:T(8,128)(2,1)}, bf16[128,768]{1,0:T(8,128)(2,1)}, u32[]{:S(2)}, u32[]{:S(2)}) collective-permute-start(bf16[128,768]{1,0:T(8,128)(2,1)} %get-tuple-element.709), channel_id=1, source_target_pairs={{0,24},{4,28},{8,0},{12,4},{16,8},{20,12},{24,16},{28,20},{1,25},{... | collective-permute-start | bytes 589832 | tf_op jit(solution)/shard_map/ppermute | solution.py:162
  (85 other events, 620.0 us)
Sparse Core Ops, SparseCore 0:
  173.3 105.9 reduce-scatter.2
  310.0 82.8 reduce-scatter.4
